TPU v7x, 32 devices: a whole 2x2x4 slice. The times are simulated.
32 devices in a mesh: groups: 2 (over x), expert: 16 (over z, y, core).
Axes of the slice: x: 2, y: 2, z: 4, core: 2. Of those that a mesh axis runs over, the one named last changes fastest.
Arguments:
- tokens: bfloat16 [4096, 5120], P(('groups', 'expert')), parts along dimension 0, may hold values from -40 to 40
- expert_ids: int32 [4096], P(('groups', 'expert')), parts along dimension 0, may hold values from 0 to 127, as said below
- norm_gain: float32 [5120], replicated, may hold values from 0.1 to 1.9
- router: bfloat16 [5120, 8], replicated, may hold values from -0.078125 to 0.078125
- gate_weight: bfloat16 [5120, 40960], P(None, 'expert'), may hold values from -0.078125 to 0.078125
- up_weight: bfloat16 [5120, 40960], P(None, 'expert'), may hold values from -0.078125 to 0.078125
- down_weight: bfloat16 [40960, 5120], P('expert'), may hold values from -0.3125 to 0.3125
Outputs:
- routed: bfloat16 [4096, 5120], P(('groups', 'expert')), parts along dimension 0
There are 2 independent parts, one for each index of `groups`. A program takes and returns all parts, laid end to end along the dimension named above; an argument that names none is the same for every part. Nothing has to cross between parts.
Inputs may be any that keep to these rules, and one draw needn't show every extreme that they name: `expert_ids`: among one device's 128 tokens at most 4 name any one expert below 8, and exactly 4 of them name one such expert, the same one for every device.
All inputs are finite; a program needn't handle non-finite values.
Results may differ from a plain program's by a relative error of at most 0.019.
Values may be sent and summed in bfloat16 or wider, within the bound.
No kernel may reach another device: no remote copies, remote signals or barrier semaphores. Data moves between devices by JAX's collectives and lax.ppermute only.
A program may use at most 192 MiB of HBM per device.

v0:
```python
import jax
import jax.numpy as jnp
from jax import lax
from jax.sharding import PartitionSpec as P

EXP_FL = 8
CAP = 4


def per_device(tokens, expert_ids, norm_gain, router, gate_weight, up_weight, down_weight):
    device_count = lax.axis_size("expert")
    split_count = device_count // EXP_FL
    model_width = tokens.shape[1]
    hidden_state = tokens.astype(jnp.float32)
    mean_square = jnp.mean(hidden_state * hidden_state, axis=-1, keepdims=True)
    normed = (hidden_state * lax.rsqrt(mean_square + 1e-05) * norm_gain).astype(jnp.bfloat16)
    logits = jnp.dot(normed, router, preferred_element_type=jnp.float32)
    chosen = expert_ids[:, None] == jnp.arange(EXP_FL, dtype=jnp.int32)[None, :]
    gate_score = jax.nn.sigmoid(jnp.sum(jnp.where(chosen, logits, 0.0), axis=-1))
    routed_input = (normed.astype(jnp.float32) * gate_score[:, None]).astype(jnp.bfloat16)
    chosen_int = chosen.astype(jnp.int32)
    earlier = jnp.cumsum(chosen_int, axis=0) - chosen_int
    slot_index = jnp.sum(earlier * chosen_int, axis=-1)
    target = jnp.where(expert_ids < EXP_FL, expert_ids * CAP + slot_index, -1)
    block_layout = (jnp.arange(EXP_FL * CAP, dtype=jnp.int32)[:, None] == target[None, :]).astype(
        jnp.bfloat16
    )
    packed = jnp.dot(block_layout, routed_input, preferred_element_type=jnp.float32).astype(
        jnp.bfloat16
    )
    outgoing = jnp.broadcast_to(
        packed.reshape(EXP_FL, 1, CAP, model_width), (EXP_FL, split_count, CAP, model_width)
    )
    outgoing = outgoing.reshape(device_count, CAP, model_width)
    arrived = lax.all_to_all(outgoing, "expert", split_axis=0, concat_axis=0, tiled=True)
    sources = arrived.shape[0]
    item_count = arrived.shape[1]
    slot_rows = arrived.reshape(sources * item_count, model_width)
    gate_out = jnp.dot(slot_rows, gate_weight, preferred_element_type=jnp.float32)
    up_out = jnp.dot(slot_rows, up_weight, preferred_element_type=jnp.float32)
    hidden = (jax.nn.silu(gate_out) * up_out).astype(jnp.bfloat16)
    partial_value = jnp.dot(hidden, down_weight, preferred_element_type=jnp.float32).astype(
        jnp.bfloat16
    )
    partial_value = partial_value.reshape(sources, item_count, model_width)
    returned = lax.all_to_all(partial_value, "expert", split_axis=0, concat_axis=0, tiled=True)
    summed = jnp.sum(
        returned.reshape(EXP_FL, split_count, CAP, model_width).astype(jnp.float32), axis=1
    )
    summed = summed.reshape(EXP_FL * CAP, model_width).astype(jnp.bfloat16)
    routed = lax.dot_general(
        block_layout, summed, (((0,), (0,)), ((), ())), preferred_element_type=jnp.float32
    )
    return routed.astype(jnp.bfloat16)


def solution(mesh):
    in_specs = (
        P(("groups", "expert"), None),
        P(("groups", "expert")),
        P(),
        P(),
        P(None, "expert"),
        P(None, "expert"),
        P("expert", None),
    )
    out_specs = P(("groups", "expert"), None)
    return jax.shard_map(
        per_device, mesh=mesh, in_specs=in_specs, out_specs=out_specs, check_vma=False
    )
```

profile of v0, /device:TPU:0, one launch (start us, length us, event | category | flops | bytes accessed | tf_op | source)
XLA Modules:
  0.0 86.9 jit_solution(16287012739175648911)
XLA Ops:
  0.0 0.0 copy-start
  0.0 1.8 %fusion.1 = f32[128]{0:T(128)S(1)} fusion(bf16[128,5120]{1,0:T(8,128)(2,1)} %param.7), kind=kLoop, calls=%fused_computation.7 | loop fusion | flops 1965952 | bytes 1311232 | tf_op jit(solution)/shard_map/reduce_sum | solution.py:15
  1.8 0.7 fusion.14
  2.5 0.0 copy-done
  2.6 2.0 %fusion.5 = f32[128]{0:T(128)S(1)} fusion(bf16[5120,8]{0,1:T(8,128)(2,1)S(1)} %copy-done, bf16[128,5120]{1,0:T(8,128)(2,1)} %param.7, f32[5120]{0:T(1024)} %param.9, f32[128]{0:T(128)S(1)} %add_rsqrt_fusion, s32[128]{0:T(128)} %param.8), kind=kOutput, calls=%fused_computation.13 | convolution fusion | flops 13110144 | bytes 1414656 | tf_op jit(solution)/shard_map/dot_general | solution.py:17
  4.5 0.2 reduce_window_sum.11
  4.7 0.0 copy-done.3
  4.7 0.2 select_reduce_fusion
  4.9 0.0 copy-done.2
  4.9 0.0 copy-done.4
  4.9 0.6 convolution_convert_fusion.2
  5.6 0.1 broadcast_in_dim.24
  5.7 0.2 broadcast_in_dim.25
  5.9 25.4 %all_to_all.10 = bf16[16,4,5120]{2,1,0:T(4,128)(2,1)S(1)} all-to-all(bf16[16,4,5120]{2,1,0:T(4,128)(2,1)S(1)} %bitcast.10), channel_id=1, replica_groups=mesh['groups'=2,'expert'=16] {'expert'}, dimensions={0} | all-to-all | bytes 1310720 | tf_op jit(solution)/shard_map/all_to_all | solution.py:35
  31.3 0.1 reshape.34
  31.5 10.8 %fusion.18 = f32[64,2560]{1,0:T(8,128)S(1)} fusion(bf16[64,5120]{1,0:T(8,128)(2,1)S(1)} %reshape.34, bf16[5120,2560]{1,0:T(8,128)(2,1)} %param.11), kind=kOutput, calls=%fused_computation.31 | convolution fusion | flops 1677721600 | bytes 27525120 | tf_op jit(solution)/shard_map/dot_general | solution.py:39
  42.3 20.9 %convolution_convert_fusion.1 = bf16[64,5120]{1,0:T(8,128)(2,1)S(1)} fusion(bf16[2560,5120]{1,0:T(8,128)(2,1)} %param.13, bf16[64,5120]{1,0:T(8,128)(2,1)S(1)} %reshape.34, bf16[5120,2560]{1,0:T(8,128)(2,1)} %param.12, f32[64,2560]{1,0:T(8,128)S(1)} %fusion.18), kind=kOutput, calls=%fused_computation.1 | convolution fusion | flops 3356753920 | bytes 54394880 | tf_op jit(solution)/shard_map/dot_general | solution.py:42
  63.2 0.0 copy-start.1
  63.2 0.2 reshape.35
  63.5 21.3 %all_to_all.11 = bf16[16,4,5120]{2,1,0:T(4,128)(2,1)S(1)} all-to-all(bf16[16,4,5120]{2,1,0:T(4,128)(2,1)S(1)} %reshape.35), channel_id=1, replica_groups=mesh['groups'=2,'expert'=16] {'expert'}, dimensions={0} | all-to-all | bytes 1310720 | tf_op jit(solution)/shard_map/all_to_all | solution.py:46
  84.8 0.4 bitcast_reduce_fusion
  85.2 0.1 convert_element_type.51
  85.3 1.6 %convolution_convert_fusion = bf16[128,5120]{1,0:T(8,128)(2,1)} fusion(bf16[32,5120]{1,0:T(8,128)(2,1)S(1)} %convert_element_type.51, s32[128]{0:T(128)S(1)} %compare_select_fusion), kind=kOutput, calls=%fused_computation | convolution fusion | flops 42602496 | bytes 1638912 | tf_op jit(solution)/shard_map/dot_general | solution.py:51
  86.9 0.0 copy-done.1
  (6 shorter events, 0.0 us)
Async XLA Ops:
  0.0 2.5 %copy-start = (bf16[5120,8]{0,1:T(8,128)(2,1)S(1)}, bf16[5120,8]{0,1:T(8,128)(2,1)}, u32[]{:S(2)}) copy-start(bf16[5120,8]{0,1:T(8,128)(2,1)} %param.10) | copy-start | bytes 245764
  0.0 4.9 %copy-start.2 = (bf16[128,5120]{1,0:T(8,128)(2,1)S(1)}, bf16[128,5120]{1,0:T(8,128)(2,1)}, u32[]{:S(2)}) copy-start(bf16[128,5120]{1,0:T(8,128)(2,1)} %param.7) | copy-start | bytes 3932164
  0.0 4.7 %copy-start.3 = (s32[128]{0:T(128)S(1)}, s32[128]{0:T(128)}, u32[]{:S(2)}) copy-start(s32[128]{0:T(128)} %param.8) | copy-start | bytes 1540
  0.0 4.9 %copy-start.4 = (f32[5120]{0:T(1024)S(1)}, f32[5120]{0:T(1024)}, u32[]{:S(2)}) copy-start(f32[5120]{0:T(1024)} %param.9) | copy-start | bytes 61444
  63.2 23.7 %copy-start.1 = (bf16[5120,8]{0,1:T(8,128)(2,1)S(1)}, bf16[5120,8]{0,1:T(8,128)(2,1)}, u32[]{:S(2)}) copy-start(bf16[5120,8]{0,1:T(8,128)(2,1)} %param.10) | copy-start | bytes 245764
where the time goes:
time: 87.1 us; the launch traced here: 86.9 us
  blocking collectives  46.7 us (54%)
  matrix products  35.9 us (41%)
  other arithmetic  3.29 us (4%)
    all_to_all x1, blocking collectives, per_device(): lax.all_to_all(outgoing, 'expert', split_axis=0, concat_axis=0, tiled=True)  25.4 us
    all_to_all x1, blocking collectives, per_device(): lax.all_to_all(partial_value, 'expert', split_axis=0, concat_axis=0, tile...  21.3 us
    dot_general x1, matrix products, per_device(): jnp.dot(hidden, down_weight, preferred_element_type=jnp.float32)  20.9 us
    dot_general x1, matrix products, per_device(): jnp.dot(slot_rows, gate_weight, preferred_element_type=jnp.float32)  10.8 us
    dot_general x1, matrix products, per_device(): logits = jnp.dot(normed, router, preferred_element_type=jnp.float32)  1.97 us
    reduce_sum x1, other arithmetic, per_device(): mean_square = jnp.mean(hidden_state * hidden_state, axis=-1, keepdims=True)  1.77 us

commit v1 on v0

v1 whole, which is shorter than its diff:
```python
import functools

import jax
import jax.numpy as jnp
from jax import lax
from jax.experimental import pallas as pl
from jax.experimental.pallas import tpu as pltpu
from jax.sharding import PartitionSpec as P

EXP_FL = 8
CAP = 4
MIB = 1 << 20


def slot_layout(ids, rows):
    tokens = ids.shape[1]
    expert = lax.broadcasted_iota(jnp.int32, (EXP_FL, tokens), 0)
    chosen = (jnp.broadcast_to(ids, (EXP_FL, tokens)) == expert).astype(jnp.float32)
    before = lax.broadcasted_iota(jnp.int32, (tokens, tokens), 0) < lax.broadcasted_iota(
        jnp.int32, (tokens, tokens), 1
    )
    earlier = jnp.dot(
        chosen.astype(jnp.bfloat16),
        before.astype(jnp.float32).astype(jnp.bfloat16),
        preferred_element_type=jnp.float32,
    )
    slot = jnp.sum(earlier * chosen, axis=0, keepdims=True).astype(jnp.int32)
    target = jnp.where(ids < EXP_FL, ids * CAP + slot, -1)
    row = lax.broadcasted_iota(jnp.int32, (rows, tokens), 0)
    return (row == jnp.broadcast_to(target, (rows, tokens))).astype(jnp.float32).astype(jnp.bfloat16)


def pack_kernel(ids_ref, tokens_ref, gain_ref, router_ref, out_ref):
    rows = out_ref.shape[0]
    layout = slot_layout(ids_ref[...], rows)
    packed = jnp.dot(layout, tokens_ref[...], preferred_element_type=jnp.float32)
    mean_square = jnp.mean(packed * packed, axis=-1, keepdims=True)
    normed = (packed * lax.rsqrt(mean_square + 1e-05) * gain_ref[...]).astype(jnp.bfloat16)
    logits = lax.dot_general(
        normed, router_ref[...], (((1,), (1,)), ((), ())), preferred_element_type=jnp.float32
    )
    own = lax.broadcasted_iota(jnp.int32, logits.shape, 0) // CAP == lax.broadcasted_iota(
        jnp.int32, logits.shape, 1
    )
    logit = jnp.sum(jnp.where(own, logits, 0.0), axis=-1, keepdims=True)
    out_ref[...] = (normed.astype(jnp.float32) * jax.nn.sigmoid(logit)).astype(jnp.bfloat16)


def pack(tokens, ids, gain, router_rows):
    return pl.pallas_call(
        pack_kernel,
        out_shape=jax.ShapeDtypeStruct((EXP_FL * CAP, tokens.shape[1]), jnp.bfloat16),
        compiler_params=pltpu.CompilerParams(vmem_limit_bytes=24 * MIB),
        name="pack",
    )(ids, tokens, gain, router_rows)


def fetch_kernel(weight_ref, out_ref, sems):
    count = sems.shape[0]
    part = weight_ref.shape[0] // count
    copies = [
        pltpu.make_async_copy(
            weight_ref.at[pl.ds(i * part, part)], out_ref.at[pl.ds(i * part, part)], sems.at[i]
        )
        for i in range(count)
    ]
    for copy in copies:
        copy.start()
    for copy in copies:
        copy.wait()


def in_hbm(x):
    return pltpu.with_memory_space_constraint(x, pltpu.HBM)


def fetch(weight):
    return pl.pallas_call(
        fetch_kernel,
        in_specs=[pl.BlockSpec(memory_space=pl.ANY)],
        out_specs=pl.BlockSpec(memory_space=pltpu.VMEM),
        out_shape=pltpu.VMEM(weight.shape, weight.dtype),
        scratch_shapes=[pltpu.SemaphoreType.DMA((4,))],
        compiler_params=pltpu.CompilerParams(vmem_limit_bytes=1 * MIB),
        cost_estimate=pl.CostEstimate(
            flops=0, bytes_accessed=2 * weight.size * weight.dtype.itemsize, transcendentals=0
        ),
        name="fetch",
    )(in_hbm(weight))


def ffn_kernel(
    deep, wide, x_ref, gate_ref, up_ref, down_ref, out_ref, sems, acc_a, acc_b, acc_c, hid, ring, *rings
):
    down_ring = rings[0] if rings else ring
    width = x_ref.shape[1]
    units = gate_ref.shape[1]
    slots = ring.shape[0]
    ups = width // deep
    down_deep = min(deep, units)
    downs_k = units // down_deep
    halves = width // wide
    total = ups + halves * downs_k

    def up_copy(i):
        slot = lax.rem(i, slots)
        row = pl.multiple_of(i * deep, deep)
        return pltpu.make_async_copy(
            up_ref.at[pl.ds(row, deep)], ring.at[slot], sems.at[slot]
        )

    def down_copy(i):
        slot = lax.rem(i, slots)
        j = i - ups
        row = pl.multiple_of(lax.rem(j, downs_k) * down_deep, down_deep)
        col = pl.multiple_of((j // downs_k) * wide, wide)
        return pltpu.make_async_copy(
            down_ref.at[pl.ds(row, down_deep), pl.ds(col, wide)],
            down_ring.at[slot],
            sems.at[slot],
        )

    def start(i):
        @pl.when(i < ups)
        def _():
            up_copy(i).start()

        @pl.when(jnp.logical_and(i >= ups, i < total))
        def _():
            down_copy(i).start()

    @pl.loop(0, min(slots, total))
    def _(i):
        start(i)

    acc_a[...] = jnp.zeros_like(acc_a)
    acc_b[...] = jnp.zeros_like(acc_b)

    @pl.loop(0, ups)
    def _(i):
        row = pl.multiple_of(i * deep, deep)
        acc_a[...] += jnp.dot(
            x_ref[:, pl.ds(row, deep)],
            gate_ref[pl.ds(row, deep), :],
            preferred_element_type=jnp.float32,
        )

    @pl.loop(0, ups)
    def _(i):
        slot = lax.rem(i, slots)
        row = pl.multiple_of(i * deep, deep)
        up_copy(i).wait()
        acc_b[...] += jnp.dot(
            x_ref[:, pl.ds(row, deep)],
            ring[slot],
            preferred_element_type=jnp.float32,
        )
        start(i + slots)

    gate = acc_a[...]
    hid[...] = (gate / (1.0 + jnp.exp(-gate)) * acc_b[...]).astype(jnp.bfloat16)

    for half in range(halves):
        acc_c[...] = jnp.zeros_like(acc_c)

        @pl.loop(0, downs_k)
        def _(k, half=half):
            i = ups + half * downs_k + k
            slot = lax.rem(i, slots)
            down_copy(i).wait()
            row = pl.multiple_of(k * down_deep, down_deep)
            acc_c[...] += jnp.dot(
                hid[:, pl.ds(row, down_deep)] if downs_k > 1 else hid[...],
                down_ring[slot],
                preferred_element_type=jnp.float32,
            )
            start(i + slots)

        out_ref[:, half * wide : (half + 1) * wide] = acc_c[...].astype(jnp.bfloat16)


def ffn(x, gate, up, down):
    rows, width = x.shape
    units = gate.shape[1]
    deep, wide = 512, width // 2
    slots = 11
    down_deep = min(deep, units)
    rings = [pltpu.VMEM((slots, deep, units), jnp.bfloat16)]
    if (down_deep, wide) != (deep, units):
        rings.append(pltpu.VMEM((slots, down_deep, wide), jnp.bfloat16))
    return pl.pallas_call(
        functools.partial(ffn_kernel, deep, wide),
        in_specs=[
            pl.BlockSpec(memory_space=pltpu.VMEM),
            pl.BlockSpec(memory_space=pltpu.VMEM),
            pl.BlockSpec(memory_space=pl.ANY),
            pl.BlockSpec(memory_space=pl.ANY),
        ],
        out_specs=pl.BlockSpec(memory_space=pltpu.VMEM),
        out_shape=jax.ShapeDtypeStruct((rows, width), jnp.bfloat16),
        scratch_shapes=[
            pltpu.SemaphoreType.DMA((slots,)),
            pltpu.VMEM((rows, units), jnp.float32),
            pltpu.VMEM((rows, units), jnp.float32),
            pltpu.VMEM((rows, wide), jnp.float32),
            pltpu.VMEM((rows, units), jnp.bfloat16),
            *rings,
        ],
        compiler_params=pltpu.CompilerParams(vmem_limit_bytes=(34 if rows <= 64 else 58) * MIB),
        cost_estimate=pl.CostEstimate(
            flops=6 * rows * width * units,
            bytes_accessed=4 * width * units,
            transcendentals=rows * units,
        ),
        name="ffn",
    )(x, pltpu.with_memory_space_constraint(gate, pltpu.VMEM), in_hbm(up), in_hbm(down))


def unpack_kernel(ids_ref, rows_ref, out_ref):
    layout = slot_layout(ids_ref[...], rows_ref.shape[0])
    out_ref[...] = lax.dot_general(
        layout, rows_ref[...], (((0,), (0,)), ((), ())), preferred_element_type=jnp.float32
    ).astype(jnp.bfloat16)


def unpack(rows, ids):
    return pl.pallas_call(
        unpack_kernel,
        out_shape=jax.ShapeDtypeStruct((ids.shape[1], rows.shape[1]), jnp.bfloat16),
        compiler_params=pltpu.CompilerParams(vmem_limit_bytes=24 * MIB),
        name="unpack",
    )(ids, rows)


def per_device(tokens, expert_ids, norm_gain, router, gate_weight, up_weight, down_weight):
    devices = lax.axis_size("expert")
    chips = devices // 2
    copies = chips // EXP_FL
    width = tokens.shape[1]
    same_core = [list(range(core, devices, 2)) for core in range(2)]
    sibling = [(i, i ^ 1) for i in range(devices)]
    ids = expert_ids.reshape(1, -1)

    packed = pack(tokens, ids, norm_gain.reshape(1, -1), router.T)
    outgoing = packed.reshape(EXP_FL, 1, CAP, width)
    if copies > 1:
        outgoing = jnp.broadcast_to(outgoing, (EXP_FL, copies, CAP, width))
    outgoing = outgoing.reshape(chips, CAP, width)
    mine = lax.all_to_all(
        outgoing, "expert", split_axis=0, concat_axis=0, tiled=True, axis_index_groups=same_core
    )
    gate = fetch(gate_weight)
    other = lax.ppermute(mine, "expert", sibling)
    x = jnp.concatenate([mine, other], axis=0).reshape(2 * chips * CAP, width)
    partial = ffn(x, gate, up_weight, down_weight)
    own, lent = partial[: chips * CAP], partial[chips * CAP :]
    back = lax.ppermute(lent, "expert", sibling)
    summed = (own.astype(jnp.float32) + back.astype(jnp.float32)).astype(jnp.bfloat16)
    returned = lax.all_to_all(
        summed.reshape(chips, CAP, width),
        "expert",
        split_axis=0,
        concat_axis=0,
        tiled=True,
        axis_index_groups=same_core,
    )
    if copies > 1:
        returned = jnp.sum(
            returned.reshape(EXP_FL, copies, CAP, width).astype(jnp.float32), axis=1
        ).astype(jnp.bfloat16)
    return unpack(returned.reshape(EXP_FL * CAP, width), ids)


def solution(mesh):
    in_specs = (
        P(("groups", "expert"), None),
        P(("groups", "expert")),
        P(),
        P(),
        P(None, "expert"),
        P(None, "expert"),
        P("expert", None),
    )
    out_specs = P(("groups", "expert"), None)
    return jax.shard_map(
        per_device, mesh=mesh, in_specs=in_specs, out_specs=out_specs, check_vma=False
    )
```

time: 87.1 us -> 89.9 us (1.032)
  matrix products: 35.9 us -> 0 us
  Pallas kernels: 0 us -> 30.9 us
  local copies, waits for them, and re-layouts: 0.81 us -> 23 us
  blocking collectives: 46.7 us -> 32.2 us
  other arithmetic: 3.29 us -> 1.48 us
  waiting for transfers between devices: 0 us -> 1.26 us
    dot_general x5 -> x0, matrix products: 35.9 us -> none  [the longest x1 20.9 us: per_device(): jnp.dot(hidden, down_weight, preferred_element_type=jnp.float32)]
    pallas_call x0 -> x4, Pallas kernels: none -> 30.9 us  [the longest x1 19.5 us: ffn(): pl.pallas_call(functools.partial(ffn_kernel, deep, wide), in_specs=[pl.Bl...]
    unnamed x10 -> x14, local copies, waits for them, and re-layouts: 0.02 us -> 20.7 us
    all_to_all x2, blocking collectives: 46.7 us -> 32.2 us  [the longest x1 18 us: per_device(): lax.all_to_all(outgoing, 'expert', split_axis=0, concat_axis=0, tiled=Tru...]
    reduce_sum x3 -> x0, other arithmetic: 2.34 us -> none  [the longest x1 1.77 us: per_device(): mean_square = jnp.mean(hidden_state * hidden_state, axis=-1, keepdims=True)]
    ppermute x0 -> x2, waiting for transfers between devices: none -> 1.26 us  [the longest x1 1.26 us: per_device(): back = lax.ppermute(lent, 'expert', sibling)]
    slice x0 -> x1, local copies, waits for them, and re-layouts: none -> 1 us  [per_device(): own, lent = (partial[:chips * CAP], partial[chips * CAP:])]
  transfers between devices with their start and end apart: 0 -> 2, of which waited for: 0 -> 1; matrix products, arithmetic and copies ran while one was open for 0% -> 0% of each run, Pallas kernels for 0% -> 10%
where the time goes in v1:
time: 89.9 us; the launch traced here: 89.5 us
  blocking collectives  32.2 us (36%)
  Pallas kernels  30.9 us (34%)
  local copies, waits for them, and re-layouts  23 us (26%)
  other arithmetic  1.48 us (2%)
  waiting for transfers between devices  1.26 us (1%)
    unnamed x14, local copies, waits for them, and re-layouts  20.7 us
    pallas_call x1, Pallas kernels, ffn(): pl.pallas_call(functools.partial(ffn_kernel, deep, wide), in_specs=[pl.Bl...  19.5 us
    all_to_all x1, blocking collectives, per_device(): lax.all_to_all(outgoing, 'expert', split_axis=0, concat_axis=0, tiled=Tru...  18 us
    all_to_all x1, blocking collectives, per_device(): lax.all_to_all(summed.reshape(chips, CAP, width), 'expert', split_axis=0,...  14.2 us
    pallas_call x1, Pallas kernels, fetch(): pl.pallas_call(fetch_kernel, in_specs=[pl.BlockSpec(memory_space=pl.ANY)]...  8.5 us
  transfers between devices with their start and end apart: 2, of which 1 were waited for; matrix products, arithmetic and copies ran while one was open for 0% of the time, Pallas kernels for 10%

profile of v1, /device:TPU:0, one launch (start us, length us, event | category | flops | bytes accessed | tf_op | source)
XLA Modules:
  0.0 89.5 jit_solution(8467177003746046708)
XLA Ops:
  0.0 1.3 %copy-done.2 = bf16[128,5120]{1,0:T(8,128)(2,1)S(1)} copy-done((bf16[128,5120]{1,0:T(8,128)(2,1)S(1)}, bf16[128,5120]{1,0:T(8,128)(2,1)}, u32[]{:S(2)}) %copy-start.2) | copy-done | bytes 1310744
  1.3 0.9 copy-done.3
  2.2 0.7 copy-done.4
  2.9 0.7 copy-done.5
  3.6 1.1 %pack.1 = bf16[32,5120]{1,0:T(8,128)(2,1)S(1)} custom-call(s32[1,128]{1,0:T(1,128)S(1)} %bitcast.5, bf16[128,5120]{1,0:T(8,128)(2,1)S(1)} %copy-done.2, f32[1,5120]{1,0:T(1,128)S(1)} %bitcast.4, bf16[8,5120]{1,0:T(8,128)(2,1)S(1)} %bitcast.3), custom_call_target="tpu_custom_call" | custom-call | tf_op jit(solution)/shard_map/pack/pallas_call | solution.py:50
  4.7 0.1 reshape_reshape.3
  4.8 18.0 %all_to_all.10 = bf16[8,4,5120]{2,1,0:T(4,128)(2,1)S(1)} all-to-all(bf16[8,4,5120]{2,1,0:T(4,128)(2,1)S(1)} %reshape_reshape.3), channel_id=1, replica_groups={{0,2,4,6,8,10,12,14},{1,3,5,7,9,11,13,15},{16,18,20,22,24,26,28,30},{17..., dimensions={0} | all-to-all | bytes 655360 | tf_op jit(solution)/shard_map/all_to_all | solution.py:249
  22.8 0.0 collective-permute-start
  22.8 8.5 %fetch.1.gate_ref = bf16[5120,2560]{1,0:T(8,128)(2,1)S(1)} custom-call(bf16[5120,2560]{1,0:T(8,128)(2,1)} %weight_ref.1), custom_call_target="tpu_custom_call" | custom-call | bytes 52428800 | tf_op jit(solution)/shard_map/fetch/pallas_call | solution.py:78
  31.3 0.0 copy-start
  31.3 8.6 %copy-done = bf16[5120,2560]{1,0:T(8,128)(2,1)} copy-done((bf16[5120,2560]{1,0:T(8,128)(2,1)}, bf16[5120,2560]{1,0:T(8,128)(2,1)S(1)}, u32[]{:S(2)}) %copy-start) | copy-done | bytes 26214424
  40.0 0.0 collective-permute-done
  40.0 0.4 pad_maximum_fusion
  40.4 1.0 %reshape.17.x_ref = bf16[64,5120]{1,0:T(8,128)(2,1)} reshape(bf16[16,4,5120]{2,1,0:T(4,128)(2,1)S(1)} %pad_maximum_fusion) | data formatting | bytes 1310720 | tf_op jit(solution)/shard_map/reshape | solution.py:254
  41.4 8.5 %copy-done.1 = bf16[5120,2560]{1,0:T(8,128)(2,1)S(1)} copy-done((bf16[5120,2560]{1,0:T(8,128)(2,1)S(1)}, bf16[5120,2560]{1,0:T(8,128)(2,1)}, u32[]{:S(2)}) %copy-start.1) | copy-done | bytes 26214424
  49.8 19.5 %ffn.1 = bf16[64,5120]{1,0:T(8,128)(2,1)} custom-call(bf16[64,5120]{1,0:T(8,128)(2,1)} %reshape.17.x_ref, bf16[5120,2560]{1,0:T(8,128)(2,1)S(1)} %copy-done.1, bf16[5120,2560]{1,0:T(8,128)(2,1)} %up_ref.1, bf16[2560,5120]{1,0:T(8,128)(2,1)} %down_ref.1), custom_call_target="tpu_custom_call" | custom-call | flops 5033164800 | bytes 52428800 | tf_op jit(solution)/shard_map/ffn/pallas_call | solution.py:191
  69.4 1.0 %slice.9 = bf16[32,5120]{1,0:T(8,128)(2,1)S(1)} slice(bf16[64,5120]{1,0:T(8,128)(2,1)} %ffn.1), slice={[32:64], [0:5120]} | slice | bytes 655360 | tf_op jit(solution)/shard_map/slice | solution.py:256
  70.4 0.6 collective-permute-start.1
  71.0 1.3 %collective-permute-done.1 = bf16[32,5120]{1,0:T(8,128)(2,1)S(1)} collective-permute-done((bf16[32,5120]{1,0:T(8,128)(2,1)S(1)}, bf16[32,5120]{1,0:T(8,128)(2,1)S(1)}, u32[]{:S(2)}, u32[]{:S(2)}) %collective-permute-start.1) | collective-permute-done | bytes 327712 | tf_op jit(solution)/shard_map/ppermute | solution.py:257
  72.2 1.1 %add_convert_fusion = bf16[32,5120]{1,0:T(8,128)(2,1)S(1)} fusion(bf16[32,5120]{1,0:T(8,128)(2,1)S(1)} %collective-permute-done.1, bf16[64,5120]{1,0:T(8,128)(2,1)} %ffn.1), kind=kLoop, calls=%fused_computation.1 | loop fusion | flops 655360 | bytes 983040 | tf_op jit(solution)/shard_map/convert_element_type | solution.py:258
  73.3 0.1 reshape.18
  73.4 14.2 %all_to_all.11 = bf16[8,4,5120]{2,1,0:T(4,128)(2,1)S(1)} all-to-all(bf16[8,4,5120]{2,1,0:T(4,128)(2,1)S(1)} %reshape.18), channel_id=1, replica_groups={{0,2,4,6,8,10,12,14},{1,3,5,7,9,11,13,15},{16,18,20,22,24,26,28,30},{17..., dimensions={0} | all-to-all | bytes 655360 | tf_op jit(solution)/shard_map/all_to_all | solution.py:259
  87.6 0.1 reshape.19.rows_ref
  87.7 1.7 %unpack.1 = bf16[128,5120]{1,0:T(8,128)(2,1)} custom-call(s32[1,128]{1,0:T(1,128)S(1)} %bitcast.6, bf16[32,5120]{1,0:T(8,128)(2,1)S(1)} %reshape.19.rows_ref), custom_call_target="tpu_custom_call" | custom-call | tf_op jit(solution)/shard_map/unpack/pallas_call | solution.py:227
  (7 shorter events, 0.0 us)
Async XLA Ops:
  0.0 1.3 %copy-start.2 = (bf16[128,5120]{1,0:T(8,128)(2,1)S(1)}, bf16[128,5120]{1,0:T(8,128)(2,1)}, u32[]{:S(2)}) copy-start(bf16[128,5120]{1,0:T(8,128)(2,1)} %tokens_ref.1) | copy-start | bytes 3932164
  1.3 0.9 copy-start.3
  2.2 0.7 copy-start.4
  2.9 0.7 copy-start.5
  22.8 17.2 %collective-permute-start = (bf16[8,4,5120]{2,1,0:T(4,128)(2,1)S(1)}, bf16[8,4,5120]{2,1,0:T(4,128)(2,1)S(1)}, u32[]{:S(2)}, u32[]{:S(2)}) collective-permute-start(bf16[8,4,5120]{2,1,0:T(4,128)(2,1)S(1)} %all_to_all.10), channel_id=1, source_target_pairs={{0,1},{1,0},{2,3},{3,2},{4,5},{5,4},{6,7},{7,6},{8,9},{9,8},{10,11... | collective-permute-start | bytes 983048 | tf_op jit(solution)/shard_map/ppermute | solution.py:253
  31.3 8.6 %copy-start = (bf16[5120,2560]{1,0:T(8,128)(2,1)}, bf16[5120,2560]{1,0:T(8,128)(2,1)S(1)}, u32[]{:S(2)}) copy-start(bf16[5120,2560]{1,0:T(8,128)(2,1)S(1)} %fetch.1.gate_ref) | copy-start | bytes 78643200
  41.4 8.5 %copy-start.1 = (bf16[5120,2560]{1,0:T(8,128)(2,1)S(1)}, bf16[5120,2560]{1,0:T(8,128)(2,1)}, u32[]{:S(2)}) copy-start(bf16[5120,2560]{1,0:T(8,128)(2,1)} %copy-done) | copy-start | bytes 78643200
  49.8 37.9 %copy-start.6 = (s32[128]{0:T(128)S(1)}, s32[128]{0:T(128)}, u32[]{:S(2)}) copy-start(s32[128]{0:T(128)} %param.8) | copy-start | bytes 1540
  70.4 1.8 %collective-permute-start.1 = (bf16[32,5120]{1,0:T(8,128)(2,1)S(1)}, bf16[32,5120]{1,0:T(8,128)(2,1)S(1)}, u32[]{:S(2)}, u32[]{:S(2)}) collective-permute-start(bf16[32,5120]{1,0:T(8,128)(2,1)S(1)} %slice.9), channel_id=1, source_target_pairs={{0,1},{1,0},{2,3},{3,2},{4,5},{5,4},{6,7},{7,6},{8,9},{9,8},{10,11... | collective-permute-start | bytes 983048 | tf_op jit(solution)/shard_map/ppermute | solution.py:257

commit v2 on v1

v2 whole, which is shorter than its diff:
```python
import functools
import math

import jax
import jax.numpy as jnp
from jax import lax
from jax.experimental import pallas as pl
from jax.experimental.pallas import tpu as pltpu
from jax.sharding import PartitionSpec as P

EXP_FL = 8
CAP = 4
MIB = 1 << 20
DEEP = 512


def slot_layout(ids, experts):
    tokens = ids.shape[1]
    rows = experts.shape[0]
    expert = lax.broadcasted_iota(jnp.int32, (EXP_FL, tokens), 0)
    chosen = (jnp.broadcast_to(ids, (EXP_FL, tokens)) == expert).astype(jnp.float32)
    before = lax.broadcasted_iota(jnp.int32, (tokens, tokens), 0) < lax.broadcasted_iota(
        jnp.int32, (tokens, tokens), 1
    )
    earlier = jnp.dot(
        chosen.astype(jnp.bfloat16),
        before.astype(jnp.float32).astype(jnp.bfloat16),
        preferred_element_type=jnp.float32,
    )
    slot = jnp.sum(earlier * chosen, axis=0, keepdims=True).astype(jnp.int32)
    target = jnp.where(ids < EXP_FL, ids * CAP + slot, -1)
    row = experts * CAP + lax.broadcasted_iota(jnp.int32, (rows, 1), 0) % CAP
    return (row == jnp.broadcast_to(target, (rows, tokens))).astype(jnp.float32).astype(jnp.bfloat16)


def grid_of(chips):
    inner = 1 << (int(math.log2(chips)) // 2)
    return chips // inner, inner


def partner_chips(chips, index):
    outers, inners = grid_of(chips)
    here = lax.axis_index("expert") // 2
    return here ^ ((index % outers) * inners + index // outers)


def in_hbm(x):
    return pltpu.with_memory_space_constraint(x, pltpu.HBM)


def in_vmem(x):
    return pltpu.with_memory_space_constraint(x, pltpu.VMEM)


def blocks_in_vmem(x):
    return in_vmem(x) if x.size <= MIB else x


def blocks_out(shape):
    if math.prod(shape) <= MIB:
        return pltpu.VMEM(shape, jnp.bfloat16)
    return jax.ShapeDtypeStruct(shape, jnp.bfloat16)


def join_rows(blocks_ref, rows_ref, first):
    for i in range(blocks_ref.shape[0]):
        rows_ref[first + i * CAP : first + (i + 1) * CAP, :] = blocks_ref[i].astype(rows_ref.dtype)


def fetch_parts(weight_ref, first, out_ref, sems):
    depth = out_ref.shape[0] // sems.shape[0]
    return [
        pltpu.make_async_copy(
            weight_ref.at[pl.ds(first + i * depth, depth)],
            out_ref.at[pl.ds(i * depth, depth)],
            sems.at[i],
        )
        for i in range(sems.shape[0])
    ]


def pack_kernel(first, outers, *refs):
    ids_ref, tokens_ref, gain_ref, router_ref, weight_ref = refs[:5]
    outs, held_ref = refs[5:-7], refs[-7]
    ids, tokens, gain, router, sems, fetch_sems = refs[-6:]
    pairs = ((ids_ref, ids), (tokens_ref, tokens), (gain_ref, gain), (router_ref, router))
    moves = [pltpu.make_async_copy(a, b, sems.at[i]) for i, (a, b) in enumerate(pairs)]
    for move in moves:
        move.start()
    parts = fetch_parts(weight_ref, first, held_ref, fetch_sems)
    for part in parts:
        part.start()
    chips = outers * len(outs)
    rows = chips * CAP
    copies = chips // EXP_FL
    index = lax.broadcasted_iota(jnp.int32, (rows, 1), 0) // CAP
    experts = partner_chips(chips, index) // copies
    moves[0].wait()
    layout = slot_layout(ids[...], experts)
    moves[1].wait()
    packed = jnp.dot(layout, tokens[...], preferred_element_type=jnp.float32)
    mean_square = jnp.mean(packed * packed, axis=-1, keepdims=True)
    moves[2].wait()
    normed = (packed * lax.rsqrt(mean_square + 1e-05) * gain[...]).astype(jnp.bfloat16)
    moves[3].wait()
    logits = lax.dot_general(
        normed, router[...], (((1,), (1,)), ((), ())), preferred_element_type=jnp.float32
    )
    own = lax.broadcasted_iota(jnp.int32, logits.shape, 1) == experts
    logit = jnp.sum(jnp.where(own, logits, 0.0), axis=-1, keepdims=True)
    routed = normed.astype(jnp.float32) * jax.nn.sigmoid(logit)
    for i in range(chips):
        outs[i // outers][i % outers] = routed[i * CAP : (i + 1) * CAP].astype(jnp.bfloat16)
    for part in parts:
        part.wait()


def pack(tokens, ids, gain, router_rows, weight, chips, first, count):
    width = tokens.shape[1]
    units = weight.shape[1]
    outers, inners = grid_of(chips)
    arrays = (ids, tokens, gain, router_rows)
    vmem = pl.BlockSpec(memory_space=pltpu.VMEM)
    outs = pl.pallas_call(
        functools.partial(pack_kernel, first * DEEP, outers),
        in_specs=[pl.BlockSpec(memory_space=pl.ANY)] * 5,
        out_specs=[vmem] * (inners + 1),
        out_shape=[blocks_out((outers, CAP, width))] * inners
        + [pltpu.VMEM((count * DEEP, units), weight.dtype)],
        scratch_shapes=[pltpu.VMEM(x.shape, x.dtype) for x in arrays]
        + [pltpu.SemaphoreType.DMA((4,)), pltpu.SemaphoreType.DMA((count,))],
        compiler_params=pltpu.CompilerParams(vmem_limit_bytes=(12 if chips <= 8 else 40) * MIB),
        name="pack",
    )(*[in_hbm(x) for x in (*arrays, weight)])
    return outs[:-1], outs[-1]


def fetch_kernel(first, weight_ref, out_ref, sems):
    parts = fetch_parts(weight_ref, first, out_ref, sems)
    for part in parts:
        part.start()
    for part in parts:
        part.wait()


def fetch(weight, first, count):
    return pl.pallas_call(
        functools.partial(fetch_kernel, first * DEEP),
        in_specs=[pl.BlockSpec(memory_space=pl.ANY)],
        out_specs=pl.BlockSpec(memory_space=pltpu.VMEM),
        out_shape=pltpu.VMEM((count * DEEP, weight.shape[1]), weight.dtype),
        scratch_shapes=[pltpu.SemaphoreType.DMA((count,))],
        compiler_params=pltpu.CompilerParams(vmem_limit_bytes=1 * MIB),
        cost_estimate=pl.CostEstimate(
            flops=0,
            bytes_accessed=count * DEEP * weight.shape[1] * weight.dtype.itemsize,
            transcendentals=0,
        ),
        name="fetch",
    )(in_hbm(weight))


def regroup_kernel(first, groups, *refs):
    for i, out_ref in enumerate(refs[groups:]):
        for j in range(groups):
            out_ref[j] = refs[j][first + i]


def regroup(arrays, first):
    count, _, width = arrays[0].shape
    vmem = pl.BlockSpec(memory_space=pltpu.VMEM)
    return pl.pallas_call(
        functools.partial(regroup_kernel, first, len(arrays)),
        in_specs=[vmem] * len(arrays),
        out_specs=[vmem] * (count - first),
        out_shape=[blocks_out((len(arrays), CAP, width))] * (count - first),
        compiler_params=pltpu.CompilerParams(vmem_limit_bytes=(4 if count <= 8 else 24) * MIB),
        name="regroup",
    )(*[blocks_in_vmem(x) for x in arrays])


def gather_kernel(kept, *refs):
    out_ref = refs[-1]
    for i in range(kept):
        out_ref[i] = refs[i][0]
    for i, ref in enumerate(refs[kept:-1]):
        out_ref[(i + 1) * kept : (i + 2) * kept] = ref[...]


def gather(kept, arrived):
    arrays = (*kept, *arrived)
    _, _, width = kept[0].shape
    chips = len(kept) * (len(arrived) + 1)
    return pl.pallas_call(
        functools.partial(gather_kernel, len(kept)),
        in_specs=[pl.BlockSpec(memory_space=pltpu.VMEM)] * len(arrays),
        out_specs=pl.BlockSpec(memory_space=pltpu.VMEM),
        out_shape=blocks_out((chips, CAP, width)),
        compiler_params=pltpu.CompilerParams(vmem_limit_bytes=(4 if chips <= 8 else 24) * MIB),
        name="gather",
    )(*[blocks_in_vmem(x) for x in arrays])


def ffn_kernel(
    deep,
    wide,
    held,
    mine_ref,
    other_ref,
    gate_ref,
    up_ref,
    down_ref,
    *refs,
):
    held_refs, (own_ref, lent_ref, sems, x_ref, acc_a, acc_b, acc_c, hid, ring, *rings) = (
        refs[: len(held)],
        refs[len(held) :],
    )
    down_ring = rings[0] if rings else ring
    chips, _, width = mine_ref.shape
    units = gate_ref.shape[1]
    slots = ring.shape[0]
    chunks = width // deep
    gates = chunks - sum(held)
    ups = gates + chunks
    down_deep = min(deep, units)
    downs_k = units // down_deep
    halves = width // wide
    total = ups + halves * downs_k

    def gate_copy(i):
        slot = lax.rem(i, slots)
        row = pl.multiple_of((i + chunks - gates) * deep, deep)
        return pltpu.make_async_copy(gate_ref.at[pl.ds(row, deep)], ring.at[slot], sems.at[slot])

    def up_copy(i):
        slot = lax.rem(i, slots)
        row = pl.multiple_of((i - gates) * deep, deep)
        return pltpu.make_async_copy(up_ref.at[pl.ds(row, deep)], ring.at[slot], sems.at[slot])

    def down_copy(i):
        slot = lax.rem(i, slots)
        j = i - ups
        row = pl.multiple_of(lax.rem(j, downs_k) * down_deep, down_deep)
        col = pl.multiple_of((j // downs_k) * wide, wide)
        return pltpu.make_async_copy(
            down_ref.at[pl.ds(row, down_deep), pl.ds(col, wide)],
            down_ring.at[slot],
            sems.at[slot],
        )

    def start(i):
        @pl.when(i < gates)
        def _():
            gate_copy(i).start()

        @pl.when(jnp.logical_and(i >= gates, i < ups))
        def _():
            up_copy(i).start()

        @pl.when(jnp.logical_and(i >= ups, i < total))
        def _():
            down_copy(i).start()

    @pl.loop(0, min(slots, total))
    def _(i):
        start(i)

    join_rows(mine_ref, x_ref, 0)
    join_rows(other_ref, x_ref, chips * CAP)
    acc_a[...] = jnp.zeros_like(acc_a)
    acc_b[...] = jnp.zeros_like(acc_b)

    done = 0
    for held_ref, count in zip(held_refs, held):

        @pl.loop(0, count)
        def _(i, held_ref=held_ref, done=done):
            acc_a[...] += jnp.dot(
                x_ref[:, pl.ds(pl.multiple_of((done + i) * deep, deep), deep)],
                held_ref[pl.ds(pl.multiple_of(i * deep, deep), deep), :],
                preferred_element_type=jnp.float32,
            )

        done += count

    for acc, copy_of, begin, end, base in (
        (acc_a, gate_copy, 0, gates, done),
        (acc_b, up_copy, gates, ups, -gates),
    ):

        @pl.loop(begin, end)
        def _(i, acc=acc, copy_of=copy_of, base=base):
            copy_of(i).wait()
            acc[...] += jnp.dot(
                x_ref[:, pl.ds(pl.multiple_of((base + i) * deep, deep), deep)],
                ring[lax.rem(i, slots)],
                preferred_element_type=jnp.float32,
            )
            start(i + slots)

    gate = acc_a[...]
    hid[...] = (gate / (1.0 + jnp.exp(-gate)) * acc_b[...]).astype(jnp.bfloat16)

    for half in range(halves):
        acc_c[...] = jnp.zeros_like(acc_c)

        @pl.loop(0, downs_k)
        def _(k, half=half):
            i = ups + half * downs_k + k
            slot = lax.rem(i, slots)
            down_copy(i).wait()
            row = pl.multiple_of(k * down_deep, down_deep)
            acc_c[...] += jnp.dot(
                hid[:, pl.ds(row, down_deep)] if downs_k > 1 else hid[...],
                down_ring[slot],
                preferred_element_type=jnp.float32,
            )
            start(i + slots)

        for i in range(chips):
            for part_ref, first in ((own_ref, 0), (lent_ref, chips * CAP)):
                part_ref[i, :, half * wide : (half + 1) * wide] = acc_c[
                    first + i * CAP : first + (i + 1) * CAP, :
                ].astype(jnp.bfloat16)


def ffn(mine, other, gate, held, up, down):
    chips, _, width = mine.shape
    rows = 2 * chips * CAP
    units = gate.shape[1]
    deep, wide = DEEP, width // 2
    slots = 11 if rows <= 64 else 6
    down_deep = min(deep, units)
    rings = [pltpu.VMEM((slots, deep, units), jnp.bfloat16)]
    if (down_deep, wide) != (deep, units):
        rings.append(pltpu.VMEM((slots, down_deep, wide), jnp.bfloat16))
    vmem = pl.BlockSpec(memory_space=pltpu.VMEM)
    return pl.pallas_call(
        functools.partial(ffn_kernel, deep, wide, [x.shape[0] // deep for x in held]),
        in_specs=[vmem] * 2 + [pl.BlockSpec(memory_space=pl.ANY)] * 3 + [vmem] * len(held),
        out_specs=[vmem, vmem],
        out_shape=[blocks_out(mine.shape)] * 2,
        scratch_shapes=[
            pltpu.SemaphoreType.DMA((slots,)),
            pltpu.VMEM((rows, width), jnp.bfloat16),
            pltpu.VMEM((rows, units), jnp.float32),
            pltpu.VMEM((rows, units), jnp.float32),
            pltpu.VMEM((rows, wide), jnp.float32),
            pltpu.VMEM((rows, units), jnp.bfloat16),
            *rings,
        ],
        compiler_params=pltpu.CompilerParams(vmem_limit_bytes=(34 if rows <= 64 else 52) * MIB),
        cost_estimate=pl.CostEstimate(
            flops=6 * rows * width * units,
            bytes_accessed=4 * width * units,
            transcendentals=rows * units,
        ),
        name="ffn",
    )(
        blocks_in_vmem(mine),
        blocks_in_vmem(other),
        in_hbm(gate),
        in_hbm(up),
        in_hbm(down),
        *[in_vmem(x) for x in held],
    )


def add_kernel(a_ref, b_ref, out_ref):
    chips = a_ref.shape[0]
    outers, inners = grid_of(chips)
    for i in range(chips):
        chip = partner_chips(chips, (i % inners) * outers + i // inners)
        out_ref[chip] = (a_ref[i].astype(jnp.float32) + b_ref[i].astype(jnp.float32)).astype(
            jnp.bfloat16
        )


def add(a, b):
    return pl.pallas_call(
        add_kernel,
        in_specs=[pl.BlockSpec(memory_space=pltpu.VMEM)] * 2,
        out_specs=pl.BlockSpec(memory_space=pltpu.VMEM),
        out_shape=blocks_out(a.shape),
        compiler_params=pltpu.CompilerParams(vmem_limit_bytes=16 * MIB),
        name="add",
    )(blocks_in_vmem(a), blocks_in_vmem(b))


def unpack_kernel(ids_ref, blocks_ref, out_ref, rows, out, sems):
    experts = lax.broadcasted_iota(jnp.int32, (rows.shape[0], 1), 0) // CAP
    layout = slot_layout(ids_ref[...], experts)
    copies = blocks_ref.shape[0] // EXP_FL
    for expert in range(EXP_FL):
        block = blocks_ref[expert * copies].astype(jnp.float32)
        for i in range(1, copies):
            block += blocks_ref[expert * copies + i].astype(jnp.float32)
        rows[expert * CAP : (expert + 1) * CAP, :] = block
    count = sems.shape[0]
    part = rows.shape[1] // count
    moves = []
    for i in range(count):
        columns = slice(i * part, (i + 1) * part)
        out[:, columns] = lax.dot_general(
            layout,
            rows[:, columns].astype(jnp.bfloat16),
            (((0,), (0,)), ((), ())),
            preferred_element_type=jnp.float32,
        ).astype(jnp.bfloat16)
        moves.append(pltpu.make_async_copy(out.at[:, columns], out_ref.at[:, columns], sems.at[i]))
        moves[-1].start()
    for move in moves:
        move.wait()


def unpack(blocks, ids):
    chips, _, width = blocks.shape
    shape = (ids.shape[1], width)
    return pl.pallas_call(
        unpack_kernel,
        in_specs=[pl.BlockSpec(memory_space=pltpu.VMEM)] * 2,
        out_specs=pl.BlockSpec(memory_space=pl.ANY),
        out_shape=jax.ShapeDtypeStruct(shape, jnp.bfloat16),
        scratch_shapes=[
            pltpu.VMEM((EXP_FL * CAP, width), jnp.float32),
            pltpu.VMEM(shape, jnp.bfloat16),
            pltpu.SemaphoreType.DMA((4,)),
        ],
        compiler_params=pltpu.CompilerParams(vmem_limit_bytes=16 * MIB),
        name="unpack",
    )(ids, blocks_in_vmem(blocks))


def per_device(tokens, expert_ids, norm_gain, router, gate_weight, up_weight, down_weight):
    devices = lax.axis_size("expert")
    chips = devices // 2
    outers, inners = grid_of(chips)
    same_core = [list(range(core, devices, 2)) for core in range(2)]
    ids = expert_ids.reshape(1, -1)

    def exchange(x, offset):
        return lax.ppermute(x, "expert", [(i, i ^ offset) for i in range(devices)])

    packed, held_a = pack(tokens, ids, norm_gain.reshape(1, -1), router.T, gate_weight, chips, 0, 2)
    arrived = [exchange(packed[i], 2 * i) for i in range(1, inners)]
    held_b = fetch(gate_weight, 2, 2)
    arrived, held_b = lax.optimization_barrier((arrived, held_b))
    near = [packed[0], *arrived]
    leaving = regroup(near, 1)
    far = [exchange(leaving[i - 1], 2 * inners * i) for i in range(1, outers)]
    leaving, gate = lax.optimization_barrier((leaving, gate_weight))
    held_c = fetch(gate, 4, 4)
    far, held_c = lax.optimization_barrier((far, held_c))
    mine = gather(near, far)
    other = exchange(mine, 1)
    own, lent = ffn(mine, other, gate_weight, (held_a, held_b, held_c), up_weight, down_weight)
    total = add(own, exchange(lent, 1))
    returned = lax.all_to_all(
        total, "expert", split_axis=0, concat_axis=0, tiled=True, axis_index_groups=same_core
    )
    return unpack(returned, ids)


def solution(mesh):
    in_specs = (
        P(("groups", "expert"), None),
        P(("groups", "expert")),
        P(),
        P(),
        P(None, "expert"),
        P(None, "expert"),
        P("expert", None),
    )
    out_specs = P(("groups", "expert"), None)
    return jax.shard_map(
        per_device, mesh=mesh, in_specs=in_specs, out_specs=out_specs, check_vma=False
    )
```

time: 89.9 us -> 59.9 us (0.67)
  local copies, waits for them, and re-layouts: 23 us -> 0.01 us
  blocking collectives: 32.2 us -> 15.1 us
  starting transfers between devices: 0.58 us -> 7.76 us
  waiting for transfers between devices: 1.26 us -> 6.98 us
  other arithmetic: 1.48 us -> 0 us
  Pallas kernels: 30.9 us -> 29.9 us
    unnamed x14 -> x2, local copies, waits for them, and re-layouts: 20.7 us -> 0.01 us
    all_to_all x2 -> x1, blocking collectives: 32.2 us -> 15.1 us  [per_device(): lax.all_to_all(total, 'expert', split_axis=0, concat_axis=0, tiled=True,...]
    ppermute x2 -> x6, starting transfers between devices: 0.58 us -> 7.76 us  [exchange(): return lax.ppermute(x, 'expert', [(i, i ^ offset) for i in range(devices)])]
    ppermute x2 -> x6, waiting for transfers between devices: 1.26 us -> 6.98 us  [exchange(): return lax.ppermute(x, 'expert', [(i, i ^ offset) for i in range(devices)])]
    reshape x3 -> x0, local copies, waits for them, and re-layouts: 1.19 us -> none  [the longest x1 0.99 us: per_device(): x = jnp.concatenate([mine, other], axis=0).reshape(2 * chips * CAP, width)]
    convert_element_type x1 -> x0, other arithmetic: 1.05 us -> none  [per_device(): (own.astype(jnp.float32) + back.astype(jnp.float32)).astype(jnp.bfloat16)]
    pallas_call x4 -> x8, Pallas kernels: 30.9 us -> 29.9 us  [the longest x1 18.5 us: ffn(): pl.pallas_call(functools.partial(ffn_kernel, deep, wide, [x.shape[0] // d...]
    slice x1 -> x0, local copies, waits for them, and re-layouts: 1 us -> none  [per_device(): own, lent = (partial[:chips * CAP], partial[chips * CAP:])]
  transfers between devices with their start and end apart: 2 -> 6, of which waited for: 1 -> 5; matrix products, arithmetic and copies ran while one was open for 0% -> 0% of each run, Pallas kernels for 10% -> 11%
where the time goes in v2:
time: 59.9 us; the launch traced here: 59.8 us
  Pallas kernels  29.9 us (50%)
  blocking collectives  15.1 us (25%)
  starting transfers between devices  7.76 us (13%)
  waiting for transfers between devices  6.98 us (12%)
    pallas_call x1, Pallas kernels, ffn(): pl.pallas_call(functools.partial(ffn_kernel, deep, wide, [x.shape[0] // d...  18.5 us
    all_to_all x1, blocking collectives, per_device(): lax.all_to_all(total, 'expert', split_axis=0, concat_axis=0, tiled=True,...  15.1 us
    ppermute x6, starting transfers between devices, exchange(): return lax.ppermute(x, 'expert', [(i, i ^ offset) for i in range(devices)])  7.76 us
    ppermute x6, waiting for transfers between devices, exchange(): return lax.ppermute(x, 'expert', [(i, i ^ offset) for i in range(devices)])  6.98 us
    pallas_call x2, Pallas kernels, fetch(): pl.pallas_call(functools.partial(fetch_kernel, first * DEEP), in_specs=[p...  6.64 us
    pallas_call x1, Pallas kernels, pack(): pl.pallas_call(functools.partial(pack_kernel, first * DEEP, outers), in_s...  3.04 us
    pallas_call x1, Pallas kernels, unpack(): pl.pallas_call(unpack_kernel, in_specs=[pl.BlockSpec(memory_space=pltpu.V...  1.54 us
  transfers between devices with their start and end apart: 6, of which 5 were waited for; matrix products, arithmetic and copies ran while one was open for 0% of the time, Pallas kernels for 11%

profile of v2, /device:TPU:0, one launch (start us, length us, event | category | flops | bytes accessed | tf_op | source)
XLA Modules:
  0.0 59.8 jit_solution(12914075946117455929)
XLA Ops:
  0.0 3.0 %pack.1 = (bf16[4,4,5120]{2,1,0:T(4,128)(2,1)S(1)}, bf16[4,4,5120]{2,1,0:T(4,128)(2,1)S(1)}, bf16[1024,2560]{1,0:T(8,128)(2,1)S(1)}) custom-call(s32[1,128]{1,0:T(1,128)} %bitcast.3, bf16[128,5120]{1,0:T(8,128)(2,1)} %refs_1_.1, f32[1,5120]{1,0:T(1,128)} %bitcast.6, bf16[8,5120]{1,0:T(8,128)(2,1)} %bitcast.5, bf16[5120,2560]{1,0:T(8,128)(2,1)} %gate_ref.1), custom_call_target="tpu_custom_call" | custom-call | tf_op jit(solution)/shard_map/pack/pallas_call | solution.py:124
  3.1 3.0 %collective-permute-start = (bf16[4,4,5120]{2,1,0:T(4,128)(2,1)S(1)}, bf16[4,4,5120]{2,1,0:T(4,128)(2,1)S(1)}, u32[]{:S(2)}, u32[]{:S(2)}) collective-permute-start(bf16[4,4,5120]{2,1,0:T(4,128)(2,1)S(1)} %get-tuple-element.21), channel_id=1, source_target_pairs={{0,2},{1,3},{2,0},{3,1},{4,6},{5,7},{6,4},{7,5},{8,10},{9,11},{10,... | collective-permute-start | bytes 491528 | tf_op jit(solution)/shard_map/ppermute | solution.py:443
  6.1 2.5 %fetch.2.refs_1_ = bf16[1024,2560]{1,0:T(8,128)(2,1)S(1)} custom-call(bf16[5120,2560]{1,0:T(8,128)(2,1)} %gate_ref.1), custom_call_target="tpu_custom_call" | custom-call | bytes 5242880 | tf_op jit(solution)/shard_map/fetch/pallas_call | solution.py:147
  8.6 1.6 %collective-permute-done.refs_1_ = bf16[4,4,5120]{2,1,0:T(4,128)(2,1)S(1)} collective-permute-done((bf16[4,4,5120]{2,1,0:T(4,128)(2,1)S(1)}, bf16[4,4,5120]{2,1,0:T(4,128)(2,1)S(1)}, u32[]{:S(2)}, u32[]{:S(2)}) %collective-permute-start) | collective-permute-done | bytes 163872 | tf_op jit(solution)/shard_map/ppermute | solution.py:443
  10.3 1.9 %collective-permute-start.1 = (bf16[2,4,5120]{2,1,0:T(4,128)(2,1)S(1)}, bf16[2,4,5120]{2,1,0:T(4,128)(2,1)S(1)}, u32[]{:S(2)}, u32[]{:S(2)}) collective-permute-start(bf16[2,4,5120]{2,1,0:T(4,128)(2,1)S(1)} %get-tuple-element.23), channel_id=1, source_target_pairs={{0,4},{1,5},{2,6},{3,7},{4,0},{5,1},{6,2},{7,3},{8,12},{9,13},{10,... | collective-permute-start | bytes 245768 | tf_op jit(solution)/shard_map/ppermute | solution.py:443
  12.2 2.6 %collective-permute-start.2 = (bf16[2,4,5120]{2,1,0:T(4,128)(2,1)S(1)}, bf16[2,4,5120]{2,1,0:T(4,128)(2,1)S(1)}, u32[]{:S(2)}, u32[]{:S(2)}) collective-permute-start(bf16[2,4,5120]{2,1,0:T(4,128)(2,1)S(1)} %get-tuple-element.24), channel_id=1, source_target_pairs={{0,8},{1,9},{2,10},{3,11},{4,12},{5,13},{6,14},{7,15},{8,0},{9,1},... | collective-permute-start | bytes 245768 | tf_op jit(solution)/shard_map/ppermute | solution.py:443
  14.8 0.0 collective-permute-start.3
  14.8 4.1 %fetch.3.refs_2_ = bf16[2048,2560]{1,0:T(8,128)(2,1)S(1)} custom-call(bf16[5120,2560]{1,0:T(8,128)(2,1)} %gate_ref.1), custom_call_target="tpu_custom_call" | custom-call | bytes 10485760 | tf_op jit(solution)/shard_map/fetch/pallas_call | solution.py:147
  18.9 0.0 collective-permute-done.1.refs_2_
  18.9 0.7 %collective-permute-done.2.refs_3_ = bf16[2,4,5120]{2,1,0:T(4,128)(2,1)S(1)} collective-permute-done((bf16[2,4,5120]{2,1,0:T(4,128)(2,1)S(1)}, bf16[2,4,5120]{2,1,0:T(4,128)(2,1)S(1)}, u32[]{:S(2)}, u32[]{:S(2)}) %collective-permute-start.2) | collective-permute-done | bytes 81952 | tf_op jit(solution)/shard_map/ppermute | solution.py:443
  19.6 1.5 %collective-permute-done.3.refs_4_ = bf16[2,4,5120]{2,1,0:T(4,128)(2,1)S(1)} collective-permute-done((bf16[2,4,5120]{2,1,0:T(4,128)(2,1)S(1)}, bf16[2,4,5120]{2,1,0:T(4,128)(2,1)S(1)}, u32[]{:S(2)}, u32[]{:S(2)}) %collective-permute-start.3) | collective-permute-done | bytes 81952 | tf_op jit(solution)/shard_map/ppermute | solution.py:443
  21.1 0.1 collective-permute-start.4
  21.2 1.6 %collective-permute-done.4.other_ref = bf16[8,4,5120]{2,1,0:T(4,128)(2,1)S(1)} collective-permute-done((bf16[8,4,5120]{2,1,0:T(4,128)(2,1)S(1)}, bf16[8,4,5120]{2,1,0:T(4,128)(2,1)S(1)}, u32[]{:S(2)}, u32[]{:S(2)}) %collective-permute-start.4) | collective-permute-done | bytes 327712 | tf_op jit(solution)/shard_map/ppermute | solution.py:443
  22.8 0.0 copy-start
  22.8 18.5 %ffn.1 = (bf16[8,4,5120]{2,1,0:T(4,128)(2,1)S(1)}, bf16[8,4,5120]{2,1,0:T(4,128)(2,1)S(1)}) custom-call(bf16[8,4,5120]{2,1,0:T(4,128)(2,1)S(1)} %gather.1.mine_ref, bf16[8,4,5120]{2,1,0:T(4,128)(2,1)S(1)} %collective-permute-done.4.other_ref, bf16[5120,2560]{1,0:T(8,128)(2,1)} %gate_ref.1, bf16[5120,2560]{1,0:T(8,128)(2,1)} %up_ref.1, ...), custom_call_target="tpu_custom_call" | custom-call | flops 5033164800 | bytes 52428800 | tf_op jit(solution)/shard_map/ffn/pallas_call | solution.py:339
  41.3 0.2 collective-permute-start.5
  41.5 1.5 %collective-permute-done.5.b_ref = bf16[8,4,5120]{2,1,0:T(4,128)(2,1)S(1)} collective-permute-done((bf16[8,4,5120]{2,1,0:T(4,128)(2,1)S(1)}, bf16[8,4,5120]{2,1,0:T(4,128)(2,1)S(1)}, u32[]{:S(2)}, u32[]{:S(2)}) %collective-permute-start.5) | collective-permute-done | bytes 327712 | tf_op jit(solution)/shard_map/ppermute | solution.py:443
  43.0 0.1 add.1
  43.1 15.1 %all_to_all.5.blocks_ref = bf16[8,4,5120]{2,1,0:T(4,128)(2,1)S(1)} all-to-all(bf16[8,4,5120]{2,1,0:T(4,128)(2,1)S(1)} %add.1), channel_id=1, replica_groups={{0,2,4,6,8,10,12,14},{1,3,5,7,9,11,13,15},{16,18,20,22,24,26,28,30},{17..., dimensions={0} | all-to-all | bytes 655360 | tf_op jit(solution)/shard_map/all_to_all | solution.py:459
  58.2 0.0 copy-done
  58.2 1.5 %unpack.1 = bf16[128,5120]{1,0:T(8,128)(2,1)} custom-call(s32[1,128]{1,0:T(1,128)S(1)} %bitcast.4, bf16[8,4,5120]{2,1,0:T(4,128)(2,1)S(1)} %all_to_all.5.blocks_ref), custom_call_target="tpu_custom_call" | custom-call | tf_op jit(solution)/shard_map/unpack/pallas_call | solution.py:420
  (2 shorter events, 0.0 us)
Async XLA Ops:
  3.1 7.2 %collective-permute-start = (bf16[4,4,5120]{2,1,0:T(4,128)(2,1)S(1)}, bf16[4,4,5120]{2,1,0:T(4,128)(2,1)S(1)}, u32[]{:S(2)}, u32[]{:S(2)}) collective-permute-start(bf16[4,4,5120]{2,1,0:T(4,128)(2,1)S(1)} %get-tuple-element.21), channel_id=1, source_target_pairs={{0,2},{1,3},{2,0},{3,1},{4,6},{5,7},{6,4},{7,5},{8,10},{9,11},{10,... | collective-permute-start | bytes 491528 | tf_op jit(solution)/shard_map/ppermute | solution.py:443
  10.3 8.6 %collective-permute-start.1 = (bf16[2,4,5120]{2,1,0:T(4,128)(2,1)S(1)}, bf16[2,4,5120]{2,1,0:T(4,128)(2,1)S(1)}, u32[]{:S(2)}, u32[]{:S(2)}) collective-permute-start(bf16[2,4,5120]{2,1,0:T(4,128)(2,1)S(1)} %get-tuple-element.23), channel_id=1, source_target_pairs={{0,4},{1,5},{2,6},{3,7},{4,0},{5,1},{6,2},{7,3},{8,12},{9,13},{10,... | collective-permute-start | bytes 245768 | tf_op jit(solution)/shard_map/ppermute | solution.py:443
  12.2 7.4 %collective-permute-start.2 = (bf16[2,4,5120]{2,1,0:T(4,128)(2,1)S(1)}, bf16[2,4,5120]{2,1,0:T(4,128)(2,1)S(1)}, u32[]{:S(2)}, u32[]{:S(2)}) collective-permute-start(bf16[2,4,5120]{2,1,0:T(4,128)(2,1)S(1)} %get-tuple-element.24), channel_id=1, source_target_pairs={{0,8},{1,9},{2,10},{3,11},{4,12},{5,13},{6,14},{7,15},{8,0},{9,1},... | collective-permute-start | bytes 245768 | tf_op jit(solution)/shard_map/ppermute | solution.py:443
  14.8 6.3 %collective-permute-start.3 = (bf16[2,4,5120]{2,1,0:T(4,128)(2,1)S(1)}, bf16[2,4,5120]{2,1,0:T(4,128)(2,1)S(1)}, u32[]{:S(2)}, u32[]{:S(2)}) collective-permute-start(bf16[2,4,5120]{2,1,0:T(4,128)(2,1)S(1)} %get-tuple-element.25), channel_id=1, source_target_pairs={{0,12},{1,13},{2,14},{3,15},{4,8},{5,9},{6,10},{7,11},{8,4},{9,5},... | collective-permute-start | bytes 245768 | tf_op jit(solution)/shard_map/ppermute | solution.py:443
  21.1 1.7 %collective-permute-start.4 = (bf16[8,4,5120]{2,1,0:T(4,128)(2,1)S(1)}, bf16[8,4,5120]{2,1,0:T(4,128)(2,1)S(1)}, u32[]{:S(2)}, u32[]{:S(2)}) collective-permute-start(bf16[8,4,5120]{2,1,0:T(4,128)(2,1)S(1)} %gather.1.mine_ref), channel_id=1, source_target_pairs={{0,1},{1,0},{2,3},{3,2},{4,5},{5,4},{6,7},{7,6},{8,9},{9,8},{10,11... | collective-permute-start | bytes 983048 | tf_op jit(solution)/shard_map/ppermute | solution.py:443
  22.8 35.4 %copy-start = (s32[128]{0:T(128)S(1)}, s32[128]{0:T(128)}, u32[]{:S(2)}) copy-start(s32[128]{0:T(128)} %param.8) | copy-start | bytes 1540
  41.3 1.7 %collective-permute-start.5 = (bf16[8,4,5120]{2,1,0:T(4,128)(2,1)S(1)}, bf16[8,4,5120]{2,1,0:T(4,128)(2,1)S(1)}, u32[]{:S(2)}, u32[]{:S(2)}) collective-permute-start(bf16[8,4,5120]{2,1,0:T(4,128)(2,1)S(1)} %get-tuple-element.34), channel_id=1, source_target_pairs={{0,1},{1,0},{2,3},{3,2},{4,5},{5,4},{6,7},{7,6},{8,9},{9,8},{10,11... | collective-permute-start | bytes 983048 | tf_op jit(solution)/shard_map/ppermute | solution.py:443

commit v3 on v2

--- a/solution.py
+++ b/solution.py
@@ -67,30 +67,15 @@
         rows_ref[first + i * CAP : first + (i + 1) * CAP, :] = blocks_ref[i].astype(rows_ref.dtype)
 
 
-def fetch_parts(weight_ref, first, out_ref, sems):
-    depth = out_ref.shape[0] // sems.shape[0]
-    return [
-        pltpu.make_async_copy(
-            weight_ref.at[pl.ds(first + i * depth, depth)],
-            out_ref.at[pl.ds(i * depth, depth)],
-            sems.at[i],
-        )
-        for i in range(sems.shape[0])
-    ]
-
-
-def pack_kernel(first, outers, *refs):
-    ids_ref, tokens_ref, gain_ref, router_ref, weight_ref = refs[:5]
-    outs, held_ref = refs[5:-7], refs[-7]
-    ids, tokens, gain, router, sems, fetch_sems = refs[-6:]
+def pack_kernel(outers, *refs):
+    ids_ref, tokens_ref, gain_ref, router_ref = refs[:4]
+    outs, (ids, tokens, gain, router, sems) = refs[5:-5], refs[-5:]
     pairs = ((ids_ref, ids), (tokens_ref, tokens), (gain_ref, gain), (router_ref, router))
     moves = [pltpu.make_async_copy(a, b, sems.at[i]) for i, (a, b) in enumerate(pairs)]
     for move in moves:
         move.start()
-    parts = fetch_parts(weight_ref, first, held_ref, fetch_sems)
-    for part in parts:
-        part.start()
-    chips = outers * len(outs)
+    inners = len(outs)
+    chips = outers * inners
     rows = chips * CAP
     copies = chips // EXP_FL
     index = lax.broadcasted_iota(jnp.int32, (rows, 1), 0) // CAP
@@ -111,53 +96,22 @@
     routed = normed.astype(jnp.float32) * jax.nn.sigmoid(logit)
     for i in range(chips):
         outs[i // outers][i % outers] = routed[i * CAP : (i + 1) * CAP].astype(jnp.bfloat16)
-    for part in parts:
-        part.wait()
-
-
-def pack(tokens, ids, gain, router_rows, weight, chips, first, count):
+
+
+def pack(tokens, ids, gain, router_rows, weight, chips):
     width = tokens.shape[1]
-    units = weight.shape[1]
     outers, inners = grid_of(chips)
     arrays = (ids, tokens, gain, router_rows)
-    vmem = pl.BlockSpec(memory_space=pltpu.VMEM)
-    outs = pl.pallas_call(
-        functools.partial(pack_kernel, first * DEEP, outers),
+    return pl.pallas_call(
+        functools.partial(pack_kernel, outers),
         in_specs=[pl.BlockSpec(memory_space=pl.ANY)] * 5,
-        out_specs=[vmem] * (inners + 1),
-        out_shape=[blocks_out((outers, CAP, width))] * inners
-        + [pltpu.VMEM((count * DEEP, units), weight.dtype)],
+        out_specs=[pl.BlockSpec(memory_space=pltpu.VMEM)] * inners,
+        out_shape=[blocks_out((outers, CAP, width))] * inners,
         scratch_shapes=[pltpu.VMEM(x.shape, x.dtype) for x in arrays]
-        + [pltpu.SemaphoreType.DMA((4,)), pltpu.SemaphoreType.DMA((count,))],
+        + [pltpu.SemaphoreType.DMA((4,))],
         compiler_params=pltpu.CompilerParams(vmem_limit_bytes=(12 if chips <= 8 else 40) * MIB),
         name="pack",
     )(*[in_hbm(x) for x in (*arrays, weight)])
-    return outs[:-1], outs[-1]
-
-
-def fetch_kernel(first, weight_ref, out_ref, sems):
-    parts = fetch_parts(weight_ref, first, out_ref, sems)
-    for part in parts:
-        part.start()
-    for part in parts:
-        part.wait()
-
-
-def fetch(weight, first, count):
-    return pl.pallas_call(
-        functools.partial(fetch_kernel, first * DEEP),
-        in_specs=[pl.BlockSpec(memory_space=pl.ANY)],
-        out_specs=pl.BlockSpec(memory_space=pltpu.VMEM),
-        out_shape=pltpu.VMEM((count * DEEP, weight.shape[1]), weight.dtype),
-        scratch_shapes=[pltpu.SemaphoreType.DMA((count,))],
-        compiler_params=pltpu.CompilerParams(vmem_limit_bytes=1 * MIB),
-        cost_estimate=pl.CostEstimate(
-            flops=0,
-            bytes_accessed=count * DEEP * weight.shape[1] * weight.dtype.itemsize,
-            transcendentals=0,
-        ),
-        name="fetch",
-    )(in_hbm(weight))
 
 
 def regroup_kernel(first, groups, *refs):
@@ -204,38 +158,35 @@
 def ffn_kernel(
     deep,
     wide,
-    held,
     mine_ref,
     other_ref,
-    gate_ref,
     up_ref,
     down_ref,
-    *refs,
+    gate_ref,
+    own_ref,
+    lent_ref,
+    sems,
+    x_ref,
+    acc_a,
+    acc_b,
+    acc_c,
+    hid,
+    ring,
+    *rings,
 ):
-    held_refs, (own_ref, lent_ref, sems, x_ref, acc_a, acc_b, acc_c, hid, ring, *rings) = (
-        refs[: len(held)],
-        refs[len(held) :],
-    )
     down_ring = rings[0] if rings else ring
     chips, _, width = mine_ref.shape
     units = gate_ref.shape[1]
     slots = ring.shape[0]
-    chunks = width // deep
-    gates = chunks - sum(held)
-    ups = gates + chunks
+    ups = width // deep
     down_deep = min(deep, units)
     downs_k = units // down_deep
     halves = width // wide
     total = ups + halves * downs_k
 
-    def gate_copy(i):
-        slot = lax.rem(i, slots)
-        row = pl.multiple_of((i + chunks - gates) * deep, deep)
-        return pltpu.make_async_copy(gate_ref.at[pl.ds(row, deep)], ring.at[slot], sems.at[slot])
-
     def up_copy(i):
         slot = lax.rem(i, slots)
-        row = pl.multiple_of((i - gates) * deep, deep)
+        row = pl.multiple_of(i * deep, deep)
         return pltpu.make_async_copy(up_ref.at[pl.ds(row, deep)], ring.at[slot], sems.at[slot])
 
     def down_copy(i):
@@ -250,11 +201,7 @@
         )
 
     def start(i):
-        @pl.when(i < gates)
-        def _():
-            gate_copy(i).start()
-
-        @pl.when(jnp.logical_and(i >= gates, i < ups))
+        @pl.when(i < ups)
         def _():
             up_copy(i).start()
 
@@ -271,33 +218,23 @@
     acc_a[...] = jnp.zeros_like(acc_a)
     acc_b[...] = jnp.zeros_like(acc_b)
 
-    done = 0
-    for held_ref, count in zip(held_refs, held):
-
-        @pl.loop(0, count)
-        def _(i, held_ref=held_ref, done=done):
-            acc_a[...] += jnp.dot(
-                x_ref[:, pl.ds(pl.multiple_of((done + i) * deep, deep), deep)],
-                held_ref[pl.ds(pl.multiple_of(i * deep, deep), deep), :],
-                preferred_element_type=jnp.float32,
-            )
-
-        done += count
-
-    for acc, copy_of, begin, end, base in (
-        (acc_a, gate_copy, 0, gates, done),
-        (acc_b, up_copy, gates, ups, -gates),
-    ):
-
-        @pl.loop(begin, end)
-        def _(i, acc=acc, copy_of=copy_of, base=base):
-            copy_of(i).wait()
-            acc[...] += jnp.dot(
-                x_ref[:, pl.ds(pl.multiple_of((base + i) * deep, deep), deep)],
-                ring[lax.rem(i, slots)],
-                preferred_element_type=jnp.float32,
-            )
-            start(i + slots)
+    @pl.loop(0, ups)
+    def _(i):
+        row = pl.multiple_of(i * deep, deep)
+        acc_a[...] += jnp.dot(
+            x_ref[:, pl.ds(row, deep)],
+            gate_ref[pl.ds(row, deep), :],
+            preferred_element_type=jnp.float32,
+        )
+
+    @pl.loop(0, ups)
+    def _(i):
+        row = pl.multiple_of(i * deep, deep)
+        up_copy(i).wait()
+        acc_b[...] += jnp.dot(
+            x_ref[:, pl.ds(row, deep)], ring[lax.rem(i, slots)], preferred_element_type=jnp.float32
+        )
+        start(i + slots)
 
     gate = acc_a[...]
     hid[...] = (gate / (1.0 + jnp.exp(-gate)) * acc_b[...]).astype(jnp.bfloat16)
@@ -325,7 +262,7 @@
                 ].astype(jnp.bfloat16)
 
 
-def ffn(mine, other, gate, held, up, down):
+def ffn(mine, other, gate, up, down):
     chips, _, width = mine.shape
     rows = 2 * chips * CAP
     units = gate.shape[1]
@@ -337,8 +274,8 @@
         rings.append(pltpu.VMEM((slots, down_deep, wide), jnp.bfloat16))
     vmem = pl.BlockSpec(memory_space=pltpu.VMEM)
     return pl.pallas_call(
-        functools.partial(ffn_kernel, deep, wide, [x.shape[0] // deep for x in held]),
-        in_specs=[vmem] * 2 + [pl.BlockSpec(memory_space=pl.ANY)] * 3 + [vmem] * len(held),
+        functools.partial(ffn_kernel, deep, wide),
+        in_specs=[vmem] * 2 + [pl.BlockSpec(memory_space=pl.ANY)] * 2 + [vmem],
         out_specs=[vmem, vmem],
         out_shape=[blocks_out(mine.shape)] * 2,
         scratch_shapes=[
@@ -360,10 +297,9 @@
     )(
         blocks_in_vmem(mine),
         blocks_in_vmem(other),
-        in_hbm(gate),
         in_hbm(up),
         in_hbm(down),
-        *[in_vmem(x) for x in held],
+        in_vmem(gate),
     )
 
 
@@ -442,19 +378,12 @@
     def exchange(x, offset):
         return lax.ppermute(x, "expert", [(i, i ^ offset) for i in range(devices)])
 
-    packed, held_a = pack(tokens, ids, norm_gain.reshape(1, -1), router.T, gate_weight, chips, 0, 2)
-    arrived = [exchange(packed[i], 2 * i) for i in range(1, inners)]
-    held_b = fetch(gate_weight, 2, 2)
-    arrived, held_b = lax.optimization_barrier((arrived, held_b))
-    near = [packed[0], *arrived]
+    packed = pack(tokens, ids, norm_gain.reshape(1, -1), router.T, up_weight, chips)
+    near = [packed[0], *[exchange(packed[i], 2 * i) for i in range(1, inners)]]
     leaving = regroup(near, 1)
     far = [exchange(leaving[i - 1], 2 * inners * i) for i in range(1, outers)]
-    leaving, gate = lax.optimization_barrier((leaving, gate_weight))
-    held_c = fetch(gate, 4, 4)
-    far, held_c = lax.optimization_barrier((far, held_c))
     mine = gather(near, far)
-    other = exchange(mine, 1)
-    own, lent = ffn(mine, other, gate_weight, (held_a, held_b, held_c), up_weight, down_weight)
+    own, lent = ffn(mine, exchange(mine, 1), gate_weight, up_weight, down_weight)
     total = add(own, exchange(lent, 1))
     returned = lax.all_to_all(
         total, "expert", split_axis=0, concat_axis=0, tiled=True, axis_index_groups=same_core

time: 59.9 us -> 58.9 us (0.983)
  Pallas kernels: 29.9 us -> 22.1 us
  waiting for transfers between devices: 6.98 us -> 13.7 us
    pallas_call x4 -> x2, Pallas kernels: 28.1 us -> 20.4 us  [the longest x1 17.8 us: ffn(): pl.pallas_call(functools.partial(ffn_kernel, deep, wide), in_specs=[vmem]...]
    ppermute x6, waiting for transfers between devices: 6.98 us -> 13.7 us  [exchange(): return lax.ppermute(x, 'expert', [(i, i ^ offset) for i in range(devices)])]
  transfers between devices with their start and end apart: 6 -> 6, of which waited for: 5 -> 6; matrix products, arithmetic and copies ran while one was open for 0% -> 0% of each run, Pallas kernels for 11% -> 0%
where the time goes in v3:
time: 58.9 us; the launch traced here: 58.7 us
  Pallas kernels  22.1 us (38%)
  blocking collectives  15.1 us (26%)
  waiting for transfers between devices  13.7 us (23%)
  starting transfers between devices  7.72 us (13%)
    pallas_call x1, Pallas kernels, ffn(): pl.pallas_call(functools.partial(ffn_kernel, deep, wide), in_specs=[vmem]...  17.8 us
    all_to_all x1, blocking collectives, per_device(): lax.all_to_all(total, 'expert', split_axis=0, concat_axis=0, tiled=True,...  15.1 us
    ppermute x6, waiting for transfers between devices, exchange(): return lax.ppermute(x, 'expert', [(i, i ^ offset) for i in range(devices)])  13.7 us
    ppermute x6, starting transfers between devices, exchange(): return lax.ppermute(x, 'expert', [(i, i ^ offset) for i in range(devices)])  7.72 us
    pallas_call x1, Pallas kernels, pack(): pl.pallas_call(functools.partial(pack_kernel, outers), in_specs=[pl.Block...  2.56 us
    pallas_call x1, Pallas kernels, unpack(): pl.pallas_call(unpack_kernel, in_specs=[pl.BlockSpec(memory_space=pltpu.V...  1.54 us
  transfers between devices with their start and end apart: 6, of which 6 were waited for; matrix products, arithmetic and copies ran while one was open for 0% of the time, Pallas kernels for 0%

profile of v3, /device:TPU:0, one launch (start us, length us, event | category | flops | bytes accessed | tf_op | source)
XLA Modules:
  0.0 58.7 jit_solution(18396665306596154491)
XLA Ops:
  0.0 0.0 copy-start
  0.0 2.6 %pack.1 = (bf16[4,4,5120]{2,1,0:T(4,128)(2,1)S(1)}, bf16[4,4,5120]{2,1,0:T(4,128)(2,1)S(1)}) custom-call(s32[1,128]{1,0:T(1,128)} %bitcast.3, bf16[128,5120]{1,0:T(8,128)(2,1)} %refs_1_.1, f32[1,5120]{1,0:T(1,128)} %bitcast.6, bf16[8,5120]{1,0:T(8,128)(2,1)} %bitcast.5, bf16[5120,2560]{1,0:T(8,128)(2,1)} %up_ref.1), custom_call_target="tpu_custom_call" | custom-call | tf_op jit(solution)/shard_map/pack/pallas_call | solution.py:105
  2.6 3.0 %collective-permute-start = (bf16[4,4,5120]{2,1,0:T(4,128)(2,1)S(1)}, bf16[4,4,5120]{2,1,0:T(4,128)(2,1)S(1)}, u32[]{:S(2)}, u32[]{:S(2)}) collective-permute-start(bf16[4,4,5120]{2,1,0:T(4,128)(2,1)S(1)} %get-tuple-element.13), channel_id=1, source_target_pairs={{0,2},{1,3},{2,0},{3,1},{4,6},{5,7},{6,4},{7,5},{8,10},{9,11},{10,... | collective-permute-start | bytes 491528 | tf_op jit(solution)/shard_map/ppermute | solution.py:379
  5.6 4.2 %collective-permute-done.refs_1_ = bf16[4,4,5120]{2,1,0:T(4,128)(2,1)S(1)} collective-permute-done((bf16[4,4,5120]{2,1,0:T(4,128)(2,1)S(1)}, bf16[4,4,5120]{2,1,0:T(4,128)(2,1)S(1)}, u32[]{:S(2)}, u32[]{:S(2)}) %collective-permute-start) | collective-permute-done | bytes 163872 | tf_op jit(solution)/shard_map/ppermute | solution.py:379
  9.8 1.9 %collective-permute-start.1 = (bf16[2,4,5120]{2,1,0:T(4,128)(2,1)S(1)}, bf16[2,4,5120]{2,1,0:T(4,128)(2,1)S(1)}, u32[]{:S(2)}, u32[]{:S(2)}) collective-permute-start(bf16[2,4,5120]{2,1,0:T(4,128)(2,1)S(1)} %get-tuple-element.14), channel_id=1, source_target_pairs={{0,4},{1,5},{2,6},{3,7},{4,0},{5,1},{6,2},{7,3},{8,12},{9,13},{10,... | collective-permute-start | bytes 245768 | tf_op jit(solution)/shard_map/ppermute | solution.py:379
  11.7 2.6 %collective-permute-start.2 = (bf16[2,4,5120]{2,1,0:T(4,128)(2,1)S(1)}, bf16[2,4,5120]{2,1,0:T(4,128)(2,1)S(1)}, u32[]{:S(2)}, u32[]{:S(2)}) collective-permute-start(bf16[2,4,5120]{2,1,0:T(4,128)(2,1)S(1)} %get-tuple-element.15), channel_id=1, source_target_pairs={{0,8},{1,9},{2,10},{3,11},{4,12},{5,13},{6,14},{7,15},{8,0},{9,1},... | collective-permute-start | bytes 245768 | tf_op jit(solution)/shard_map/ppermute | solution.py:379
  14.3 0.0 collective-permute-start.3
  14.3 0.9 %collective-permute-done.1.refs_2_ = bf16[2,4,5120]{2,1,0:T(4,128)(2,1)S(1)} collective-permute-done((bf16[2,4,5120]{2,1,0:T(4,128)(2,1)S(1)}, bf16[2,4,5120]{2,1,0:T(4,128)(2,1)S(1)}, u32[]{:S(2)}, u32[]{:S(2)}) %collective-permute-start.1) | collective-permute-done | bytes 81952 | tf_op jit(solution)/shard_map/ppermute | solution.py:379
  15.1 4.0 %collective-permute-done.2.refs_3_ = bf16[2,4,5120]{2,1,0:T(4,128)(2,1)S(1)} collective-permute-done((bf16[2,4,5120]{2,1,0:T(4,128)(2,1)S(1)}, bf16[2,4,5120]{2,1,0:T(4,128)(2,1)S(1)}, u32[]{:S(2)}, u32[]{:S(2)}) %collective-permute-start.2) | collective-permute-done | bytes 81952 | tf_op jit(solution)/shard_map/ppermute | solution.py:379
  19.1 1.5 %collective-permute-done.3.refs_4_ = bf16[2,4,5120]{2,1,0:T(4,128)(2,1)S(1)} collective-permute-done((bf16[2,4,5120]{2,1,0:T(4,128)(2,1)S(1)}, bf16[2,4,5120]{2,1,0:T(4,128)(2,1)S(1)}, u32[]{:S(2)}, u32[]{:S(2)}) %collective-permute-start.3) | collective-permute-done | bytes 81952 | tf_op jit(solution)/shard_map/ppermute | solution.py:379
  20.6 0.0 copy-start.1
  20.7 0.1 collective-permute-start.4
  20.7 1.6 %collective-permute-done.4.other_ref = bf16[8,4,5120]{2,1,0:T(4,128)(2,1)S(1)} collective-permute-done((bf16[8,4,5120]{2,1,0:T(4,128)(2,1)S(1)}, bf16[8,4,5120]{2,1,0:T(4,128)(2,1)S(1)}, u32[]{:S(2)}, u32[]{:S(2)}) %collective-permute-start.4) | collective-permute-done | bytes 327712 | tf_op jit(solution)/shard_map/ppermute | solution.py:379
  22.4 0.0 copy-done
  22.4 17.8 %ffn.1 = (bf16[8,4,5120]{2,1,0:T(4,128)(2,1)S(1)}, bf16[8,4,5120]{2,1,0:T(4,128)(2,1)S(1)}) custom-call(bf16[8,4,5120]{2,1,0:T(4,128)(2,1)S(1)} %gather.1.mine_ref, bf16[8,4,5120]{2,1,0:T(4,128)(2,1)S(1)} %collective-permute-done.4.other_ref, bf16[5120,2560]{1,0:T(8,128)(2,1)} %up_ref.1, bf16[2560,5120]{1,0:T(8,128)(2,1)} %down_ref.1, ...), custom_call_target="tpu_custom_call" | custom-call | flops 5033164800 | bytes 52428800 | tf_op jit(solution)/shard_map/ffn/pallas_call | solution.py:276
  40.2 0.2 collective-permute-start.5
  40.4 1.5 %collective-permute-done.5.b_ref = bf16[8,4,5120]{2,1,0:T(4,128)(2,1)S(1)} collective-permute-done((bf16[8,4,5120]{2,1,0:T(4,128)(2,1)S(1)}, bf16[8,4,5120]{2,1,0:T(4,128)(2,1)S(1)}, u32[]{:S(2)}, u32[]{:S(2)}) %collective-permute-start.5) | collective-permute-done | bytes 327712 | tf_op jit(solution)/shard_map/ppermute | solution.py:379
  41.9 0.1 add.1
  42.0 15.1 %all_to_all.5.blocks_ref = bf16[8,4,5120]{2,1,0:T(4,128)(2,1)S(1)} all-to-all(bf16[8,4,5120]{2,1,0:T(4,128)(2,1)S(1)} %add.1), channel_id=1, replica_groups={{0,2,4,6,8,10,12,14},{1,3,5,7,9,11,13,15},{16,18,20,22,24,26,28,30},{17..., dimensions={0} | all-to-all | bytes 655360 | tf_op jit(solution)/shard_map/all_to_all | solution.py:388
  57.1 0.0 copy-done.1
  57.2 1.5 %unpack.1 = bf16[128,5120]{1,0:T(8,128)(2,1)} custom-call(s32[1,128]{1,0:T(1,128)S(1)} %bitcast.4, bf16[8,4,5120]{2,1,0:T(4,128)(2,1)S(1)} %all_to_all.5.blocks_ref), custom_call_target="tpu_custom_call" | custom-call | tf_op jit(solution)/shard_map/unpack/pallas_call | solution.py:356
  (2 shorter events, 0.0 us)
Async XLA Ops:
  0.0 22.4 %copy-start = (bf16[5120,2560]{1,0:T(8,128)(2,1)S(1)}, bf16[5120,2560]{1,0:T(8,128)(2,1)}, u32[]{:S(2)}) copy-start(bf16[5120,2560]{1,0:T(8,128)(2,1)} %gate_ref.1) | copy-start | bytes 78643200
  2.6 7.2 %collective-permute-start = (bf16[4,4,5120]{2,1,0:T(4,128)(2,1)S(1)}, bf16[4,4,5120]{2,1,0:T(4,128)(2,1)S(1)}, u32[]{:S(2)}, u32[]{:S(2)}) collective-permute-start(bf16[4,4,5120]{2,1,0:T(4,128)(2,1)S(1)} %get-tuple-element.13), channel_id=1, source_target_pairs={{0,2},{1,3},{2,0},{3,1},{4,6},{5,7},{6,4},{7,5},{8,10},{9,11},{10,... | collective-permute-start | bytes 491528 | tf_op jit(solution)/shard_map/ppermute | solution.py:379
  9.8 5.3 %collective-permute-start.1 = (bf16[2,4,5120]{2,1,0:T(4,128)(2,1)S(1)}, bf16[2,4,5120]{2,1,0:T(4,128)(2,1)S(1)}, u32[]{:S(2)}, u32[]{:S(2)}) collective-permute-start(bf16[2,4,5120]{2,1,0:T(4,128)(2,1)S(1)} %get-tuple-element.14), channel_id=1, source_target_pairs={{0,4},{1,5},{2,6},{3,7},{4,0},{5,1},{6,2},{7,3},{8,12},{9,13},{10,... | collective-permute-start | bytes 245768 | tf_op jit(solution)/shard_map/ppermute | solution.py:379
  11.7 7.4 %collective-permute-start.2 = (bf16[2,4,5120]{2,1,0:T(4,128)(2,1)S(1)}, bf16[2,4,5120]{2,1,0:T(4,128)(2,1)S(1)}, u32[]{:S(2)}, u32[]{:S(2)}) collective-permute-start(bf16[2,4,5120]{2,1,0:T(4,128)(2,1)S(1)} %get-tuple-element.15), channel_id=1, source_target_pairs={{0,8},{1,9},{2,10},{3,11},{4,12},{5,13},{6,14},{7,15},{8,0},{9,1},... | collective-permute-start | bytes 245768 | tf_op jit(solution)/shard_map/ppermute | solution.py:379
  14.3 6.3 %collective-permute-start.3 = (bf16[2,4,5120]{2,1,0:T(4,128)(2,1)S(1)}, bf16[2,4,5120]{2,1,0:T(4,128)(2,1)S(1)}, u32[]{:S(2)}, u32[]{:S(2)}) collective-permute-start(bf16[2,4,5120]{2,1,0:T(4,128)(2,1)S(1)} %get-tuple-element.16), channel_id=1, source_target_pairs={{0,12},{1,13},{2,14},{3,15},{4,8},{5,9},{6,10},{7,11},{8,4},{9,5},... | collective-permute-start | bytes 245768 | tf_op jit(solution)/shard_map/ppermute | solution.py:379
  20.6 36.5 %copy-start.1 = (s32[128]{0:T(128)S(1)}, s32[128]{0:T(128)}, u32[]{:S(2)}) copy-start(s32[128]{0:T(128)} %param.8) | copy-start | bytes 1540
  20.7 1.7 %collective-permute-start.4 = (bf16[8,4,5120]{2,1,0:T(4,128)(2,1)S(1)}, bf16[8,4,5120]{2,1,0:T(4,128)(2,1)S(1)}, u32[]{:S(2)}, u32[]{:S(2)}) collective-permute-start(bf16[8,4,5120]{2,1,0:T(4,128)(2,1)S(1)} %gather.1.mine_ref), channel_id=1, source_target_pairs={{0,1},{1,0},{2,3},{3,2},{4,5},{5,4},{6,7},{7,6},{8,9},{9,8},{10,11... | collective-permute-start | bytes 983048 | tf_op jit(solution)/shard_map/ppermute | solution.py:379
  40.2 1.7 %collective-permute-start.5 = (bf16[8,4,5120]{2,1,0:T(4,128)(2,1)S(1)}, bf16[8,4,5120]{2,1,0:T(4,128)(2,1)S(1)}, u32[]{:S(2)}, u32[]{:S(2)}) collective-permute-start(bf16[8,4,5120]{2,1,0:T(4,128)(2,1)S(1)} %get-tuple-element.18), channel_id=1, source_target_pairs={{0,1},{1,0},{2,3},{3,2},{4,5},{5,4},{6,7},{7,6},{8,9},{9,8},{10,11... | collective-permute-start | bytes 983048 | tf_op jit(solution)/shard_map/ppermute | solution.py:379

commit v4 on v3

--- a/solution.py
+++ b/solution.py
@@ -14,9 +14,8 @@
 DEEP = 512
 
 
-def slot_layout(ids, experts):
+def token_rows(ids):
     tokens = ids.shape[1]
-    rows = experts.shape[0]
     expert = lax.broadcasted_iota(jnp.int32, (EXP_FL, tokens), 0)
     chosen = (jnp.broadcast_to(ids, (EXP_FL, tokens)) == expert).astype(jnp.float32)
     before = lax.broadcasted_iota(jnp.int32, (tokens, tokens), 0) < lax.broadcasted_iota(
@@ -28,7 +27,11 @@
         preferred_element_type=jnp.float32,
     )
     slot = jnp.sum(earlier * chosen, axis=0, keepdims=True).astype(jnp.int32)
-    target = jnp.where(ids < EXP_FL, ids * CAP + slot, -1)
+    return jnp.where(ids < EXP_FL, ids * CAP + slot, -1)
+
+
+def slot_layout(target, experts):
+    rows, tokens = experts.shape[0], target.shape[1]
     row = experts * CAP + lax.broadcasted_iota(jnp.int32, (rows, 1), 0) % CAP
     return (row == jnp.broadcast_to(target, (rows, tokens))).astype(jnp.float32).astype(jnp.bfloat16)
 
@@ -41,7 +44,7 @@
 def partner_chips(chips, index):
     outers, inners = grid_of(chips)
     here = lax.axis_index("expert") // 2
-    return here ^ ((index % outers) * inners + index // outers)
+    return here ^ (index % outers * inners + index // outers)
 
 
 def in_hbm(x):
@@ -67,21 +70,39 @@
         rows_ref[first + i * CAP : first + (i + 1) * CAP, :] = blocks_ref[i].astype(rows_ref.dtype)
 
 
+def store_blocks(values, singles, groups):
+    outers = len(singles)
+    for i in range(values.shape[0] // CAP):
+        block = values[i * CAP : (i + 1) * CAP].astype(jnp.bfloat16)
+        if i < outers:
+            singles[i][0] = block
+        else:
+            groups[i // outers - 1][i % outers] = block
+
+
+def blocks_shapes(chips, width):
+    outers, inners = grid_of(chips)
+    return [blocks_out((1, CAP, width))] * outers + [blocks_out((outers, CAP, width))] * (inners - 1)
+
+
 def pack_kernel(outers, *refs):
     ids_ref, tokens_ref, gain_ref, router_ref = refs[:4]
-    outs, (ids, tokens, gain, router, sems) = refs[5:-5], refs[-5:]
+    outs, target_ref = refs[5:-6], refs[-6]
+    ids, tokens, gain, router, sems = refs[-5:]
     pairs = ((ids_ref, ids), (tokens_ref, tokens), (gain_ref, gain), (router_ref, router))
     moves = [pltpu.make_async_copy(a, b, sems.at[i]) for i, (a, b) in enumerate(pairs)]
     for move in moves:
         move.start()
-    inners = len(outs)
+    inners = len(outs) - outers + 1
     chips = outers * inners
     rows = chips * CAP
     copies = chips // EXP_FL
     index = lax.broadcasted_iota(jnp.int32, (rows, 1), 0) // CAP
     experts = partner_chips(chips, index) // copies
     moves[0].wait()
-    layout = slot_layout(ids[...], experts)
+    target = token_rows(ids[...])
+    target_ref[...] = target
+    layout = slot_layout(target, experts)
     moves[1].wait()
     packed = jnp.dot(layout, tokens[...], preferred_element_type=jnp.float32)
     mean_square = jnp.mean(packed * packed, axis=-1, keepdims=True)
@@ -94,65 +115,72 @@
     own = lax.broadcasted_iota(jnp.int32, logits.shape, 1) == experts
     logit = jnp.sum(jnp.where(own, logits, 0.0), axis=-1, keepdims=True)
     routed = normed.astype(jnp.float32) * jax.nn.sigmoid(logit)
-    for i in range(chips):
-        outs[i // outers][i % outers] = routed[i * CAP : (i + 1) * CAP].astype(jnp.bfloat16)
+    store_blocks(routed, outs[:outers], outs[outers:])
 
 
 def pack(tokens, ids, gain, router_rows, weight, chips):
     width = tokens.shape[1]
     outers, inners = grid_of(chips)
     arrays = (ids, tokens, gain, router_rows)
-    return pl.pallas_call(
+    outs = pl.pallas_call(
         functools.partial(pack_kernel, outers),
         in_specs=[pl.BlockSpec(memory_space=pl.ANY)] * 5,
-        out_specs=[pl.BlockSpec(memory_space=pltpu.VMEM)] * inners,
-        out_shape=[blocks_out((outers, CAP, width))] * inners,
+        out_specs=[pl.BlockSpec(memory_space=pltpu.VMEM)] * (outers + inners),
+        out_shape=blocks_shapes(chips, width) + [pltpu.VMEM(ids.shape, jnp.int32)],
         scratch_shapes=[pltpu.VMEM(x.shape, x.dtype) for x in arrays]
         + [pltpu.SemaphoreType.DMA((4,))],
         compiler_params=pltpu.CompilerParams(vmem_limit_bytes=(12 if chips <= 8 else 40) * MIB),
         name="pack",
     )(*[in_hbm(x) for x in (*arrays, weight)])
-
-
-def regroup_kernel(first, groups, *refs):
+    return outs[:-1], outs[-1]
+
+
+def forward_kernel(groups, *refs):
     for i, out_ref in enumerate(refs[groups:]):
         for j in range(groups):
-            out_ref[j] = refs[j][first + i]
-
-
-def regroup(arrays, first):
-    count, _, width = arrays[0].shape
+            out_ref[j] = refs[j][i + 1]
+
+
+def forward(arrays):
+    outers, _, width = arrays[0].shape
     vmem = pl.BlockSpec(memory_space=pltpu.VMEM)
     return pl.pallas_call(
-        functools.partial(regroup_kernel, first, len(arrays)),
+        functools.partial(forward_kernel, len(arrays)),
         in_specs=[vmem] * len(arrays),
-        out_specs=[vmem] * (count - first),
-        out_shape=[blocks_out((len(arrays), CAP, width))] * (count - first),
-        compiler_params=pltpu.CompilerParams(vmem_limit_bytes=(4 if count <= 8 else 24) * MIB),
-        name="regroup",
+        out_specs=[vmem] * (outers - 1),
+        out_shape=[blocks_out((len(arrays), CAP, width))] * (outers - 1),
+        compiler_params=pltpu.CompilerParams(vmem_limit_bytes=(4 if outers <= 4 else 24) * MIB),
+        name="forward",
     )(*[blocks_in_vmem(x) for x in arrays])
 
 
-def gather_kernel(kept, *refs):
-    out_ref = refs[-1]
-    for i in range(kept):
-        out_ref[i] = refs[i][0]
-    for i, ref in enumerate(refs[kept:-1]):
-        out_ref[(i + 1) * kept : (i + 2) * kept] = ref[...]
-
-
-def gather(kept, arrived):
-    arrays = (*kept, *arrived)
-    _, _, width = kept[0].shape
-    chips = len(kept) * (len(arrived) + 1)
+def piece_blocks(outers, inners, refs):
+    singles, groups, forwarded = refs[:outers], refs[outers : outers + inners - 1], refs[outers + inners - 1 :]
+    for i in range(outers):
+        yield i, singles[i][0]
+    for i in range(1, inners):
+        yield i * outers, groups[i - 1][0]
+        for j in range(1, outers):
+            yield i * outers + j, forwarded[j - 1][i - 1]
+
+
+def gather_kernel(outers, inners, *refs):
+    for i, block in piece_blocks(outers, inners, refs[:-1]):
+        refs[-1][i] = block
+
+
+def gather(pieces, chips):
+    outers, inners = grid_of(chips)
+    width = pieces[0].shape[2]
+    vmem = pl.BlockSpec(memory_space=pltpu.VMEM)
     return pl.pallas_call(
-        functools.partial(gather_kernel, len(kept)),
-        in_specs=[pl.BlockSpec(memory_space=pltpu.VMEM)] * len(arrays),
-        out_specs=pl.BlockSpec(memory_space=pltpu.VMEM),
+        functools.partial(gather_kernel, outers, inners),
+        in_specs=[vmem] * len(pieces),
+        out_specs=vmem,
         out_shape=blocks_out((chips, CAP, width)),
         compiler_params=pltpu.CompilerParams(vmem_limit_bytes=(4 if chips <= 8 else 24) * MIB),
         name="gather",
-    )(*[blocks_in_vmem(x) for x in arrays])
+    )(*[blocks_in_vmem(x) for x in pieces])
 
 
 def ffn_kernel(
@@ -305,9 +333,8 @@
 
 def add_kernel(a_ref, b_ref, out_ref):
     chips = a_ref.shape[0]
-    outers, inners = grid_of(chips)
     for i in range(chips):
-        chip = partner_chips(chips, (i % inners) * outers + i // inners)
+        chip = partner_chips(chips, i)
         out_ref[chip] = (a_ref[i].astype(jnp.float32) + b_ref[i].astype(jnp.float32)).astype(
             jnp.bfloat16
         )
@@ -324,9 +351,9 @@
     )(blocks_in_vmem(a), blocks_in_vmem(b))
 
 
-def unpack_kernel(ids_ref, blocks_ref, out_ref, rows, out, sems):
+def unpack_kernel(target_ref, blocks_ref, out_ref, rows, out, sems):
     experts = lax.broadcasted_iota(jnp.int32, (rows.shape[0], 1), 0) // CAP
-    layout = slot_layout(ids_ref[...], experts)
+    layout = slot_layout(target_ref[...], experts)
     copies = blocks_ref.shape[0] // EXP_FL
     for expert in range(EXP_FL):
         block = blocks_ref[expert * copies].astype(jnp.float32)
@@ -350,9 +377,9 @@
         move.wait()
 
 
-def unpack(blocks, ids):
+def unpack(blocks, target):
     chips, _, width = blocks.shape
-    shape = (ids.shape[1], width)
+    shape = (target.shape[1], width)
     return pl.pallas_call(
         unpack_kernel,
         in_specs=[pl.BlockSpec(memory_space=pltpu.VMEM)] * 2,
@@ -365,7 +392,7 @@
         ],
         compiler_params=pltpu.CompilerParams(vmem_limit_bytes=16 * MIB),
         name="unpack",
-    )(ids, blocks_in_vmem(blocks))
+    )(in_vmem(target), blocks_in_vmem(blocks))
 
 
 def per_device(tokens, expert_ids, norm_gain, router, gate_weight, up_weight, down_weight):
@@ -378,17 +405,19 @@
     def exchange(x, offset):
         return lax.ppermute(x, "expert", [(i, i ^ offset) for i in range(devices)])
 
-    packed = pack(tokens, ids, norm_gain.reshape(1, -1), router.T, up_weight, chips)
-    near = [packed[0], *[exchange(packed[i], 2 * i) for i in range(1, inners)]]
-    leaving = regroup(near, 1)
-    far = [exchange(leaving[i - 1], 2 * inners * i) for i in range(1, outers)]
-    mine = gather(near, far)
+    blocks, target = pack(tokens, ids, norm_gain.reshape(1, -1), router.T, up_weight, chips)
+    singles, groups = blocks[:outers], blocks[outers:]
+    steps = [2 * inners * i for i in range(1, outers)]
+    near = [exchange(x, 2 * (i + 1)) for i, x in enumerate(groups)]
+    direct = [exchange(x, step) for x, step in zip(singles[1:], steps)]
+    onward = [exchange(x, step) for x, step in zip(forward(near), steps)]
+    mine = gather([singles[0], *direct, *near, *onward], chips)
     own, lent = ffn(mine, exchange(mine, 1), gate_weight, up_weight, down_weight)
     total = add(own, exchange(lent, 1))
     returned = lax.all_to_all(
         total, "expert", split_axis=0, concat_axis=0, tiled=True, axis_index_groups=same_core
     )
-    return unpack(returned, ids)
+    return unpack(returned, target)
 
 
 def solution(mesh):

time: 58.9 us -> 56.9 us (0.966)
  waiting for transfers between devices: 13.7 us -> 8.75 us
  starting transfers between devices: 7.72 us -> 12.1 us
  blocking collectives: 15.1 us -> 13.9 us
    ppermute x6 -> x9, waiting for transfers between devices: 13.7 us -> 8.75 us  [exchange(): return lax.ppermute(x, 'expert', [(i, i ^ offset) for i in range(devices)])]
    ppermute x6 -> x9, starting transfers between devices: 7.72 us -> 12.1 us  [exchange(): return lax.ppermute(x, 'expert', [(i, i ^ offset) for i in range(devices)])]
    all_to_all x1, blocking collectives: 15.1 us -> 13.9 us  [per_device(): lax.all_to_all(total, 'expert', split_axis=0, concat_axis=0, tiled=True,...]
  transfers between devices with their start and end apart: 6 -> 9, of which waited for: 6 -> 5; matrix products, arithmetic and copies ran while one was open for 0% -> 0% of each run, Pallas kernels for 0% -> 0%
where the time goes in v4:
time: 56.9 us; the launch traced here: 56.7 us
  Pallas kernels  22 us (39%)
  blocking collectives  13.9 us (24%)
  starting transfers between devices  12.1 us (21%)
  waiting for transfers between devices  8.75 us (15%)
    pallas_call x1, Pallas kernels, ffn(): pl.pallas_call(functools.partial(ffn_kernel, deep, wide), in_specs=[vmem]...  17.8 us
    all_to_all x1, blocking collectives, per_device(): lax.all_to_all(total, 'expert', split_axis=0, concat_axis=0, tiled=True,...  13.9 us
    ppermute x9, starting transfers between devices, exchange(): return lax.ppermute(x, 'expert', [(i, i ^ offset) for i in range(devices)])  12.1 us
    ppermute x9, waiting for transfers between devices, exchange(): return lax.ppermute(x, 'expert', [(i, i ^ offset) for i in range(devices)])  8.75 us
    pallas_call x1, Pallas kernels, pack(): pl.pallas_call(functools.partial(pack_kernel, outers), in_specs=[pl.Block...  2.56 us
    pallas_call x1, Pallas kernels, unpack(): pl.pallas_call(unpack_kernel, in_specs=[pl.BlockSpec(memory_space=pltpu.V...  1.39 us
  transfers between devices with their start and end apart: 9, of which 5 were waited for; matrix products, arithmetic and copies ran while one was open for 0% of the time, Pallas kernels for 0%

profile of v4, /device:TPU:0, one launch (start us, length us, event | category | flops | bytes accessed | tf_op | source)
XLA Modules:
  0.0 56.7 jit_solution(1910478075594900627)
XLA Ops:
  0.0 2.6 %pack.1 = (bf16[1,4,5120]{2,1,0:T(4,128)(2,1)S(1)}, bf16[1,4,5120]{2,1,0:T(4,128)(2,1)S(1)}, bf16[1,4,5120]{2,1,0:T(4,128)(2,1)S(1)}, bf16[1,4,5120]{2,1,0:T(4,1...) custom-call(s32[1,128]{1,0:T(1,128)} %bitcast.5, bf16[128,5120]{1,0:T(8,128)(2,1)} %refs_1_.1, ...), custom_call_target="tpu_custom_call" | custom-call | tf_op jit(solution)/shard_map/pack/pallas_call | solution.py:125
  2.6 3.0 %collective-permute-start.3 = (bf16[4,4,5120]{2,1,0:T(4,128)(2,1)S(1)}, bf16[4,4,5120]{2,1,0:T(4,128)(2,1)S(1)}, u32[]{:S(2)}, u32[]{:S(2)}) collective-permute-start(bf16[4,4,5120]{2,1,0:T(4,128)(2,1)S(1)} %get-tuple-element.21), channel_id=1, source_target_pairs={{0,2},{1,3},{2,0},{3,1},{4,6},{5,7},{6,4},{7,5},{8,10},{9,11},{10,... | collective-permute-start | bytes 491528 | tf_op jit(solution)/shard_map/ppermute | solution.py:406
  5.6 1.6 %collective-permute-start = (bf16[1,4,5120]{2,1,0:T(4,128)(2,1)S(1)}, bf16[1,4,5120]{2,1,0:T(4,128)(2,1)S(1)}, u32[]{:S(2)}, u32[]{:S(2)}) collective-permute-start(bf16[1,4,5120]{2,1,0:T(4,128)(2,1)S(1)} %get-tuple-element.18), channel_id=1, source_target_pairs={{0,4},{1,5},{2,6},{3,7},{4,0},{5,1},{6,2},{7,3},{8,12},{9,13},{10,... | collective-permute-start | bytes 122888 | tf_op jit(solution)/shard_map/ppermute | solution.py:406
  7.2 2.6 %collective-permute-start.1 = (bf16[1,4,5120]{2,1,0:T(4,128)(2,1)S(1)}, bf16[1,4,5120]{2,1,0:T(4,128)(2,1)S(1)}, u32[]{:S(2)}, u32[]{:S(2)}) collective-permute-start(bf16[1,4,5120]{2,1,0:T(4,128)(2,1)S(1)} %get-tuple-element.19), channel_id=1, source_target_pairs={{0,8},{1,9},{2,10},{3,11},{4,12},{5,13},{6,14},{7,15},{8,0},{9,1},... | collective-permute-start | bytes 122888 | tf_op jit(solution)/shard_map/ppermute | solution.py:406
  9.8 0.2 collective-permute-start.2
  10.0 0.0 collective-permute-done.3.refs_0_.refs_4_
  10.0 1.7 %collective-permute-start.4 = (bf16[1,4,5120]{2,1,0:T(4,128)(2,1)S(1)}, bf16[1,4,5120]{2,1,0:T(4,128)(2,1)S(1)}, u32[]{:S(2)}, u32[]{:S(2)}) collective-permute-start(bf16[1,4,5120]{2,1,0:T(4,128)(2,1)S(1)} %get-tuple-element.22), channel_id=1, source_target_pairs={{0,4},{1,5},{2,6},{3,7},{4,0},{5,1},{6,2},{7,3},{8,12},{9,13},{10,... | collective-permute-start | bytes 122888 | tf_op jit(solution)/shard_map/ppermute | solution.py:406
  11.7 2.6 %collective-permute-start.5 = (bf16[1,4,5120]{2,1,0:T(4,128)(2,1)S(1)}, bf16[1,4,5120]{2,1,0:T(4,128)(2,1)S(1)}, u32[]{:S(2)}, u32[]{:S(2)}) collective-permute-start(bf16[1,4,5120]{2,1,0:T(4,128)(2,1)S(1)} %get-tuple-element.23), channel_id=1, source_target_pairs={{0,8},{1,9},{2,10},{3,11},{4,12},{5,13},{6,14},{7,15},{8,0},{9,1},... | collective-permute-start | bytes 122888 | tf_op jit(solution)/shard_map/ppermute | solution.py:406
  14.3 0.0 collective-permute-done.refs_1_
  14.3 0.2 collective-permute-start.6
  14.5 0.0 collective-permute-done.1.refs_2_
  14.5 1.1 %collective-permute-done.2.refs_3_ = bf16[1,4,5120]{2,1,0:T(4,128)(2,1)S(1)} collective-permute-done((bf16[1,4,5120]{2,1,0:T(4,128)(2,1)S(1)}, bf16[1,4,5120]{2,1,0:T(4,128)(2,1)S(1)}, u32[]{:S(2)}, u32[]{:S(2)}) %collective-permute-start.2) | collective-permute-done | bytes 40992 | tf_op jit(solution)/shard_map/ppermute | solution.py:406
  15.6 0.0 collective-permute-done.4.refs_5_
  15.6 1.4 %collective-permute-done.5.refs_6_ = bf16[1,4,5120]{2,1,0:T(4,128)(2,1)S(1)} collective-permute-done((bf16[1,4,5120]{2,1,0:T(4,128)(2,1)S(1)}, bf16[1,4,5120]{2,1,0:T(4,128)(2,1)S(1)}, u32[]{:S(2)}, u32[]{:S(2)}) %collective-permute-start.5) | collective-permute-done | bytes 40992 | tf_op jit(solution)/shard_map/ppermute | solution.py:406
  17.0 3.1 %collective-permute-done.6.refs_7_ = bf16[1,4,5120]{2,1,0:T(4,128)(2,1)S(1)} collective-permute-done((bf16[1,4,5120]{2,1,0:T(4,128)(2,1)S(1)}, bf16[1,4,5120]{2,1,0:T(4,128)(2,1)S(1)}, u32[]{:S(2)}, u32[]{:S(2)}) %collective-permute-start.6) | collective-permute-done | bytes 40992 | tf_op jit(solution)/shard_map/ppermute | solution.py:406
  20.1 0.1 collective-permute-start.7
  20.2 1.6 %collective-permute-done.7.other_ref = bf16[8,4,5120]{2,1,0:T(4,128)(2,1)S(1)} collective-permute-done((bf16[8,4,5120]{2,1,0:T(4,128)(2,1)S(1)}, bf16[8,4,5120]{2,1,0:T(4,128)(2,1)S(1)}, u32[]{:S(2)}, u32[]{:S(2)}) %collective-permute-start.7) | collective-permute-done | bytes 327712 | tf_op jit(solution)/shard_map/ppermute | solution.py:406
  21.8 0.0 copy-done
  21.8 17.8 %ffn.1 = (bf16[8,4,5120]{2,1,0:T(4,128)(2,1)S(1)}, bf16[8,4,5120]{2,1,0:T(4,128)(2,1)S(1)}) custom-call(bf16[8,4,5120]{2,1,0:T(4,128)(2,1)S(1)} %gather.1.mine_ref, bf16[8,4,5120]{2,1,0:T(4,128)(2,1)S(1)} %collective-permute-done.7.other_ref, bf16[5120,2560]{1,0:T(8,128)(2,1)} %up_ref.1, bf16[2560,5120]{1,0:T(8,128)(2,1)} %down_ref.1, ...), custom_call_target="tpu_custom_call" | custom-call | flops 5033164800 | bytes 52428800 | tf_op jit(solution)/shard_map/ffn/pallas_call | solution.py:304
  39.6 0.2 collective-permute-start.8
  39.8 1.5 %collective-permute-done.8.b_ref = bf16[8,4,5120]{2,1,0:T(4,128)(2,1)S(1)} collective-permute-done((bf16[8,4,5120]{2,1,0:T(4,128)(2,1)S(1)}, bf16[8,4,5120]{2,1,0:T(4,128)(2,1)S(1)}, u32[]{:S(2)}, u32[]{:S(2)}) %collective-permute-start.8) | collective-permute-done | bytes 327712 | tf_op jit(solution)/shard_map/ppermute | solution.py:406
  41.3 0.1 add.1
  41.5 13.9 %all_to_all.5.blocks_ref = bf16[8,4,5120]{2,1,0:T(4,128)(2,1)S(1)} all-to-all(bf16[8,4,5120]{2,1,0:T(4,128)(2,1)S(1)} %add.1), channel_id=1, replica_groups={{0,2,4,6,8,10,12,14},{1,3,5,7,9,11,13,15},{16,18,20,22,24,26,28,30},{17..., dimensions={0} | all-to-all | bytes 655360 | tf_op jit(solution)/shard_map/all_to_all | solution.py:417
  55.4 1.4 %unpack.1 = bf16[128,5120]{1,0:T(8,128)(2,1)} custom-call(s32[1,128]{1,0:T(1,128)S(1)} %get-tuple-element.16.target_ref, bf16[8,4,5120]{2,1,0:T(4,128)(2,1)S(1)} %all_to_all.5.blocks_ref), custom_call_target="tpu_custom_call" | custom-call | tf_op jit(solution)/shard_map/unpack/pallas_call | solution.py:383
  (3 shorter events, 0.0 us)
Async XLA Ops:
  0.0 21.8 %copy-start = (bf16[5120,2560]{1,0:T(8,128)(2,1)S(1)}, bf16[5120,2560]{1,0:T(8,128)(2,1)}, u32[]{:S(2)}) copy-start(bf16[5120,2560]{1,0:T(8,128)(2,1)} %gate_ref.1) | copy-start | bytes 78643200
  2.6 7.4 %collective-permute-start.3 = (bf16[4,4,5120]{2,1,0:T(4,128)(2,1)S(1)}, bf16[4,4,5120]{2,1,0:T(4,128)(2,1)S(1)}, u32[]{:S(2)}, u32[]{:S(2)}) collective-permute-start(bf16[4,4,5120]{2,1,0:T(4,128)(2,1)S(1)} %get-tuple-element.21), channel_id=1, source_target_pairs={{0,2},{1,3},{2,0},{3,1},{4,6},{5,7},{6,4},{7,5},{8,10},{9,11},{10,... | collective-permute-start | bytes 491528 | tf_op jit(solution)/shard_map/ppermute | solution.py:406
  5.6 8.7 %collective-permute-start = (bf16[1,4,5120]{2,1,0:T(4,128)(2,1)S(1)}, bf16[1,4,5120]{2,1,0:T(4,128)(2,1)S(1)}, u32[]{:S(2)}, u32[]{:S(2)}) collective-permute-start(bf16[1,4,5120]{2,1,0:T(4,128)(2,1)S(1)} %get-tuple-element.18), channel_id=1, source_target_pairs={{0,4},{1,5},{2,6},{3,7},{4,0},{5,1},{6,2},{7,3},{8,12},{9,13},{10,... | collective-permute-start | bytes 122888 | tf_op jit(solution)/shard_map/ppermute | solution.py:406
  7.2 7.3 %collective-permute-start.1 = (bf16[1,4,5120]{2,1,0:T(4,128)(2,1)S(1)}, bf16[1,4,5120]{2,1,0:T(4,128)(2,1)S(1)}, u32[]{:S(2)}, u32[]{:S(2)}) collective-permute-start(bf16[1,4,5120]{2,1,0:T(4,128)(2,1)S(1)} %get-tuple-element.19), channel_id=1, source_target_pairs={{0,8},{1,9},{2,10},{3,11},{4,12},{5,13},{6,14},{7,15},{8,0},{9,1},... | collective-permute-start | bytes 122888 | tf_op jit(solution)/shard_map/ppermute | solution.py:406
  9.8 5.8 %collective-permute-start.2 = (bf16[1,4,5120]{2,1,0:T(4,128)(2,1)S(1)}, bf16[1,4,5120]{2,1,0:T(4,128)(2,1)S(1)}, u32[]{:S(2)}, u32[]{:S(2)}) collective-permute-start(bf16[1,4,5120]{2,1,0:T(4,128)(2,1)S(1)} %get-tuple-element.20), channel_id=1, source_target_pairs={{0,12},{1,13},{2,14},{3,15},{4,8},{5,9},{6,10},{7,11},{8,4},{9,5},... | collective-permute-start | bytes 122888 | tf_op jit(solution)/shard_map/ppermute | solution.py:406
  10.0 5.6 %collective-permute-start.4 = (bf16[1,4,5120]{2,1,0:T(4,128)(2,1)S(1)}, bf16[1,4,5120]{2,1,0:T(4,128)(2,1)S(1)}, u32[]{:S(2)}, u32[]{:S(2)}) collective-permute-start(bf16[1,4,5120]{2,1,0:T(4,128)(2,1)S(1)} %get-tuple-element.22), channel_id=1, source_target_pairs={{0,4},{1,5},{2,6},{3,7},{4,0},{5,1},{6,2},{7,3},{8,12},{9,13},{10,... | collective-permute-start | bytes 122888 | tf_op jit(solution)/shard_map/ppermute | solution.py:406
  11.7 5.3 %collective-permute-start.5 = (bf16[1,4,5120]{2,1,0:T(4,128)(2,1)S(1)}, bf16[1,4,5120]{2,1,0:T(4,128)(2,1)S(1)}, u32[]{:S(2)}, u32[]{:S(2)}) collective-permute-start(bf16[1,4,5120]{2,1,0:T(4,128)(2,1)S(1)} %get-tuple-element.23), channel_id=1, source_target_pairs={{0,8},{1,9},{2,10},{3,11},{4,12},{5,13},{6,14},{7,15},{8,0},{9,1},... | collective-permute-start | bytes 122888 | tf_op jit(solution)/shard_map/ppermute | solution.py:406
  14.3 5.8 %collective-permute-start.6 = (bf16[1,4,5120]{2,1,0:T(4,128)(2,1)S(1)}, bf16[1,4,5120]{2,1,0:T(4,128)(2,1)S(1)}, u32[]{:S(2)}, u32[]{:S(2)}) collective-permute-start(bf16[1,4,5120]{2,1,0:T(4,128)(2,1)S(1)} %get-tuple-element.24), channel_id=1, source_target_pairs={{0,12},{1,13},{2,14},{3,15},{4,8},{5,9},{6,10},{7,11},{8,4},{9,5},... | collective-permute-start | bytes 122888 | tf_op jit(solution)/shard_map/ppermute | solution.py:406
  20.1 1.7 %collective-permute-start.7 = (bf16[8,4,5120]{2,1,0:T(4,128)(2,1)S(1)}, bf16[8,4,5120]{2,1,0:T(4,128)(2,1)S(1)}, u32[]{:S(2)}, u32[]{:S(2)}) collective-permute-start(bf16[8,4,5120]{2,1,0:T(4,128)(2,1)S(1)} %gather.1.mine_ref), channel_id=1, source_target_pairs={{0,1},{1,0},{2,3},{3,2},{4,5},{5,4},{6,7},{7,6},{8,9},{9,8},{10,11... | collective-permute-start | bytes 983048 | tf_op jit(solution)/shard_map/ppermute | solution.py:406
  39.6 1.7 %collective-permute-start.8 = (bf16[8,4,5120]{2,1,0:T(4,128)(2,1)S(1)}, bf16[8,4,5120]{2,1,0:T(4,128)(2,1)S(1)}, u32[]{:S(2)}, u32[]{:S(2)}) collective-permute-start(bf16[8,4,5120]{2,1,0:T(4,128)(2,1)S(1)} %get-tuple-element.26), channel_id=1, source_target_pairs={{0,1},{1,0},{2,3},{3,2},{4,5},{5,4},{6,7},{7,6},{8,9},{9,8},{10,11... | collective-permute-start | bytes 983048 | tf_op jit(solution)/shard_map/ppermute | solution.py:406

commit v5 on v4

--- a/solution.py
+++ b/solution.py
@@ -331,35 +331,37 @@
     )
 
 
-def add_kernel(a_ref, b_ref, out_ref):
+def add_kernel(outers, a_ref, b_ref, *outs):
     chips = a_ref.shape[0]
     for i in range(chips):
-        chip = partner_chips(chips, i)
-        out_ref[chip] = (a_ref[i].astype(jnp.float32) + b_ref[i].astype(jnp.float32)).astype(
-            jnp.bfloat16
-        )
+        block = (a_ref[i].astype(jnp.float32) + b_ref[i].astype(jnp.float32)).astype(jnp.bfloat16)
+        if i < outers:
+            outs[i][0] = block
+        else:
+            outs[outers + i // outers - 1][i % outers] = block
 
 
 def add(a, b):
+    chips, _, width = a.shape
+    outers, inners = grid_of(chips)
+    vmem = pl.BlockSpec(memory_space=pltpu.VMEM)
     return pl.pallas_call(
-        add_kernel,
-        in_specs=[pl.BlockSpec(memory_space=pltpu.VMEM)] * 2,
-        out_specs=pl.BlockSpec(memory_space=pltpu.VMEM),
-        out_shape=blocks_out(a.shape),
+        functools.partial(add_kernel, outers),
+        in_specs=[vmem] * 2,
+        out_specs=[vmem] * (outers + inners - 1),
+        out_shape=blocks_shapes(chips, width),
         compiler_params=pltpu.CompilerParams(vmem_limit_bytes=16 * MIB),
         name="add",
     )(blocks_in_vmem(a), blocks_in_vmem(b))
 
 
-def unpack_kernel(target_ref, blocks_ref, out_ref, rows, out, sems):
-    experts = lax.broadcasted_iota(jnp.int32, (rows.shape[0], 1), 0) // CAP
-    layout = slot_layout(target_ref[...], experts)
-    copies = blocks_ref.shape[0] // EXP_FL
-    for expert in range(EXP_FL):
-        block = blocks_ref[expert * copies].astype(jnp.float32)
-        for i in range(1, copies):
-            block += blocks_ref[expert * copies + i].astype(jnp.float32)
-        rows[expert * CAP : (expert + 1) * CAP, :] = block
+def unpack_kernel(outers, inners, target_ref, *refs):
+    pieces, (out_ref, rows, out, sems) = refs[:-4], refs[-4:]
+    chips = outers * inners
+    index = lax.broadcasted_iota(jnp.int32, (rows.shape[0], 1), 0) // CAP
+    layout = slot_layout(target_ref[...], partner_chips(chips, index) // (chips // EXP_FL))
+    for i, block in piece_blocks(outers, inners, pieces):
+        rows[i * CAP : (i + 1) * CAP, :] = block.astype(jnp.float32)
     count = sems.shape[0]
     part = rows.shape[1] // count
     moves = []
@@ -377,47 +379,45 @@
         move.wait()
 
 
-def unpack(blocks, target):
-    chips, _, width = blocks.shape
+def unpack(pieces, target, chips):
+    width = pieces[0].shape[2]
     shape = (target.shape[1], width)
     return pl.pallas_call(
-        unpack_kernel,
-        in_specs=[pl.BlockSpec(memory_space=pltpu.VMEM)] * 2,
+        functools.partial(unpack_kernel, *grid_of(chips)),
+        in_specs=[pl.BlockSpec(memory_space=pltpu.VMEM)] * (1 + len(pieces)),
         out_specs=pl.BlockSpec(memory_space=pl.ANY),
         out_shape=jax.ShapeDtypeStruct(shape, jnp.bfloat16),
         scratch_shapes=[
-            pltpu.VMEM((EXP_FL * CAP, width), jnp.float32),
+            pltpu.VMEM((chips * CAP, width), jnp.float32),
             pltpu.VMEM(shape, jnp.bfloat16),
             pltpu.SemaphoreType.DMA((4,)),
         ],
-        compiler_params=pltpu.CompilerParams(vmem_limit_bytes=16 * MIB),
+        compiler_params=pltpu.CompilerParams(vmem_limit_bytes=(16 if chips <= 8 else 32) * MIB),
         name="unpack",
-    )(in_vmem(target), blocks_in_vmem(blocks))
+    )(in_vmem(target), *[blocks_in_vmem(x) for x in pieces])
 
 
 def per_device(tokens, expert_ids, norm_gain, router, gate_weight, up_weight, down_weight):
     devices = lax.axis_size("expert")
     chips = devices // 2
     outers, inners = grid_of(chips)
-    same_core = [list(range(core, devices, 2)) for core in range(2)]
     ids = expert_ids.reshape(1, -1)
-
-    def exchange(x, offset):
+    steps = [2 * inners * i for i in range(1, outers)]
+
+    def send(x, offset):
         return lax.ppermute(x, "expert", [(i, i ^ offset) for i in range(devices)])
 
+    def exchange(blocks):
+        singles, groups = blocks[:outers], blocks[outers:]
+        near = [send(x, 2 * (i + 1)) for i, x in enumerate(groups)]
+        direct = [send(x, step) for x, step in zip(singles[1:], steps)]
+        onward = [send(x, step) for x, step in zip(forward(near), steps)]
+        return [singles[0], *direct, *near, *onward]
+
     blocks, target = pack(tokens, ids, norm_gain.reshape(1, -1), router.T, up_weight, chips)
-    singles, groups = blocks[:outers], blocks[outers:]
-    steps = [2 * inners * i for i in range(1, outers)]
-    near = [exchange(x, 2 * (i + 1)) for i, x in enumerate(groups)]
-    direct = [exchange(x, step) for x, step in zip(singles[1:], steps)]
-    onward = [exchange(x, step) for x, step in zip(forward(near), steps)]
-    mine = gather([singles[0], *direct, *near, *onward], chips)
-    own, lent = ffn(mine, exchange(mine, 1), gate_weight, up_weight, down_weight)
-    total = add(own, exchange(lent, 1))
-    returned = lax.all_to_all(
-        total, "expert", split_axis=0, concat_axis=0, tiled=True, axis_index_groups=same_core
-    )
-    return unpack(returned, target)
+    mine = gather(exchange(blocks), chips)
+    own, lent = ffn(mine, send(mine, 1), gate_weight, up_weight, down_weight)
+    return unpack(exchange(add(own, send(lent, 1))), target, chips)
 
 
 def solution(mesh):

time: 56.9 us -> 56.2 us (0.988)
  blocking collectives: 13.9 us -> 0 us
  starting transfers between devices: 12.1 us -> 22.5 us
  waiting for transfers between devices: 8.75 us -> 11.5 us
    all_to_all x1 -> x0, blocking collectives: 13.9 us -> none  [per_device(): lax.all_to_all(total, 'expert', split_axis=0, concat_axis=0, tiled=True,...]
    ppermute x9 -> x16, starting transfers between devices: 12.1 us -> 22.5 us  [send(): return lax.ppermute(x, 'expert', [(i, i ^ offset) for i in range(devices)])]
    ppermute x9 -> x16, waiting for transfers between devices: 8.75 us -> 11.5 us  [send(): return lax.ppermute(x, 'expert', [(i, i ^ offset) for i in range(devices)])]
  transfers between devices with their start and end apart: 9 -> 16, of which waited for: 5 -> 8; matrix products, arithmetic and copies ran while one was open for 0% -> 0% of each run, Pallas kernels for 0% -> 0%
where the time goes in v5:
time: 56.2 us; the launch traced here: 56.1 us
  starting transfers between devices  22.5 us (40%)
  Pallas kernels  22 us (39%)
  waiting for transfers between devices  11.5 us (20%)
    ppermute x16, starting transfers between devices, send(): return lax.ppermute(x, 'expert', [(i, i ^ offset) for i in range(devices)])  22.5 us
    pallas_call x1, Pallas kernels, ffn(): pl.pallas_call(functools.partial(ffn_kernel, deep, wide), in_specs=[vmem]...  17.8 us
    ppermute x16, waiting for transfers between devices, send(): return lax.ppermute(x, 'expert', [(i, i ^ offset) for i in range(devices)])  11.5 us
    pallas_call x1, Pallas kernels, pack(): pl.pallas_call(functools.partial(pack_kernel, outers), in_specs=[pl.Block...  2.56 us
    pallas_call x1, Pallas kernels, unpack(): pl.pallas_call(functools.partial(unpack_kernel, *grid_of(chips)), in_spec...  1.4 us
  transfers between devices with their start and end apart: 16, of which 8 were waited for; matrix products, arithmetic and copies ran while one was open for 0% of the time, Pallas kernels for 0%

profile of v5, /device:TPU:0, one launch (start us, length us, event | category | flops | bytes accessed | tf_op | source)
XLA Modules:
  0.0 56.1 jit_solution(8911736435474155860)
XLA Ops:
  0.0 2.6 %pack.1 = (bf16[1,4,5120]{2,1,0:T(4,128)(2,1)S(1)}, bf16[1,4,5120]{2,1,0:T(4,128)(2,1)S(1)}, bf16[1,4,5120]{2,1,0:T(4,128)(2,1)S(1)}, bf16[1,4,5120]{2,1,0:T(4,1...) custom-call(s32[1,128]{1,0:T(1,128)} %bitcast.5, bf16[128,5120]{1,0:T(8,128)(2,1)} %refs_1_.1, ...), custom_call_target="tpu_custom_call" | custom-call | tf_op jit(solution)/shard_map/pack/pallas_call | solution.py:125
  2.6 3.0 %collective-permute-start.3 = (bf16[4,4,5120]{2,1,0:T(4,128)(2,1)S(1)}, bf16[4,4,5120]{2,1,0:T(4,128)(2,1)S(1)}, u32[]{:S(2)}, u32[]{:S(2)}) collective-permute-start(bf16[4,4,5120]{2,1,0:T(4,128)(2,1)S(1)} %get-tuple-element.29), channel_id=1, source_target_pairs={{0,2},{1,3},{2,0},{3,1},{4,6},{5,7},{6,4},{7,5},{8,10},{9,11},{10,... | collective-permute-start | bytes 491528 | tf_op jit(solution)/shard_map/ppermute | solution.py:408
  5.6 1.6 %collective-permute-start = (bf16[1,4,5120]{2,1,0:T(4,128)(2,1)S(1)}, bf16[1,4,5120]{2,1,0:T(4,128)(2,1)S(1)}, u32[]{:S(2)}, u32[]{:S(2)}) collective-permute-start(bf16[1,4,5120]{2,1,0:T(4,128)(2,1)S(1)} %get-tuple-element.26), channel_id=1, source_target_pairs={{0,4},{1,5},{2,6},{3,7},{4,0},{5,1},{6,2},{7,3},{8,12},{9,13},{10,... | collective-permute-start | bytes 122888 | tf_op jit(solution)/shard_map/ppermute | solution.py:408
  7.2 2.6 %collective-permute-start.1 = (bf16[1,4,5120]{2,1,0:T(4,128)(2,1)S(1)}, bf16[1,4,5120]{2,1,0:T(4,128)(2,1)S(1)}, u32[]{:S(2)}, u32[]{:S(2)}) collective-permute-start(bf16[1,4,5120]{2,1,0:T(4,128)(2,1)S(1)} %get-tuple-element.27), channel_id=1, source_target_pairs={{0,8},{1,9},{2,10},{3,11},{4,12},{5,13},{6,14},{7,15},{8,0},{9,1},... | collective-permute-start | bytes 122888 | tf_op jit(solution)/shard_map/ppermute | solution.py:408
  9.8 0.2 collective-permute-start.2
  10.0 1.7 %collective-permute-start.4 = (bf16[1,4,5120]{2,1,0:T(4,128)(2,1)S(1)}, bf16[1,4,5120]{2,1,0:T(4,128)(2,1)S(1)}, u32[]{:S(2)}, u32[]{:S(2)}) collective-permute-start(bf16[1,4,5120]{2,1,0:T(4,128)(2,1)S(1)} %get-tuple-element.30), channel_id=1, source_target_pairs={{0,4},{1,5},{2,6},{3,7},{4,0},{5,1},{6,2},{7,3},{8,12},{9,13},{10,... | collective-permute-start | bytes 122888 | tf_op jit(solution)/shard_map/ppermute | solution.py:408
  11.7 2.6 %collective-permute-start.5 = (bf16[1,4,5120]{2,1,0:T(4,128)(2,1)S(1)}, bf16[1,4,5120]{2,1,0:T(4,128)(2,1)S(1)}, u32[]{:S(2)}, u32[]{:S(2)}) collective-permute-start(bf16[1,4,5120]{2,1,0:T(4,128)(2,1)S(1)} %get-tuple-element.31), channel_id=1, source_target_pairs={{0,8},{1,9},{2,10},{3,11},{4,12},{5,13},{6,14},{7,15},{8,0},{9,1},... | collective-permute-start | bytes 122888 | tf_op jit(solution)/shard_map/ppermute | solution.py:408
  14.3 0.2 collective-permute-start.6
  14.5 1.1 %collective-permute-done.2.refs_3_ = bf16[1,4,5120]{2,1,0:T(4,128)(2,1)S(1)} collective-permute-done((bf16[1,4,5120]{2,1,0:T(4,128)(2,1)S(1)}, bf16[1,4,5120]{2,1,0:T(4,128)(2,1)S(1)}, u32[]{:S(2)}, u32[]{:S(2)}) %collective-permute-start.2) | collective-permute-done | bytes 40992 | tf_op jit(solution)/shard_map/ppermute | solution.py:408
  15.6 1.4 %collective-permute-done.5.refs_6_ = bf16[1,4,5120]{2,1,0:T(4,128)(2,1)S(1)} collective-permute-done((bf16[1,4,5120]{2,1,0:T(4,128)(2,1)S(1)}, bf16[1,4,5120]{2,1,0:T(4,128)(2,1)S(1)}, u32[]{:S(2)}, u32[]{:S(2)}) %collective-permute-start.5) | collective-permute-done | bytes 40992 | tf_op jit(solution)/shard_map/ppermute | solution.py:408
  17.0 3.1 %collective-permute-done.6.refs_7_ = bf16[1,4,5120]{2,1,0:T(4,128)(2,1)S(1)} collective-permute-done((bf16[1,4,5120]{2,1,0:T(4,128)(2,1)S(1)}, bf16[1,4,5120]{2,1,0:T(4,128)(2,1)S(1)}, u32[]{:S(2)}, u32[]{:S(2)}) %collective-permute-start.6) | collective-permute-done | bytes 40992 | tf_op jit(solution)/shard_map/ppermute | solution.py:408
  20.2 1.6 %collective-permute-done.7.other_ref = bf16[8,4,5120]{2,1,0:T(4,128)(2,1)S(1)} collective-permute-done((bf16[8,4,5120]{2,1,0:T(4,128)(2,1)S(1)}, bf16[8,4,5120]{2,1,0:T(4,128)(2,1)S(1)}, u32[]{:S(2)}, u32[]{:S(2)}) %collective-permute-start.7) | collective-permute-done | bytes 327712 | tf_op jit(solution)/shard_map/ppermute | solution.py:408
  21.8 17.8 %ffn.1 = (bf16[8,4,5120]{2,1,0:T(4,128)(2,1)S(1)}, bf16[8,4,5120]{2,1,0:T(4,128)(2,1)S(1)}) custom-call(bf16[8,4,5120]{2,1,0:T(4,128)(2,1)S(1)} %gather.1.mine_ref, bf16[8,4,5120]{2,1,0:T(4,128)(2,1)S(1)} %collective-permute-done.7.other_ref, bf16[5120,2560]{1,0:T(8,128)(2,1)} %up_ref.1, bf16[2560,5120]{1,0:T(8,128)(2,1)} %down_ref.1, ...), custom_call_target="tpu_custom_call" | custom-call | flops 5033164800 | bytes 52428800 | tf_op jit(solution)/shard_map/ffn/pallas_call | solution.py:304
  39.6 0.2 collective-permute-start.8
  39.8 1.5 %collective-permute-done.8.b_ref = bf16[8,4,5120]{2,1,0:T(4,128)(2,1)S(1)} collective-permute-done((bf16[8,4,5120]{2,1,0:T(4,128)(2,1)S(1)}, bf16[8,4,5120]{2,1,0:T(4,128)(2,1)S(1)}, u32[]{:S(2)}, u32[]{:S(2)}) %collective-permute-start.8) | collective-permute-done | bytes 327712 | tf_op jit(solution)/shard_map/ppermute | solution.py:408
  41.5 1.6 %collective-permute-start.12 = (bf16[4,4,5120]{2,1,0:T(4,128)(2,1)S(1)}, bf16[4,4,5120]{2,1,0:T(4,128)(2,1)S(1)}, u32[]{:S(2)}, u32[]{:S(2)}) collective-permute-start(bf16[4,4,5120]{2,1,0:T(4,128)(2,1)S(1)} %get-tuple-element.39), channel_id=1, source_target_pairs={{0,2},{1,3},{2,0},{3,1},{4,6},{5,7},{6,4},{7,5},{8,10},{9,11},{10,... | collective-permute-start | bytes 491528 | tf_op jit(solution)/shard_map/ppermute | solution.py:408
  43.1 1.0 %collective-permute-start.10 = (bf16[1,4,5120]{2,1,0:T(4,128)(2,1)S(1)}, bf16[1,4,5120]{2,1,0:T(4,128)(2,1)S(1)}, u32[]{:S(2)}, u32[]{:S(2)}) collective-permute-start(bf16[1,4,5120]{2,1,0:T(4,128)(2,1)S(1)} %get-tuple-element.37), channel_id=1, source_target_pairs={{0,8},{1,9},{2,10},{3,11},{4,12},{5,13},{6,14},{7,15},{8,0},{9,1},... | collective-permute-start | bytes 122888 | tf_op jit(solution)/shard_map/ppermute | solution.py:408
  44.1 3.4 %collective-permute-start.11 = (bf16[1,4,5120]{2,1,0:T(4,128)(2,1)S(1)}, bf16[1,4,5120]{2,1,0:T(4,128)(2,1)S(1)}, u32[]{:S(2)}, u32[]{:S(2)}) collective-permute-start(bf16[1,4,5120]{2,1,0:T(4,128)(2,1)S(1)} %get-tuple-element.38), channel_id=1, source_target_pairs={{0,12},{1,13},{2,14},{3,15},{4,8},{5,9},{6,10},{7,11},{8,4},{9,5},... | collective-permute-start | bytes 122888 | tf_op jit(solution)/shard_map/ppermute | solution.py:408
  47.5 0.3 collective-permute-done.12.refs_0_.refs_4_
  47.9 1.0 %collective-permute-start.14 = (bf16[1,4,5120]{2,1,0:T(4,128)(2,1)S(1)}, bf16[1,4,5120]{2,1,0:T(4,128)(2,1)S(1)}, u32[]{:S(2)}, u32[]{:S(2)}) collective-permute-start(bf16[1,4,5120]{2,1,0:T(4,128)(2,1)S(1)} %get-tuple-element.41), channel_id=1, source_target_pairs={{0,8},{1,9},{2,10},{3,11},{4,12},{5,13},{6,14},{7,15},{8,0},{9,1},... | collective-permute-start | bytes 122888 | tf_op jit(solution)/shard_map/ppermute | solution.py:408
  48.9 3.4 %collective-permute-start.15 = (bf16[1,4,5120]{2,1,0:T(4,128)(2,1)S(1)}, bf16[1,4,5120]{2,1,0:T(4,128)(2,1)S(1)}, u32[]{:S(2)}, u32[]{:S(2)}) collective-permute-start(bf16[1,4,5120]{2,1,0:T(4,128)(2,1)S(1)} %get-tuple-element.42), channel_id=1, source_target_pairs={{0,12},{1,13},{2,14},{3,15},{4,8},{5,9},{6,10},{7,11},{8,4},{9,5},... | collective-permute-start | bytes 122888 | tf_op jit(solution)/shard_map/ppermute | solution.py:408
  52.3 0.9 %collective-permute-done.14.refs_6_ = bf16[1,4,5120]{2,1,0:T(4,128)(2,1)S(1)} collective-permute-done((bf16[1,4,5120]{2,1,0:T(4,128)(2,1)S(1)}, bf16[1,4,5120]{2,1,0:T(4,128)(2,1)S(1)}, u32[]{:S(2)}, u32[]{:S(2)}) %collective-permute-start.14) | collective-permute-done | bytes 40992 | tf_op jit(solution)/shard_map/ppermute | solution.py:408
  53.2 1.5 %collective-permute-done.15.refs_7_ = bf16[1,4,5120]{2,1,0:T(4,128)(2,1)S(1)} collective-permute-done((bf16[1,4,5120]{2,1,0:T(4,128)(2,1)S(1)}, bf16[1,4,5120]{2,1,0:T(4,128)(2,1)S(1)}, u32[]{:S(2)}, u32[]{:S(2)}) %collective-permute-start.15) | collective-permute-done | bytes 40992 | tf_op jit(solution)/shard_map/ppermute | solution.py:408
  54.7 1.4 %unpack.1 = bf16[128,5120]{1,0:T(8,128)(2,1)} custom-call(s32[1,128]{1,0:T(1,128)S(1)} %get-tuple-element.24.target_ref, bf16[1,4,5120]{2,1,0:T(4,128)(2,1)S(1)} %get-tuple-element.35.refs_0_, bf16[1,4,5120]{2,1,0:T(4,128)(2,1)S(1)} %collective-permute-done.9.refs_1_, bf16[1,4,5120]{2,1,0:T(4,128)(2,1)S(1)} %collective-permute-done.10.refs_2_, ...), custom_call_target="tpu_custom_call" | custom-call | tf_op jit(solution)/shard_map/unpack/pallas_call | solution.py:385
  (17 shorter events, 0.4 us)
Async XLA Ops:
  0.0 21.8 %copy-start = (bf16[5120,2560]{1,0:T(8,128)(2,1)S(1)}, bf16[5120,2560]{1,0:T(8,128)(2,1)}, u32[]{:S(2)}) copy-start(bf16[5120,2560]{1,0:T(8,128)(2,1)} %gate_ref.1) | copy-start | bytes 78643200
  2.6 7.4 %collective-permute-start.3 = (bf16[4,4,5120]{2,1,0:T(4,128)(2,1)S(1)}, bf16[4,4,5120]{2,1,0:T(4,128)(2,1)S(1)}, u32[]{:S(2)}, u32[]{:S(2)}) collective-permute-start(bf16[4,4,5120]{2,1,0:T(4,128)(2,1)S(1)} %get-tuple-element.29), channel_id=1, source_target_pairs={{0,2},{1,3},{2,0},{3,1},{4,6},{5,7},{6,4},{7,5},{8,10},{9,11},{10,... | collective-permute-start | bytes 491528 | tf_op jit(solution)/shard_map/ppermute | solution.py:408
  5.6 8.7 %collective-permute-start = (bf16[1,4,5120]{2,1,0:T(4,128)(2,1)S(1)}, bf16[1,4,5120]{2,1,0:T(4,128)(2,1)S(1)}, u32[]{:S(2)}, u32[]{:S(2)}) collective-permute-start(bf16[1,4,5120]{2,1,0:T(4,128)(2,1)S(1)} %get-tuple-element.26), channel_id=1, source_target_pairs={{0,4},{1,5},{2,6},{3,7},{4,0},{5,1},{6,2},{7,3},{8,12},{9,13},{10,... | collective-permute-start | bytes 122888 | tf_op jit(solution)/shard_map/ppermute | solution.py:408
  7.2 7.3 %collective-permute-start.1 = (bf16[1,4,5120]{2,1,0:T(4,128)(2,1)S(1)}, bf16[1,4,5120]{2,1,0:T(4,128)(2,1)S(1)}, u32[]{:S(2)}, u32[]{:S(2)}) collective-permute-start(bf16[1,4,5120]{2,1,0:T(4,128)(2,1)S(1)} %get-tuple-element.27), channel_id=1, source_target_pairs={{0,8},{1,9},{2,10},{3,11},{4,12},{5,13},{6,14},{7,15},{8,0},{9,1},... | collective-permute-start | bytes 122888 | tf_op jit(solution)/shard_map/ppermute | solution.py:408
  9.8 5.8 %collective-permute-start.2 = (bf16[1,4,5120]{2,1,0:T(4,128)(2,1)S(1)}, bf16[1,4,5120]{2,1,0:T(4,128)(2,1)S(1)}, u32[]{:S(2)}, u32[]{:S(2)}) collective-permute-start(bf16[1,4,5120]{2,1,0:T(4,128)(2,1)S(1)} %get-tuple-element.28), channel_id=1, source_target_pairs={{0,12},{1,13},{2,14},{3,15},{4,8},{5,9},{6,10},{7,11},{8,4},{9,5},... | collective-permute-start | bytes 122888 | tf_op jit(solution)/shard_map/ppermute | solution.py:408
  10.0 5.6 %collective-permute-start.4 = (bf16[1,4,5120]{2,1,0:T(4,128)(2,1)S(1)}, bf16[1,4,5120]{2,1,0:T(4,128)(2,1)S(1)}, u32[]{:S(2)}, u32[]{:S(2)}) collective-permute-start(bf16[1,4,5120]{2,1,0:T(4,128)(2,1)S(1)} %get-tuple-element.30), channel_id=1, source_target_pairs={{0,4},{1,5},{2,6},{3,7},{4,0},{5,1},{6,2},{7,3},{8,12},{9,13},{10,... | collective-permute-start | bytes 122888 | tf_op jit(solution)/shard_map/ppermute | solution.py:408
  11.7 5.3 %collective-permute-start.5 = (bf16[1,4,5120]{2,1,0:T(4,128)(2,1)S(1)}, bf16[1,4,5120]{2,1,0:T(4,128)(2,1)S(1)}, u32[]{:S(2)}, u32[]{:S(2)}) collective-permute-start(bf16[1,4,5120]{2,1,0:T(4,128)(2,1)S(1)} %get-tuple-element.31), channel_id=1, source_target_pairs={{0,8},{1,9},{2,10},{3,11},{4,12},{5,13},{6,14},{7,15},{8,0},{9,1},... | collective-permute-start | bytes 122888 | tf_op jit(solution)/shard_map/ppermute | solution.py:408
  14.3 5.8 %collective-permute-start.6 = (bf16[1,4,5120]{2,1,0:T(4,128)(2,1)S(1)}, bf16[1,4,5120]{2,1,0:T(4,128)(2,1)S(1)}, u32[]{:S(2)}, u32[]{:S(2)}) collective-permute-start(bf16[1,4,5120]{2,1,0:T(4,128)(2,1)S(1)} %get-tuple-element.32), channel_id=1, source_target_pairs={{0,12},{1,13},{2,14},{3,15},{4,8},{5,9},{6,10},{7,11},{8,4},{9,5},... | collective-permute-start | bytes 122888 | tf_op jit(solution)/shard_map/ppermute | solution.py:408
  20.1 1.7 %collective-permute-start.7 = (bf16[8,4,5120]{2,1,0:T(4,128)(2,1)S(1)}, bf16[8,4,5120]{2,1,0:T(4,128)(2,1)S(1)}, u32[]{:S(2)}, u32[]{:S(2)}) collective-permute-start(bf16[8,4,5120]{2,1,0:T(4,128)(2,1)S(1)} %gather.1.mine_ref), channel_id=1, source_target_pairs={{0,1},{1,0},{2,3},{3,2},{4,5},{5,4},{6,7},{7,6},{8,9},{9,8},{10,11... | collective-permute-start | bytes 983048 | tf_op jit(solution)/shard_map/ppermute | solution.py:408
  39.6 1.7 %collective-permute-start.8 = (bf16[8,4,5120]{2,1,0:T(4,128)(2,1)S(1)}, bf16[8,4,5120]{2,1,0:T(4,128)(2,1)S(1)}, u32[]{:S(2)}, u32[]{:S(2)}) collective-permute-start(bf16[8,4,5120]{2,1,0:T(4,128)(2,1)S(1)} %get-tuple-element.34), channel_id=1, source_target_pairs={{0,1},{1,0},{2,3},{3,2},{4,5},{5,4},{6,7},{7,6},{8,9},{9,8},{10,11... | collective-permute-start | bytes 983048 | tf_op jit(solution)/shard_map/ppermute | solution.py:408
  41.5 6.3 %collective-permute-start.12 = (bf16[4,4,5120]{2,1,0:T(4,128)(2,1)S(1)}, bf16[4,4,5120]{2,1,0:T(4,128)(2,1)S(1)}, u32[]{:S(2)}, u32[]{:S(2)}) collective-permute-start(bf16[4,4,5120]{2,1,0:T(4,128)(2,1)S(1)} %get-tuple-element.39), channel_id=1, source_target_pairs={{0,2},{1,3},{2,0},{3,1},{4,6},{5,7},{6,4},{7,5},{8,10},{9,11},{10,... | collective-permute-start | bytes 491528 | tf_op jit(solution)/shard_map/ppermute | solution.py:408
  43.1 5.8 %collective-permute-start.9 = (bf16[1,4,5120]{2,1,0:T(4,128)(2,1)S(1)}, bf16[1,4,5120]{2,1,0:T(4,128)(2,1)S(1)}, u32[]{:S(2)}, u32[]{:S(2)}) collective-permute-start(bf16[1,4,5120]{2,1,0:T(4,128)(2,1)S(1)} %get-tuple-element.36), channel_id=1, source_target_pairs={{0,4},{1,5},{2,6},{3,7},{4,0},{5,1},{6,2},{7,3},{8,12},{9,13},{10,... | collective-permute-start | bytes 122888 | tf_op jit(solution)/shard_map/ppermute | solution.py:408
  43.1 9.2 %collective-permute-start.10 = (bf16[1,4,5120]{2,1,0:T(4,128)(2,1)S(1)}, bf16[1,4,5120]{2,1,0:T(4,128)(2,1)S(1)}, u32[]{:S(2)}, u32[]{:S(2)}) collective-permute-start(bf16[1,4,5120]{2,1,0:T(4,128)(2,1)S(1)} %get-tuple-element.37), channel_id=1, source_target_pairs={{0,8},{1,9},{2,10},{3,11},{4,12},{5,13},{6,14},{7,15},{8,0},{9,1},... | collective-permute-start | bytes 122888 | tf_op jit(solution)/shard_map/ppermute | solution.py:408
  44.1 8.2 %collective-permute-start.11 = (bf16[1,4,5120]{2,1,0:T(4,128)(2,1)S(1)}, bf16[1,4,5120]{2,1,0:T(4,128)(2,1)S(1)}, u32[]{:S(2)}, u32[]{:S(2)}) collective-permute-start(bf16[1,4,5120]{2,1,0:T(4,128)(2,1)S(1)} %get-tuple-element.38), channel_id=1, source_target_pairs={{0,12},{1,13},{2,14},{3,15},{4,8},{5,9},{6,10},{7,11},{8,4},{9,5},... | collective-permute-start | bytes 122888 | tf_op jit(solution)/shard_map/ppermute | solution.py:408
  47.8 4.5 %collective-permute-start.13 = (bf16[1,4,5120]{2,1,0:T(4,128)(2,1)S(1)}, bf16[1,4,5120]{2,1,0:T(4,128)(2,1)S(1)}, u32[]{:S(2)}, u32[]{:S(2)}) collective-permute-start(bf16[1,4,5120]{2,1,0:T(4,128)(2,1)S(1)} %get-tuple-element.40), channel_id=1, source_target_pairs={{0,4},{1,5},{2,6},{3,7},{4,0},{5,1},{6,2},{7,3},{8,12},{9,13},{10,... | collective-permute-start | bytes 122888 | tf_op jit(solution)/shard_map/ppermute | solution.py:408
  47.9 5.3 %collective-permute-start.14 = (bf16[1,4,5120]{2,1,0:T(4,128)(2,1)S(1)}, bf16[1,4,5120]{2,1,0:T(4,128)(2,1)S(1)}, u32[]{:S(2)}, u32[]{:S(2)}) collective-permute-start(bf16[1,4,5120]{2,1,0:T(4,128)(2,1)S(1)} %get-tuple-element.41), channel_id=1, source_target_pairs={{0,8},{1,9},{2,10},{3,11},{4,12},{5,13},{6,14},{7,15},{8,0},{9,1},... | collective-permute-start | bytes 122888 | tf_op jit(solution)/shard_map/ppermute | solution.py:408
  48.9 5.8 %collective-permute-start.15 = (bf16[1,4,5120]{2,1,0:T(4,128)(2,1)S(1)}, bf16[1,4,5120]{2,1,0:T(4,128)(2,1)S(1)}, u32[]{:S(2)}, u32[]{:S(2)}) collective-permute-start(bf16[1,4,5120]{2,1,0:T(4,128)(2,1)S(1)} %get-tuple-element.42), channel_id=1, source_target_pairs={{0,12},{1,13},{2,14},{3,15},{4,8},{5,9},{6,10},{7,11},{8,4},{9,5},... | collective-permute-start | bytes 122888 | tf_op jit(solution)/shard_map/ppermute | solution.py:408

commit v6 on v5

--- a/solution.py
+++ b/solution.py
@@ -70,19 +70,21 @@
         rows_ref[first + i * CAP : first + (i + 1) * CAP, :] = blocks_ref[i].astype(rows_ref.dtype)
 
 
-def store_blocks(values, singles, groups):
-    outers = len(singles)
-    for i in range(values.shape[0] // CAP):
-        block = values[i * CAP : (i + 1) * CAP].astype(jnp.bfloat16)
-        if i < outers:
-            singles[i][0] = block
-        else:
-            groups[i // outers - 1][i % outers] = block
+def block_refs(outers, inners, refs):
+    for i in range(inners):
+        for j in range(outers):
+            if j == 1:
+                yield i * outers + j, refs[1], i
+            elif i == 0:
+                yield j, refs[j], 0
+            else:
+                yield i * outers + j, refs[outers + i - 1], max(j - 1, 0)
 
 
 def blocks_shapes(chips, width):
     outers, inners = grid_of(chips)
-    return [blocks_out((1, CAP, width))] * outers + [blocks_out((outers, CAP, width))] * (inners - 1)
+    counts = [1, inners] + [1] * (outers - 2) + [outers - 1] * (inners - 1)
+    return [blocks_out((count, CAP, width)) for count in counts]
 
 
 def pack_kernel(outers, *refs):
@@ -103,19 +105,23 @@
     target = token_rows(ids[...])
     target_ref[...] = target
     layout = slot_layout(target, experts)
+    moves[3].wait()
+    own = lax.broadcasted_iota(jnp.int32, (rows, EXP_FL), 1) == experts
+    column = jnp.dot(
+        own.astype(jnp.float32).astype(jnp.bfloat16),
+        router[...],
+        preferred_element_type=jnp.float32,
+    )
     moves[1].wait()
     packed = jnp.dot(layout, tokens[...], preferred_element_type=jnp.float32)
     mean_square = jnp.mean(packed * packed, axis=-1, keepdims=True)
     moves[2].wait()
     normed = (packed * lax.rsqrt(mean_square + 1e-05) * gain[...]).astype(jnp.bfloat16)
-    moves[3].wait()
-    logits = lax.dot_general(
-        normed, router[...], (((1,), (1,)), ((), ())), preferred_element_type=jnp.float32
-    )
-    own = lax.broadcasted_iota(jnp.int32, logits.shape, 1) == experts
-    logit = jnp.sum(jnp.where(own, logits, 0.0), axis=-1, keepdims=True)
-    routed = normed.astype(jnp.float32) * jax.nn.sigmoid(logit)
-    store_blocks(routed, outs[:outers], outs[outers:])
+    normed = normed.astype(jnp.float32)
+    logit = jnp.sum(normed * column, axis=-1, keepdims=True)
+    routed = normed * jax.nn.sigmoid(logit)
+    for i, ref, j in block_refs(outers, inners, outs):
+        ref[j] = routed[i * CAP : (i + 1) * CAP].astype(jnp.bfloat16)
 
 
 def pack(tokens, ids, gain, router_rows, weight, chips):
@@ -135,33 +141,39 @@
     return outs[:-1], outs[-1]
 
 
-def forward_kernel(groups, *refs):
+def forward_kernel(first, groups, *refs):
     for i, out_ref in enumerate(refs[groups:]):
         for j in range(groups):
-            out_ref[j] = refs[j][i + 1]
+            out_ref[j] = refs[j][first + i]
 
 
 def forward(arrays):
-    outers, _, width = arrays[0].shape
+    count, _, width = arrays[0].shape
     vmem = pl.BlockSpec(memory_space=pltpu.VMEM)
     return pl.pallas_call(
-        functools.partial(forward_kernel, len(arrays)),
+        functools.partial(forward_kernel, 1, len(arrays)),
         in_specs=[vmem] * len(arrays),
-        out_specs=[vmem] * (outers - 1),
-        out_shape=[blocks_out((len(arrays), CAP, width))] * (outers - 1),
-        compiler_params=pltpu.CompilerParams(vmem_limit_bytes=(4 if outers <= 4 else 24) * MIB),
+        out_specs=[vmem] * (count - 1),
+        out_shape=[blocks_out((len(arrays), CAP, width))] * (count - 1),
+        compiler_params=pltpu.CompilerParams(vmem_limit_bytes=(4 if count <= 4 else 24) * MIB),
         name="forward",
     )(*[blocks_in_vmem(x) for x in arrays])
 
 
 def piece_blocks(outers, inners, refs):
-    singles, groups, forwarded = refs[:outers], refs[outers : outers + inners - 1], refs[outers + inners - 1 :]
-    for i in range(outers):
-        yield i, singles[i][0]
-    for i in range(1, inners):
-        yield i * outers, groups[i - 1][0]
-        for j in range(1, outers):
-            yield i * outers + j, forwarded[j - 1][i - 1]
+    direct, near = refs[:outers], refs[outers : outers + inners - 1]
+    onward, beside = refs[outers + inners - 1 : 1 - inners], refs[1 - inners :]
+    for i in range(inners):
+        for j in range(outers):
+            if i == 0:
+                block = direct[j][0]
+            elif j == 0:
+                block = near[i - 1][0]
+            elif j == 1:
+                block = beside[i - 1][0]
+            else:
+                block = onward[j - 2][i - 1]
+            yield i * outers + j, block
 
 
 def gather_kernel(outers, inners, *refs):
@@ -331,14 +343,9 @@
     )
 
 
-def add_kernel(outers, a_ref, b_ref, *outs):
-    chips = a_ref.shape[0]
-    for i in range(chips):
-        block = (a_ref[i].astype(jnp.float32) + b_ref[i].astype(jnp.float32)).astype(jnp.bfloat16)
-        if i < outers:
-            outs[i][0] = block
-        else:
-            outs[outers + i // outers - 1][i % outers] = block
+def add_kernel(outers, inners, a_ref, b_ref, *outs):
+    for i, ref, j in block_refs(outers, inners, outs):
+        ref[j] = (a_ref[i].astype(jnp.float32) + b_ref[i].astype(jnp.float32)).astype(jnp.bfloat16)
 
 
 def add(a, b):
@@ -346,7 +353,7 @@
     outers, inners = grid_of(chips)
     vmem = pl.BlockSpec(memory_space=pltpu.VMEM)
     return pl.pallas_call(
-        functools.partial(add_kernel, outers),
+        functools.partial(add_kernel, outers, inners),
         in_specs=[vmem] * 2,
         out_specs=[vmem] * (outers + inners - 1),
         out_shape=blocks_shapes(chips, width),
@@ -408,11 +415,11 @@
         return lax.ppermute(x, "expert", [(i, i ^ offset) for i in range(devices)])
 
     def exchange(blocks):
-        singles, groups = blocks[:outers], blocks[outers:]
-        near = [send(x, 2 * (i + 1)) for i, x in enumerate(groups)]
-        direct = [send(x, step) for x, step in zip(singles[1:], steps)]
-        onward = [send(x, step) for x, step in zip(forward(near), steps)]
-        return [singles[0], *direct, *near, *onward]
+        near = [send(x, 2 * (i + 1)) for i, x in enumerate(blocks[outers:])]
+        direct = [send(x, step) for x, step in zip(blocks[1:outers], steps)]
+        onward = [send(x, step) for x, step in zip(forward(near), steps[1:])]
+        beside = [send(x, 2 * (i + 1)) for i, x in enumerate(forward(direct[:1]))]
+        return [blocks[0], *direct, *near, *onward, *beside]
 
     blocks, target = pack(tokens, ids, norm_gain.reshape(1, -1), router.T, up_weight, chips)
     mine = gather(exchange(blocks), chips)

time: 56.2 us -> 54.7 us (0.973)
  starting transfers between devices: 22.5 us -> 21.1 us
    ppermute x16, starting transfers between devices: 22.5 us -> 21.1 us  [send(): return lax.ppermute(x, 'expert', [(i, i ^ offset) for i in range(devices)])]
  transfers between devices with their start and end apart: 16 -> 16, of which waited for: 8 -> 11; matrix products, arithmetic and copies ran while one was open for 0% -> 0% of each run, Pallas kernels for 0% -> 0%
where the time goes in v6:
time: 54.7 us; the launch traced here: 54.5 us
  Pallas kernels  21.8 us (40%)
  starting transfers between devices  21.1 us (39%)
  waiting for transfers between devices  11.5 us (21%)
    ppermute x16, starting transfers between devices, send(): return lax.ppermute(x, 'expert', [(i, i ^ offset) for i in range(devices)])  21.1 us
    pallas_call x1, Pallas kernels, ffn(): pl.pallas_call(functools.partial(ffn_kernel, deep, wide), in_specs=[vmem]...  17.8 us
    ppermute x16, waiting for transfers between devices, send(): return lax.ppermute(x, 'expert', [(i, i ^ offset) for i in range(devices)])  11.5 us
    pallas_call x1, Pallas kernels, pack(): pl.pallas_call(functools.partial(pack_kernel, outers), in_specs=[pl.Block...  2.37 us
    pallas_call x1, Pallas kernels, unpack(): pl.pallas_call(functools.partial(unpack_kernel, *grid_of(chips)), in_spec...  1.4 us
  transfers between devices with their start and end apart: 16, of which 11 were waited for; matrix products, arithmetic and copies ran while one was open for 0% of the time, Pallas kernels for 0%

profile of v6, /device:TPU:0, one launch (start us, length us, event | category | flops | bytes accessed | tf_op | source)
XLA Modules:
  0.0 54.5 jit_solution(12690184276690830018)
XLA Ops:
  0.0 2.4 %pack.1 = (bf16[1,4,5120]{2,1,0:T(4,128)(2,1)S(1)}, bf16[2,4,5120]{2,1,0:T(4,128)(2,1)S(1)}, bf16[1,4,5120]{2,1,0:T(4,128)(2,1)S(1)}, bf16[1,4,5120]{2,1,0:T(4,1...) custom-call(s32[1,128]{1,0:T(1,128)} %bitcast.5, bf16[128,5120]{1,0:T(8,128)(2,1)} %refs_1_.1, ...), custom_call_target="tpu_custom_call" | custom-call | tf_op jit(solution)/shard_map/pack/pallas_call | solution.py:131
  2.4 3.0 %collective-permute-start.3 = (bf16[3,4,5120]{2,1,0:T(4,128)(2,1)S(1)}, bf16[3,4,5120]{2,1,0:T(4,128)(2,1)S(1)}, u32[]{:S(2)}, u32[]{:S(2)}) collective-permute-start(bf16[3,4,5120]{2,1,0:T(4,128)(2,1)S(1)} %get-tuple-element.27), channel_id=1, source_target_pairs={{0,2},{1,3},{2,0},{3,1},{4,6},{5,7},{6,4},{7,5},{8,10},{9,11},{10,... | collective-permute-start | bytes 368648 | tf_op jit(solution)/shard_map/ppermute | solution.py:415
  5.4 1.6 %collective-permute-start = (bf16[2,4,5120]{2,1,0:T(4,128)(2,1)S(1)}, bf16[2,4,5120]{2,1,0:T(4,128)(2,1)S(1)}, u32[]{:S(2)}, u32[]{:S(2)}) collective-permute-start(bf16[2,4,5120]{2,1,0:T(4,128)(2,1)S(1)} %get-tuple-element.24), channel_id=1, source_target_pairs={{0,4},{1,5},{2,6},{3,7},{4,0},{5,1},{6,2},{7,3},{8,12},{9,13},{10,... | collective-permute-start | bytes 245768 | tf_op jit(solution)/shard_map/ppermute | solution.py:415
  7.0 2.6 %collective-permute-start.1 = (bf16[1,4,5120]{2,1,0:T(4,128)(2,1)S(1)}, bf16[1,4,5120]{2,1,0:T(4,128)(2,1)S(1)}, u32[]{:S(2)}, u32[]{:S(2)}) collective-permute-start(bf16[1,4,5120]{2,1,0:T(4,128)(2,1)S(1)} %get-tuple-element.25), channel_id=1, source_target_pairs={{0,8},{1,9},{2,10},{3,11},{4,12},{5,13},{6,14},{7,15},{8,0},{9,1},... | collective-permute-start | bytes 122888 | tf_op jit(solution)/shard_map/ppermute | solution.py:415
  9.6 0.2 collective-permute-start.2
  9.9 0.3 collective-permute-start.6
  10.2 2.9 %collective-permute-start.4 = (bf16[1,4,5120]{2,1,0:T(4,128)(2,1)S(1)}, bf16[1,4,5120]{2,1,0:T(4,128)(2,1)S(1)}, u32[]{:S(2)}, u32[]{:S(2)}) collective-permute-start(bf16[1,4,5120]{2,1,0:T(4,128)(2,1)S(1)} %get-tuple-element.28), channel_id=1, source_target_pairs={{0,8},{1,9},{2,10},{3,11},{4,12},{5,13},{6,14},{7,15},{8,0},{9,1},... | collective-permute-start | bytes 122888 | tf_op jit(solution)/shard_map/ppermute | solution.py:415
  13.0 1.3 %collective-permute-start.5 = (bf16[1,4,5120]{2,1,0:T(4,128)(2,1)S(1)}, bf16[1,4,5120]{2,1,0:T(4,128)(2,1)S(1)}, u32[]{:S(2)}, u32[]{:S(2)}) collective-permute-start(bf16[1,4,5120]{2,1,0:T(4,128)(2,1)S(1)} %get-tuple-element.29), channel_id=1, source_target_pairs={{0,12},{1,13},{2,14},{3,15},{4,8},{5,9},{6,10},{7,11},{8,4},{9,5},... | collective-permute-start | bytes 122888 | tf_op jit(solution)/shard_map/ppermute | solution.py:415
  14.4 1.2 %collective-permute-done.2.refs_3_ = bf16[1,4,5120]{2,1,0:T(4,128)(2,1)S(1)} collective-permute-done((bf16[1,4,5120]{2,1,0:T(4,128)(2,1)S(1)}, bf16[1,4,5120]{2,1,0:T(4,128)(2,1)S(1)}, u32[]{:S(2)}, u32[]{:S(2)}) %collective-permute-start.2) | collective-permute-done | bytes 40992 | tf_op jit(solution)/shard_map/ppermute | solution.py:415
  15.6 1.3 %collective-permute-done.4.refs_5_ = bf16[1,4,5120]{2,1,0:T(4,128)(2,1)S(1)} collective-permute-done((bf16[1,4,5120]{2,1,0:T(4,128)(2,1)S(1)}, bf16[1,4,5120]{2,1,0:T(4,128)(2,1)S(1)}, u32[]{:S(2)}, u32[]{:S(2)}) %collective-permute-start.4) | collective-permute-done | bytes 40992 | tf_op jit(solution)/shard_map/ppermute | solution.py:415
  16.9 2.0 %collective-permute-done.5.refs_6_ = bf16[1,4,5120]{2,1,0:T(4,128)(2,1)S(1)} collective-permute-done((bf16[1,4,5120]{2,1,0:T(4,128)(2,1)S(1)}, bf16[1,4,5120]{2,1,0:T(4,128)(2,1)S(1)}, u32[]{:S(2)}, u32[]{:S(2)}) %collective-permute-start.5) | collective-permute-done | bytes 40992 | tf_op jit(solution)/shard_map/ppermute | solution.py:415
  18.9 1.6 %collective-permute-done.7.other_ref = bf16[8,4,5120]{2,1,0:T(4,128)(2,1)S(1)} collective-permute-done((bf16[8,4,5120]{2,1,0:T(4,128)(2,1)S(1)}, bf16[8,4,5120]{2,1,0:T(4,128)(2,1)S(1)}, u32[]{:S(2)}, u32[]{:S(2)}) %collective-permute-start.7) | collective-permute-done | bytes 327712 | tf_op jit(solution)/shard_map/ppermute | solution.py:415
  20.6 17.8 %ffn.1 = (bf16[8,4,5120]{2,1,0:T(4,128)(2,1)S(1)}, bf16[8,4,5120]{2,1,0:T(4,128)(2,1)S(1)}) custom-call(bf16[8,4,5120]{2,1,0:T(4,128)(2,1)S(1)} %gather.1.mine_ref, bf16[8,4,5120]{2,1,0:T(4,128)(2,1)S(1)} %collective-permute-done.7.other_ref, bf16[5120,2560]{1,0:T(8,128)(2,1)} %up_ref.1, bf16[2560,5120]{1,0:T(8,128)(2,1)} %down_ref.1, ...), custom_call_target="tpu_custom_call" | custom-call | flops 5033164800 | bytes 52428800 | tf_op jit(solution)/shard_map/ffn/pallas_call | solution.py:316
  38.6 1.5 %collective-permute-done.8.b_ref = bf16[8,4,5120]{2,1,0:T(4,128)(2,1)S(1)} collective-permute-done((bf16[8,4,5120]{2,1,0:T(4,128)(2,1)S(1)}, bf16[8,4,5120]{2,1,0:T(4,128)(2,1)S(1)}, u32[]{:S(2)}, u32[]{:S(2)}) %collective-permute-start.8) | collective-permute-done | bytes 327712 | tf_op jit(solution)/shard_map/ppermute | solution.py:415
  40.3 1.6 %collective-permute-start.12 = (bf16[3,4,5120]{2,1,0:T(4,128)(2,1)S(1)}, bf16[3,4,5120]{2,1,0:T(4,128)(2,1)S(1)}, u32[]{:S(2)}, u32[]{:S(2)}) collective-permute-start(bf16[3,4,5120]{2,1,0:T(4,128)(2,1)S(1)} %get-tuple-element.36), channel_id=1, source_target_pairs={{0,2},{1,3},{2,0},{3,1},{4,6},{5,7},{6,4},{7,5},{8,10},{9,11},{10,... | collective-permute-start | bytes 368648 | tf_op jit(solution)/shard_map/ppermute | solution.py:415
  41.8 1.9 %collective-permute-start.10 = (bf16[1,4,5120]{2,1,0:T(4,128)(2,1)S(1)}, bf16[1,4,5120]{2,1,0:T(4,128)(2,1)S(1)}, u32[]{:S(2)}, u32[]{:S(2)}) collective-permute-start(bf16[1,4,5120]{2,1,0:T(4,128)(2,1)S(1)} %get-tuple-element.34), channel_id=1, source_target_pairs={{0,8},{1,9},{2,10},{3,11},{4,12},{5,13},{6,14},{7,15},{8,0},{9,1},... | collective-permute-start | bytes 122888 | tf_op jit(solution)/shard_map/ppermute | solution.py:415
  43.7 2.5 %collective-permute-start.11 = (bf16[1,4,5120]{2,1,0:T(4,128)(2,1)S(1)}, bf16[1,4,5120]{2,1,0:T(4,128)(2,1)S(1)}, u32[]{:S(2)}, u32[]{:S(2)}) collective-permute-start(bf16[1,4,5120]{2,1,0:T(4,128)(2,1)S(1)} %get-tuple-element.35), channel_id=1, source_target_pairs={{0,12},{1,13},{2,14},{3,15},{4,8},{5,9},{6,10},{7,11},{8,4},{9,5},... | collective-permute-start | bytes 122888 | tf_op jit(solution)/shard_map/ppermute | solution.py:415
  46.2 0.4 collective-permute-done.9.refs_0_.refs_1_
  46.7 0.5 collective-permute-start.15
  47.3 2.4 %collective-permute-start.14 = (bf16[1,4,5120]{2,1,0:T(4,128)(2,1)S(1)}, bf16[1,4,5120]{2,1,0:T(4,128)(2,1)S(1)}, u32[]{:S(2)}, u32[]{:S(2)}) collective-permute-start(bf16[1,4,5120]{2,1,0:T(4,128)(2,1)S(1)} %get-tuple-element.38), channel_id=1, source_target_pairs={{0,12},{1,13},{2,14},{3,15},{4,8},{5,9},{6,10},{7,11},{8,4},{9,5},... | collective-permute-start | bytes 122888 | tf_op jit(solution)/shard_map/ppermute | solution.py:415
  49.8 0.9 %collective-permute-done.15.refs_7_ = bf16[1,4,5120]{2,1,0:T(4,128)(2,1)S(1)} collective-permute-done((bf16[1,4,5120]{2,1,0:T(4,128)(2,1)S(1)}, bf16[1,4,5120]{2,1,0:T(4,128)(2,1)S(1)}, u32[]{:S(2)}, u32[]{:S(2)}) %collective-permute-start.15) | collective-permute-done | bytes 40992 | tf_op jit(solution)/shard_map/ppermute | solution.py:415
  50.7 1.5 %collective-permute-done.13.refs_5_ = bf16[1,4,5120]{2,1,0:T(4,128)(2,1)S(1)} collective-permute-done((bf16[1,4,5120]{2,1,0:T(4,128)(2,1)S(1)}, bf16[1,4,5120]{2,1,0:T(4,128)(2,1)S(1)}, u32[]{:S(2)}, u32[]{:S(2)}) %collective-permute-start.13) | collective-permute-done | bytes 40992 | tf_op jit(solution)/shard_map/ppermute | solution.py:415
  52.2 1.0 %collective-permute-done.14.refs_6_ = bf16[1,4,5120]{2,1,0:T(4,128)(2,1)S(1)} collective-permute-done((bf16[1,4,5120]{2,1,0:T(4,128)(2,1)S(1)}, bf16[1,4,5120]{2,1,0:T(4,128)(2,1)S(1)}, u32[]{:S(2)}, u32[]{:S(2)}) %collective-permute-start.14) | collective-permute-done | bytes 40992 | tf_op jit(solution)/shard_map/ppermute | solution.py:415
  53.1 1.4 %unpack.1 = bf16[128,5120]{1,0:T(8,128)(2,1)} custom-call(s32[1,128]{1,0:T(1,128)S(1)} %get-tuple-element.22.target_ref, bf16[1,4,5120]{2,1,0:T(4,128)(2,1)S(1)} %get-tuple-element.32.refs_0_, bf16[2,4,5120]{2,1,0:T(4,128)(2,1)S(1)} %collective-permute-done.9.refs_0_.refs_1_, bf16[1,4,5120]{2,1,0:T(4,128)(2,1)S(1)} %collective-permute-done.10.refs_2_, ...), custom_call_target="tpu_custom_call" | custom-call | tf_op jit(solution)/shard_map/unpack/pallas_call | solution.py:392
  (19 shorter events, 0.7 us)
Async XLA Ops:
  0.0 20.6 %copy-start = (bf16[5120,2560]{1,0:T(8,128)(2,1)S(1)}, bf16[5120,2560]{1,0:T(8,128)(2,1)}, u32[]{:S(2)}) copy-start(bf16[5120,2560]{1,0:T(8,128)(2,1)} %gate_ref.1) | copy-start | bytes 78643200
  2.4 7.8 %collective-permute-start.3 = (bf16[3,4,5120]{2,1,0:T(4,128)(2,1)S(1)}, bf16[3,4,5120]{2,1,0:T(4,128)(2,1)S(1)}, u32[]{:S(2)}, u32[]{:S(2)}) collective-permute-start(bf16[3,4,5120]{2,1,0:T(4,128)(2,1)S(1)} %get-tuple-element.27), channel_id=1, source_target_pairs={{0,2},{1,3},{2,0},{3,1},{4,6},{5,7},{6,4},{7,5},{8,10},{9,11},{10,... | collective-permute-start | bytes 368648 | tf_op jit(solution)/shard_map/ppermute | solution.py:415
  5.4 4.5 %collective-permute-start = (bf16[2,4,5120]{2,1,0:T(4,128)(2,1)S(1)}, bf16[2,4,5120]{2,1,0:T(4,128)(2,1)S(1)}, u32[]{:S(2)}, u32[]{:S(2)}) collective-permute-start(bf16[2,4,5120]{2,1,0:T(4,128)(2,1)S(1)} %get-tuple-element.24), channel_id=1, source_target_pairs={{0,4},{1,5},{2,6},{3,7},{4,0},{5,1},{6,2},{7,3},{8,12},{9,13},{10,... | collective-permute-start | bytes 245768 | tf_op jit(solution)/shard_map/ppermute | solution.py:415
  7.0 7.4 %collective-permute-start.1 = (bf16[1,4,5120]{2,1,0:T(4,128)(2,1)S(1)}, bf16[1,4,5120]{2,1,0:T(4,128)(2,1)S(1)}, u32[]{:S(2)}, u32[]{:S(2)}) collective-permute-start(bf16[1,4,5120]{2,1,0:T(4,128)(2,1)S(1)} %get-tuple-element.25), channel_id=1, source_target_pairs={{0,8},{1,9},{2,10},{3,11},{4,12},{5,13},{6,14},{7,15},{8,0},{9,1},... | collective-permute-start | bytes 122888 | tf_op jit(solution)/shard_map/ppermute | solution.py:415
  9.6 6.0 %collective-permute-start.2 = (bf16[1,4,5120]{2,1,0:T(4,128)(2,1)S(1)}, bf16[1,4,5120]{2,1,0:T(4,128)(2,1)S(1)}, u32[]{:S(2)}, u32[]{:S(2)}) collective-permute-start(bf16[1,4,5120]{2,1,0:T(4,128)(2,1)S(1)} %get-tuple-element.26), channel_id=1, source_target_pairs={{0,12},{1,13},{2,14},{3,15},{4,8},{5,9},{6,10},{7,11},{8,4},{9,5},... | collective-permute-start | bytes 122888 | tf_op jit(solution)/shard_map/ppermute | solution.py:415
  9.9 5.7 %collective-permute-start.6 = (bf16[1,4,5120]{2,1,0:T(4,128)(2,1)S(1)}, bf16[1,4,5120]{2,1,0:T(4,128)(2,1)S(1)}, u32[]{:S(2)}, u32[]{:S(2)}) collective-permute-start(bf16[1,4,5120]{2,1,0:T(4,128)(2,1)S(1)} %forward.5), channel_id=1, source_target_pairs={{0,2},{1,3},{2,0},{3,1},{4,6},{5,7},{6,4},{7,5},{8,10},{9,11},{10,... | collective-permute-start | bytes 122888 | tf_op jit(solution)/shard_map/ppermute | solution.py:415
  10.2 6.7 %collective-permute-start.4 = (bf16[1,4,5120]{2,1,0:T(4,128)(2,1)S(1)}, bf16[1,4,5120]{2,1,0:T(4,128)(2,1)S(1)}, u32[]{:S(2)}, u32[]{:S(2)}) collective-permute-start(bf16[1,4,5120]{2,1,0:T(4,128)(2,1)S(1)} %get-tuple-element.28), channel_id=1, source_target_pairs={{0,8},{1,9},{2,10},{3,11},{4,12},{5,13},{6,14},{7,15},{8,0},{9,1},... | collective-permute-start | bytes 122888 | tf_op jit(solution)/shard_map/ppermute | solution.py:415
  13.0 5.8 %collective-permute-start.5 = (bf16[1,4,5120]{2,1,0:T(4,128)(2,1)S(1)}, bf16[1,4,5120]{2,1,0:T(4,128)(2,1)S(1)}, u32[]{:S(2)}, u32[]{:S(2)}) collective-permute-start(bf16[1,4,5120]{2,1,0:T(4,128)(2,1)S(1)} %get-tuple-element.29), channel_id=1, source_target_pairs={{0,12},{1,13},{2,14},{3,15},{4,8},{5,9},{6,10},{7,11},{8,4},{9,5},... | collective-permute-start | bytes 122888 | tf_op jit(solution)/shard_map/ppermute | solution.py:415
  18.9 1.7 %collective-permute-start.7 = (bf16[8,4,5120]{2,1,0:T(4,128)(2,1)S(1)}, bf16[8,4,5120]{2,1,0:T(4,128)(2,1)S(1)}, u32[]{:S(2)}, u32[]{:S(2)}) collective-permute-start(bf16[8,4,5120]{2,1,0:T(4,128)(2,1)S(1)} %gather.1.mine_ref), channel_id=1, source_target_pairs={{0,1},{1,0},{2,3},{3,2},{4,5},{5,4},{6,7},{7,6},{8,9},{9,8},{10,11... | collective-permute-start | bytes 983048 | tf_op jit(solution)/shard_map/ppermute | solution.py:415
  38.4 1.7 %collective-permute-start.8 = (bf16[8,4,5120]{2,1,0:T(4,128)(2,1)S(1)}, bf16[8,4,5120]{2,1,0:T(4,128)(2,1)S(1)}, u32[]{:S(2)}, u32[]{:S(2)}) collective-permute-start(bf16[8,4,5120]{2,1,0:T(4,128)(2,1)S(1)} %get-tuple-element.31), channel_id=1, source_target_pairs={{0,1},{1,0},{2,3},{3,2},{4,5},{5,4},{6,7},{7,6},{8,9},{9,8},{10,11... | collective-permute-start | bytes 983048 | tf_op jit(solution)/shard_map/ppermute | solution.py:415
  40.3 6.9 %collective-permute-start.12 = (bf16[3,4,5120]{2,1,0:T(4,128)(2,1)S(1)}, bf16[3,4,5120]{2,1,0:T(4,128)(2,1)S(1)}, u32[]{:S(2)}, u32[]{:S(2)}) collective-permute-start(bf16[3,4,5120]{2,1,0:T(4,128)(2,1)S(1)} %get-tuple-element.36), channel_id=1, source_target_pairs={{0,2},{1,3},{2,0},{3,1},{4,6},{5,7},{6,4},{7,5},{8,10},{9,11},{10,... | collective-permute-start | bytes 368648 | tf_op jit(solution)/shard_map/ppermute | solution.py:415
  41.8 4.8 %collective-permute-start.9 = (bf16[2,4,5120]{2,1,0:T(4,128)(2,1)S(1)}, bf16[2,4,5120]{2,1,0:T(4,128)(2,1)S(1)}, u32[]{:S(2)}, u32[]{:S(2)}) collective-permute-start(bf16[2,4,5120]{2,1,0:T(4,128)(2,1)S(1)} %get-tuple-element.33), channel_id=1, source_target_pairs={{0,4},{1,5},{2,6},{3,7},{4,0},{5,1},{6,2},{7,3},{8,12},{9,13},{10,... | collective-permute-start | bytes 245768 | tf_op jit(solution)/shard_map/ppermute | solution.py:415
  41.8 7.9 %collective-permute-start.10 = (bf16[1,4,5120]{2,1,0:T(4,128)(2,1)S(1)}, bf16[1,4,5120]{2,1,0:T(4,128)(2,1)S(1)}, u32[]{:S(2)}, u32[]{:S(2)}) collective-permute-start(bf16[1,4,5120]{2,1,0:T(4,128)(2,1)S(1)} %get-tuple-element.34), channel_id=1, source_target_pairs={{0,8},{1,9},{2,10},{3,11},{4,12},{5,13},{6,14},{7,15},{8,0},{9,1},... | collective-permute-start | bytes 122888 | tf_op jit(solution)/shard_map/ppermute | solution.py:415
  43.7 6.1 %collective-permute-start.11 = (bf16[1,4,5120]{2,1,0:T(4,128)(2,1)S(1)}, bf16[1,4,5120]{2,1,0:T(4,128)(2,1)S(1)}, u32[]{:S(2)}, u32[]{:S(2)}) collective-permute-start(bf16[1,4,5120]{2,1,0:T(4,128)(2,1)S(1)} %get-tuple-element.35), channel_id=1, source_target_pairs={{0,12},{1,13},{2,14},{3,15},{4,8},{5,9},{6,10},{7,11},{8,4},{9,5},... | collective-permute-start | bytes 122888 | tf_op jit(solution)/shard_map/ppermute | solution.py:415
  46.7 4.0 %collective-permute-start.15 = (bf16[1,4,5120]{2,1,0:T(4,128)(2,1)S(1)}, bf16[1,4,5120]{2,1,0:T(4,128)(2,1)S(1)}, u32[]{:S(2)}, u32[]{:S(2)}) collective-permute-start(bf16[1,4,5120]{2,1,0:T(4,128)(2,1)S(1)} %forward.7), channel_id=1, source_target_pairs={{0,2},{1,3},{2,0},{3,1},{4,6},{5,7},{6,4},{7,5},{8,10},{9,11},{10,... | collective-permute-start | bytes 122888 | tf_op jit(solution)/shard_map/ppermute | solution.py:415
  47.2 5.0 %collective-permute-start.13 = (bf16[1,4,5120]{2,1,0:T(4,128)(2,1)S(1)}, bf16[1,4,5120]{2,1,0:T(4,128)(2,1)S(1)}, u32[]{:S(2)}, u32[]{:S(2)}) collective-permute-start(bf16[1,4,5120]{2,1,0:T(4,128)(2,1)S(1)} %get-tuple-element.37), channel_id=1, source_target_pairs={{0,8},{1,9},{2,10},{3,11},{4,12},{5,13},{6,14},{7,15},{8,0},{9,1},... | collective-permute-start | bytes 122888 | tf_op jit(solution)/shard_map/ppermute | solution.py:415
  47.3 5.9 %collective-permute-start.14 = (bf16[1,4,5120]{2,1,0:T(4,128)(2,1)S(1)}, bf16[1,4,5120]{2,1,0:T(4,128)(2,1)S(1)}, u32[]{:S(2)}, u32[]{:S(2)}) collective-permute-start(bf16[1,4,5120]{2,1,0:T(4,128)(2,1)S(1)} %get-tuple-element.38), channel_id=1, source_target_pairs={{0,12},{1,13},{2,14},{3,15},{4,8},{5,9},{6,10},{7,11},{8,4},{9,5},... | collective-permute-start | bytes 122888 | tf_op jit(solution)/shard_map/ppermute | solution.py:415

commit v7 on v6

--- a/solution.py
+++ b/solution.py
@@ -161,8 +161,9 @@
 
 
 def piece_blocks(outers, inners, refs):
-    direct, near = refs[:outers], refs[outers : outers + inners - 1]
-    onward, beside = refs[outers + inners - 1 : 1 - inners], refs[1 - inners :]
+    onward, beside = refs[: outers - 2], refs[outers - 2 : outers + inners - 3]
+    rest = refs[outers + inners - 3 :]
+    direct, near = [rest[-1], *rest[: outers - 1][::-1]], rest[outers - 1 : -1]
     for i in range(inners):
         for j in range(outers):
             if i == 0:
@@ -419,7 +420,7 @@
         direct = [send(x, step) for x, step in zip(blocks[1:outers], steps)]
         onward = [send(x, step) for x, step in zip(forward(near), steps[1:])]
         beside = [send(x, 2 * (i + 1)) for i, x in enumerate(forward(direct[:1]))]
-        return [blocks[0], *direct, *near, *onward, *beside]
+        return [*onward, *beside, *direct[::-1], *near, blocks[0]]
 
     blocks, target = pack(tokens, ids, norm_gain.reshape(1, -1), router.T, up_weight, chips)
     mine = gather(exchange(blocks), chips)

time: 54.7 us -> 54.5 us (level)
  no operation moved by 1% of the time
where the time goes in v7:
time: 54.5 us; the launch traced here: 54.4 us
  Pallas kernels  21.8 us (40%)
  starting transfers between devices  21 us (39%)
  waiting for transfers between devices  11.5 us (21%)
    ppermute x16, starting transfers between devices, send(): return lax.ppermute(x, 'expert', [(i, i ^ offset) for i in range(devices)])  21 us
    pallas_call x1, Pallas kernels, ffn(): pl.pallas_call(functools.partial(ffn_kernel, deep, wide), in_specs=[vmem]...  17.8 us
    ppermute x16, waiting for transfers between devices, send(): return lax.ppermute(x, 'expert', [(i, i ^ offset) for i in range(devices)])  11.5 us
    pallas_call x1, Pallas kernels, pack(): pl.pallas_call(functools.partial(pack_kernel, outers), in_specs=[pl.Block...  2.37 us
    pallas_call x1, Pallas kernels, unpack(): pl.pallas_call(functools.partial(unpack_kernel, *grid_of(chips)), in_spec...  1.4 us
  transfers between devices with their start and end apart: 16, of which 11 were waited for; matrix products, arithmetic and copies ran while one was open for 0% of the time, Pallas kernels for 0%

profile of v7, /device:TPU:0, one launch (start us, length us, event | category | flops | bytes accessed | tf_op | source)
XLA Modules:
  0.0 54.4 jit_solution(15883556529681354849)
XLA Ops:
  0.0 2.4 %pack.1 = (bf16[1,4,5120]{2,1,0:T(4,128)(2,1)S(1)}, bf16[2,4,5120]{2,1,0:T(4,128)(2,1)S(1)}, bf16[1,4,5120]{2,1,0:T(4,128)(2,1)S(1)}, bf16[1,4,5120]{2,1,0:T(4,1...) custom-call(s32[1,128]{1,0:T(1,128)} %bitcast.5, bf16[128,5120]{1,0:T(8,128)(2,1)} %refs_1_.1, ...), custom_call_target="tpu_custom_call" | custom-call | tf_op jit(solution)/shard_map/pack/pallas_call | solution.py:131
  2.4 3.0 %collective-permute-start = (bf16[3,4,5120]{2,1,0:T(4,128)(2,1)S(1)}, bf16[3,4,5120]{2,1,0:T(4,128)(2,1)S(1)}, u32[]{:S(2)}, u32[]{:S(2)}) collective-permute-start(bf16[3,4,5120]{2,1,0:T(4,128)(2,1)S(1)} %get-tuple-element.23), channel_id=1, source_target_pairs={{0,2},{1,3},{2,0},{3,1},{4,6},{5,7},{6,4},{7,5},{8,10},{9,11},{10,... | collective-permute-start | bytes 368648 | tf_op jit(solution)/shard_map/ppermute | solution.py:416
  5.4 1.6 %collective-permute-start.3 = (bf16[2,4,5120]{2,1,0:T(4,128)(2,1)S(1)}, bf16[2,4,5120]{2,1,0:T(4,128)(2,1)S(1)}, u32[]{:S(2)}, u32[]{:S(2)}) collective-permute-start(bf16[2,4,5120]{2,1,0:T(4,128)(2,1)S(1)} %get-tuple-element.26), channel_id=1, source_target_pairs={{0,4},{1,5},{2,6},{3,7},{4,0},{5,1},{6,2},{7,3},{8,12},{9,13},{10,... | collective-permute-start | bytes 245768 | tf_op jit(solution)/shard_map/ppermute | solution.py:416
  7.0 2.5 %collective-permute-start.5 = (bf16[1,4,5120]{2,1,0:T(4,128)(2,1)S(1)}, bf16[1,4,5120]{2,1,0:T(4,128)(2,1)S(1)}, u32[]{:S(2)}, u32[]{:S(2)}) collective-permute-start(bf16[1,4,5120]{2,1,0:T(4,128)(2,1)S(1)} %get-tuple-element.27), channel_id=1, source_target_pairs={{0,12},{1,13},{2,14},{3,15},{4,8},{5,9},{6,10},{7,11},{8,4},{9,5},... | collective-permute-start | bytes 122888 | tf_op jit(solution)/shard_map/ppermute | solution.py:416
  9.6 0.3 collective-permute-done.3.refs_0_.refs_5_
  9.9 0.3 collective-permute-start.4
  10.1 3.0 %collective-permute-start.1 = (bf16[1,4,5120]{2,1,0:T(4,128)(2,1)S(1)}, bf16[1,4,5120]{2,1,0:T(4,128)(2,1)S(1)}, u32[]{:S(2)}, u32[]{:S(2)}) collective-permute-start(bf16[1,4,5120]{2,1,0:T(4,128)(2,1)S(1)} %get-tuple-element.24), channel_id=1, source_target_pairs={{0,8},{1,9},{2,10},{3,11},{4,12},{5,13},{6,14},{7,15},{8,0},{9,1},... | collective-permute-start | bytes 122888 | tf_op jit(solution)/shard_map/ppermute | solution.py:416
  13.1 1.6 %collective-permute-start.2 = (bf16[1,4,5120]{2,1,0:T(4,128)(2,1)S(1)}, bf16[1,4,5120]{2,1,0:T(4,128)(2,1)S(1)}, u32[]{:S(2)}, u32[]{:S(2)}) collective-permute-start(bf16[1,4,5120]{2,1,0:T(4,128)(2,1)S(1)} %get-tuple-element.25), channel_id=1, source_target_pairs={{0,12},{1,13},{2,14},{3,15},{4,8},{5,9},{6,10},{7,11},{8,4},{9,5},... | collective-permute-start | bytes 122888 | tf_op jit(solution)/shard_map/ppermute | solution.py:416
  14.7 0.6 %collective-permute-done.6.refs_4_ = bf16[1,4,5120]{2,1,0:T(4,128)(2,1)S(1)} collective-permute-done((bf16[1,4,5120]{2,1,0:T(4,128)(2,1)S(1)}, bf16[1,4,5120]{2,1,0:T(4,128)(2,1)S(1)}, u32[]{:S(2)}, u32[]{:S(2)}) %collective-permute-start.6) | collective-permute-done | bytes 40992 | tf_op jit(solution)/shard_map/ppermute | solution.py:416
  15.3 1.5 %collective-permute-done.1.refs_0_ = bf16[1,4,5120]{2,1,0:T(4,128)(2,1)S(1)} collective-permute-done((bf16[1,4,5120]{2,1,0:T(4,128)(2,1)S(1)}, bf16[1,4,5120]{2,1,0:T(4,128)(2,1)S(1)}, u32[]{:S(2)}, u32[]{:S(2)}) %collective-permute-start.1) | collective-permute-done | bytes 40992 | tf_op jit(solution)/shard_map/ppermute | solution.py:416
  16.8 2.3 %collective-permute-done.2.refs_1_ = bf16[1,4,5120]{2,1,0:T(4,128)(2,1)S(1)} collective-permute-done((bf16[1,4,5120]{2,1,0:T(4,128)(2,1)S(1)}, bf16[1,4,5120]{2,1,0:T(4,128)(2,1)S(1)}, u32[]{:S(2)}, u32[]{:S(2)}) %collective-permute-start.2) | collective-permute-done | bytes 40992 | tf_op jit(solution)/shard_map/ppermute | solution.py:416
  19.1 1.6 %collective-permute-done.7.other_ref = bf16[8,4,5120]{2,1,0:T(4,128)(2,1)S(1)} collective-permute-done((bf16[8,4,5120]{2,1,0:T(4,128)(2,1)S(1)}, bf16[8,4,5120]{2,1,0:T(4,128)(2,1)S(1)}, u32[]{:S(2)}, u32[]{:S(2)}) %collective-permute-start.7) | collective-permute-done | bytes 327712 | tf_op jit(solution)/shard_map/ppermute | solution.py:416
  20.8 17.8 %ffn.1 = (bf16[8,4,5120]{2,1,0:T(4,128)(2,1)S(1)}, bf16[8,4,5120]{2,1,0:T(4,128)(2,1)S(1)}) custom-call(bf16[8,4,5120]{2,1,0:T(4,128)(2,1)S(1)} %gather.1.mine_ref, bf16[8,4,5120]{2,1,0:T(4,128)(2,1)S(1)} %collective-permute-done.7.other_ref, bf16[5120,2560]{1,0:T(8,128)(2,1)} %up_ref.1, bf16[2560,5120]{1,0:T(8,128)(2,1)} %down_ref.1, ...), custom_call_target="tpu_custom_call" | custom-call | flops 5033164800 | bytes 52428800 | tf_op jit(solution)/shard_map/ffn/pallas_call | solution.py:317
  38.8 1.5 %collective-permute-done.8.b_ref = bf16[8,4,5120]{2,1,0:T(4,128)(2,1)S(1)} collective-permute-done((bf16[8,4,5120]{2,1,0:T(4,128)(2,1)S(1)}, bf16[8,4,5120]{2,1,0:T(4,128)(2,1)S(1)}, u32[]{:S(2)}, u32[]{:S(2)}) %collective-permute-start.8) | collective-permute-done | bytes 327712 | tf_op jit(solution)/shard_map/ppermute | solution.py:416
  40.5 1.6 %collective-permute-start.9 = (bf16[3,4,5120]{2,1,0:T(4,128)(2,1)S(1)}, bf16[3,4,5120]{2,1,0:T(4,128)(2,1)S(1)}, u32[]{:S(2)}, u32[]{:S(2)}) collective-permute-start(bf16[3,4,5120]{2,1,0:T(4,128)(2,1)S(1)} %get-tuple-element.32), channel_id=1, source_target_pairs={{0,2},{1,3},{2,0},{3,1},{4,6},{5,7},{6,4},{7,5},{8,10},{9,11},{10,... | collective-permute-start | bytes 368648 | tf_op jit(solution)/shard_map/ppermute | solution.py:416
  42.0 0.6 %collective-permute-start.12 = (bf16[2,4,5120]{2,1,0:T(4,128)(2,1)S(1)}, bf16[2,4,5120]{2,1,0:T(4,128)(2,1)S(1)}, u32[]{:S(2)}, u32[]{:S(2)}) collective-permute-start(bf16[2,4,5120]{2,1,0:T(4,128)(2,1)S(1)} %get-tuple-element.35), channel_id=1, source_target_pairs={{0,4},{1,5},{2,6},{3,7},{4,0},{5,1},{6,2},{7,3},{8,12},{9,13},{10,... | collective-permute-start | bytes 245768 | tf_op jit(solution)/shard_map/ppermute | solution.py:416
  42.6 0.9 %collective-permute-start.14 = (bf16[1,4,5120]{2,1,0:T(4,128)(2,1)S(1)}, bf16[1,4,5120]{2,1,0:T(4,128)(2,1)S(1)}, u32[]{:S(2)}, u32[]{:S(2)}) collective-permute-start(bf16[1,4,5120]{2,1,0:T(4,128)(2,1)S(1)} %get-tuple-element.36), channel_id=1, source_target_pairs={{0,12},{1,13},{2,14},{3,15},{4,8},{5,9},{6,10},{7,11},{8,4},{9,5},... | collective-permute-start | bytes 122888 | tf_op jit(solution)/shard_map/ppermute | solution.py:416
  43.5 2.0 %collective-permute-start.15 = (bf16[1,4,5120]{2,1,0:T(4,128)(2,1)S(1)}, bf16[1,4,5120]{2,1,0:T(4,128)(2,1)S(1)}, u32[]{:S(2)}, u32[]{:S(2)}) collective-permute-start(bf16[1,4,5120]{2,1,0:T(4,128)(2,1)S(1)} %get-tuple-element.37), channel_id=1, source_target_pairs={{0,8},{1,9},{2,10},{3,11},{4,12},{5,13},{6,14},{7,15},{8,0},{9,1},... | collective-permute-start | bytes 122888 | tf_op jit(solution)/shard_map/ppermute | solution.py:416
  45.5 1.0 %collective-permute-done.12.refs_0_.refs_5_ = bf16[2,4,5120]{2,1,0:T(4,128)(2,1)S(1)} collective-permute-done((bf16[2,4,5120]{2,1,0:T(4,128)(2,1)S(1)}, bf16[2,4,5120]{2,1,0:T(4,128)(2,1)S(1)}, u32[]{:S(2)}, u32[]{:S(2)}) %collective-permute-start.12) | collective-permute-done | bytes 81952 | tf_op jit(solution)/shard_map/ppermute | solution.py:416
  46.5 0.5 collective-permute-start.13
  47.1 3.1 %collective-permute-start.11 = (bf16[1,4,5120]{2,1,0:T(4,128)(2,1)S(1)}, bf16[1,4,5120]{2,1,0:T(4,128)(2,1)S(1)}, u32[]{:S(2)}, u32[]{:S(2)}) collective-permute-start(bf16[1,4,5120]{2,1,0:T(4,128)(2,1)S(1)} %get-tuple-element.34), channel_id=1, source_target_pairs={{0,12},{1,13},{2,14},{3,15},{4,8},{5,9},{6,10},{7,11},{8,4},{9,5},... | collective-permute-start | bytes 122888 | tf_op jit(solution)/shard_map/ppermute | solution.py:416
  50.5 1.9 %collective-permute-done.10.refs_0_ = bf16[1,4,5120]{2,1,0:T(4,128)(2,1)S(1)} collective-permute-done((bf16[1,4,5120]{2,1,0:T(4,128)(2,1)S(1)}, bf16[1,4,5120]{2,1,0:T(4,128)(2,1)S(1)}, u32[]{:S(2)}, u32[]{:S(2)}) %collective-permute-start.10) | collective-permute-done | bytes 40992 | tf_op jit(solution)/shard_map/ppermute | solution.py:416
  52.4 0.6 %collective-permute-done.11.refs_1_ = bf16[1,4,5120]{2,1,0:T(4,128)(2,1)S(1)} collective-permute-done((bf16[1,4,5120]{2,1,0:T(4,128)(2,1)S(1)}, bf16[1,4,5120]{2,1,0:T(4,128)(2,1)S(1)}, u32[]{:S(2)}, u32[]{:S(2)}) %collective-permute-start.11) | collective-permute-done | bytes 40992 | tf_op jit(solution)/shard_map/ppermute | solution.py:416
  53.0 1.4 %unpack.1 = bf16[128,5120]{1,0:T(8,128)(2,1)} custom-call(s32[1,128]{1,0:T(1,128)S(1)} %get-tuple-element.22.target_ref, bf16[1,4,5120]{2,1,0:T(4,128)(2,1)S(1)} %collective-permute-done.10.refs_0_, bf16[1,4,5120]{2,1,0:T(4,128)(2,1)S(1)} %collective-permute-done.11.refs_1_, bf16[1,4,5120]{2,1,0:T(4,128)(2,1)S(1)} %collective-permute-done.13.refs_2_, ...), custom_call_target="tpu_custom_call" | custom-call | tf_op jit(solution)/shard_map/unpack/pallas_call | solution.py:393
  (19 shorter events, 0.9 us)
Async XLA Ops:
  0.0 20.8 %copy-start = (bf16[5120,2560]{1,0:T(8,128)(2,1)S(1)}, bf16[5120,2560]{1,0:T(8,128)(2,1)}, u32[]{:S(2)}) copy-start(bf16[5120,2560]{1,0:T(8,128)(2,1)} %gate_ref.1) | copy-start | bytes 78643200
  2.4 7.8 %collective-permute-start = (bf16[3,4,5120]{2,1,0:T(4,128)(2,1)S(1)}, bf16[3,4,5120]{2,1,0:T(4,128)(2,1)S(1)}, u32[]{:S(2)}, u32[]{:S(2)}) collective-permute-start(bf16[3,4,5120]{2,1,0:T(4,128)(2,1)S(1)} %get-tuple-element.23), channel_id=1, source_target_pairs={{0,2},{1,3},{2,0},{3,1},{4,6},{5,7},{6,4},{7,5},{8,10},{9,11},{10,... | collective-permute-start | bytes 368648 | tf_op jit(solution)/shard_map/ppermute | solution.py:416
  5.4 4.4 %collective-permute-start.3 = (bf16[2,4,5120]{2,1,0:T(4,128)(2,1)S(1)}, bf16[2,4,5120]{2,1,0:T(4,128)(2,1)S(1)}, u32[]{:S(2)}, u32[]{:S(2)}) collective-permute-start(bf16[2,4,5120]{2,1,0:T(4,128)(2,1)S(1)} %get-tuple-element.26), channel_id=1, source_target_pairs={{0,4},{1,5},{2,6},{3,7},{4,0},{5,1},{6,2},{7,3},{8,12},{9,13},{10,... | collective-permute-start | bytes 245768 | tf_op jit(solution)/shard_map/ppermute | solution.py:416
  7.0 7.7 %collective-permute-start.5 = (bf16[1,4,5120]{2,1,0:T(4,128)(2,1)S(1)}, bf16[1,4,5120]{2,1,0:T(4,128)(2,1)S(1)}, u32[]{:S(2)}, u32[]{:S(2)}) collective-permute-start(bf16[1,4,5120]{2,1,0:T(4,128)(2,1)S(1)} %get-tuple-element.27), channel_id=1, source_target_pairs={{0,12},{1,13},{2,14},{3,15},{4,8},{5,9},{6,10},{7,11},{8,4},{9,5},... | collective-permute-start | bytes 122888 | tf_op jit(solution)/shard_map/ppermute | solution.py:416
  9.5 5.8 %collective-permute-start.6 = (bf16[1,4,5120]{2,1,0:T(4,128)(2,1)S(1)}, bf16[1,4,5120]{2,1,0:T(4,128)(2,1)S(1)}, u32[]{:S(2)}, u32[]{:S(2)}) collective-permute-start(bf16[1,4,5120]{2,1,0:T(4,128)(2,1)S(1)} %get-tuple-element.28), channel_id=1, source_target_pairs={{0,8},{1,9},{2,10},{3,11},{4,12},{5,13},{6,14},{7,15},{8,0},{9,1},... | collective-permute-start | bytes 122888 | tf_op jit(solution)/shard_map/ppermute | solution.py:416
  9.9 5.4 %collective-permute-start.4 = (bf16[1,4,5120]{2,1,0:T(4,128)(2,1)S(1)}, bf16[1,4,5120]{2,1,0:T(4,128)(2,1)S(1)}, u32[]{:S(2)}, u32[]{:S(2)}) collective-permute-start(bf16[1,4,5120]{2,1,0:T(4,128)(2,1)S(1)} %forward.5), channel_id=1, source_target_pairs={{0,2},{1,3},{2,0},{3,1},{4,6},{5,7},{6,4},{7,5},{8,10},{9,11},{10,... | collective-permute-start | bytes 122888 | tf_op jit(solution)/shard_map/ppermute | solution.py:416
  10.1 6.6 %collective-permute-start.1 = (bf16[1,4,5120]{2,1,0:T(4,128)(2,1)S(1)}, bf16[1,4,5120]{2,1,0:T(4,128)(2,1)S(1)}, u32[]{:S(2)}, u32[]{:S(2)}) collective-permute-start(bf16[1,4,5120]{2,1,0:T(4,128)(2,1)S(1)} %get-tuple-element.24), channel_id=1, source_target_pairs={{0,8},{1,9},{2,10},{3,11},{4,12},{5,13},{6,14},{7,15},{8,0},{9,1},... | collective-permute-start | bytes 122888 | tf_op jit(solution)/shard_map/ppermute | solution.py:416
  13.1 5.9 %collective-permute-start.2 = (bf16[1,4,5120]{2,1,0:T(4,128)(2,1)S(1)}, bf16[1,4,5120]{2,1,0:T(4,128)(2,1)S(1)}, u32[]{:S(2)}, u32[]{:S(2)}) collective-permute-start(bf16[1,4,5120]{2,1,0:T(4,128)(2,1)S(1)} %get-tuple-element.25), channel_id=1, source_target_pairs={{0,12},{1,13},{2,14},{3,15},{4,8},{5,9},{6,10},{7,11},{8,4},{9,5},... | collective-permute-start | bytes 122888 | tf_op jit(solution)/shard_map/ppermute | solution.py:416
  19.1 1.7 %collective-permute-start.7 = (bf16[8,4,5120]{2,1,0:T(4,128)(2,1)S(1)}, bf16[8,4,5120]{2,1,0:T(4,128)(2,1)S(1)}, u32[]{:S(2)}, u32[]{:S(2)}) collective-permute-start(bf16[8,4,5120]{2,1,0:T(4,128)(2,1)S(1)} %gather.1.mine_ref), channel_id=1, source_target_pairs={{0,1},{1,0},{2,3},{3,2},{4,5},{5,4},{6,7},{7,6},{8,9},{9,8},{10,11... | collective-permute-start | bytes 983048 | tf_op jit(solution)/shard_map/ppermute | solution.py:416
  38.6 1.7 %collective-permute-start.8 = (bf16[8,4,5120]{2,1,0:T(4,128)(2,1)S(1)}, bf16[8,4,5120]{2,1,0:T(4,128)(2,1)S(1)}, u32[]{:S(2)}, u32[]{:S(2)}) collective-permute-start(bf16[8,4,5120]{2,1,0:T(4,128)(2,1)S(1)} %get-tuple-element.31), channel_id=1, source_target_pairs={{0,1},{1,0},{2,3},{3,2},{4,5},{5,4},{6,7},{7,6},{8,9},{9,8},{10,11... | collective-permute-start | bytes 983048 | tf_op jit(solution)/shard_map/ppermute | solution.py:416
  40.5 6.5 %collective-permute-start.9 = (bf16[3,4,5120]{2,1,0:T(4,128)(2,1)S(1)}, bf16[3,4,5120]{2,1,0:T(4,128)(2,1)S(1)}, u32[]{:S(2)}, u32[]{:S(2)}) collective-permute-start(bf16[3,4,5120]{2,1,0:T(4,128)(2,1)S(1)} %get-tuple-element.32), channel_id=1, source_target_pairs={{0,2},{1,3},{2,0},{3,1},{4,6},{5,7},{6,4},{7,5},{8,10},{9,11},{10,... | collective-permute-start | bytes 368648 | tf_op jit(solution)/shard_map/ppermute | solution.py:416
  42.0 4.4 %collective-permute-start.12 = (bf16[2,4,5120]{2,1,0:T(4,128)(2,1)S(1)}, bf16[2,4,5120]{2,1,0:T(4,128)(2,1)S(1)}, u32[]{:S(2)}, u32[]{:S(2)}) collective-permute-start(bf16[2,4,5120]{2,1,0:T(4,128)(2,1)S(1)} %get-tuple-element.35), channel_id=1, source_target_pairs={{0,4},{1,5},{2,6},{3,7},{4,0},{5,1},{6,2},{7,3},{8,12},{9,13},{10,... | collective-permute-start | bytes 245768 | tf_op jit(solution)/shard_map/ppermute | solution.py:416
  42.6 7.6 %collective-permute-start.14 = (bf16[1,4,5120]{2,1,0:T(4,128)(2,1)S(1)}, bf16[1,4,5120]{2,1,0:T(4,128)(2,1)S(1)}, u32[]{:S(2)}, u32[]{:S(2)}) collective-permute-start(bf16[1,4,5120]{2,1,0:T(4,128)(2,1)S(1)} %get-tuple-element.36), channel_id=1, source_target_pairs={{0,12},{1,13},{2,14},{3,15},{4,8},{5,9},{6,10},{7,11},{8,4},{9,5},... | collective-permute-start | bytes 122888 | tf_op jit(solution)/shard_map/ppermute | solution.py:416
  43.5 6.8 %collective-permute-start.15 = (bf16[1,4,5120]{2,1,0:T(4,128)(2,1)S(1)}, bf16[1,4,5120]{2,1,0:T(4,128)(2,1)S(1)}, u32[]{:S(2)}, u32[]{:S(2)}) collective-permute-start(bf16[1,4,5120]{2,1,0:T(4,128)(2,1)S(1)} %get-tuple-element.37), channel_id=1, source_target_pairs={{0,8},{1,9},{2,10},{3,11},{4,12},{5,13},{6,14},{7,15},{8,0},{9,1},... | collective-permute-start | bytes 122888 | tf_op jit(solution)/shard_map/ppermute | solution.py:416
  46.5 4.0 %collective-permute-start.13 = (bf16[1,4,5120]{2,1,0:T(4,128)(2,1)S(1)}, bf16[1,4,5120]{2,1,0:T(4,128)(2,1)S(1)}, u32[]{:S(2)}, u32[]{:S(2)}) collective-permute-start(bf16[1,4,5120]{2,1,0:T(4,128)(2,1)S(1)} %forward.7), channel_id=1, source_target_pairs={{0,2},{1,3},{2,0},{3,1},{4,6},{5,7},{6,4},{7,5},{8,10},{9,11},{10,... | collective-permute-start | bytes 122888 | tf_op jit(solution)/shard_map/ppermute | solution.py:416
  47.0 5.4 %collective-permute-start.10 = (bf16[1,4,5120]{2,1,0:T(4,128)(2,1)S(1)}, bf16[1,4,5120]{2,1,0:T(4,128)(2,1)S(1)}, u32[]{:S(2)}, u32[]{:S(2)}) collective-permute-start(bf16[1,4,5120]{2,1,0:T(4,128)(2,1)S(1)} %get-tuple-element.33), channel_id=1, source_target_pairs={{0,8},{1,9},{2,10},{3,11},{4,12},{5,13},{6,14},{7,15},{8,0},{9,1},... | collective-permute-start | bytes 122888 | tf_op jit(solution)/shard_map/ppermute | solution.py:416
  47.1 5.9 %collective-permute-start.11 = (bf16[1,4,5120]{2,1,0:T(4,128)(2,1)S(1)}, bf16[1,4,5120]{2,1,0:T(4,128)(2,1)S(1)}, u32[]{:S(2)}, u32[]{:S(2)}) collective-permute-start(bf16[1,4,5120]{2,1,0:T(4,128)(2,1)S(1)} %get-tuple-element.34), channel_id=1, source_target_pairs={{0,12},{1,13},{2,14},{3,15},{4,8},{5,9},{6,10},{7,11},{8,4},{9,5},... | collective-permute-start | bytes 122888 | tf_op jit(solution)/shard_map/ppermute | solution.py:416

commit v8 on v7

--- a/solution.py
+++ b/solution.py
@@ -259,7 +259,7 @@
     acc_a[...] = jnp.zeros_like(acc_a)
     acc_b[...] = jnp.zeros_like(acc_b)
 
-    @pl.loop(0, ups)
+    @pl.loop(0, ups, unroll=5)
     def _(i):
         row = pl.multiple_of(i * deep, deep)
         acc_a[...] += jnp.dot(
@@ -268,7 +268,7 @@
             preferred_element_type=jnp.float32,
         )
 
-    @pl.loop(0, ups)
+    @pl.loop(0, ups, unroll=5)
     def _(i):
         row = pl.multiple_of(i * deep, deep)
         up_copy(i).wait()
@@ -283,7 +283,7 @@
     for half in range(halves):
         acc_c[...] = jnp.zeros_like(acc_c)
 
-        @pl.loop(0, downs_k)
+        @pl.loop(0, downs_k, unroll=downs_k)
         def _(k, half=half):
             i = ups + half * downs_k + k
             slot = lax.rem(i, slots)

time: 54.5 us -> 53.6 us (0.983)
  Pallas kernels: 21.8 us -> 20.8 us
    pallas_call x1, Pallas kernels: 17.8 us -> 16.9 us  [ffn(): pl.pallas_call(functools.partial(ffn_kernel, deep, wide), in_specs=[vmem]...]
where the time goes in v8:
time: 53.6 us; the launch traced here: 53.4 us
  starting transfers between devices  21.1 us (39%)
  Pallas kernels  20.8 us (39%)
  waiting for transfers between devices  11.5 us (21%)
    ppermute x16, starting transfers between devices, send(): return lax.ppermute(x, 'expert', [(i, i ^ offset) for i in range(devices)])  21.1 us
    pallas_call x1, Pallas kernels, ffn(): pl.pallas_call(functools.partial(ffn_kernel, deep, wide), in_specs=[vmem]...  16.9 us
    ppermute x16, waiting for transfers between devices, send(): return lax.ppermute(x, 'expert', [(i, i ^ offset) for i in range(devices)])  11.5 us
    pallas_call x1, Pallas kernels, pack(): pl.pallas_call(functools.partial(pack_kernel, outers), in_specs=[pl.Block...  2.37 us
    pallas_call x1, Pallas kernels, unpack(): pl.pallas_call(functools.partial(unpack_kernel, *grid_of(chips)), in_spec...  1.4 us
  transfers between devices with their start and end apart: 16, of which 11 were waited for; matrix products, arithmetic and copies ran while one was open for 0% of the time, Pallas kernels for 0%

profile of v8, /device:TPU:0, one launch (start us, length us, event | category | flops | bytes accessed | tf_op | source)
XLA Modules:
  0.0 53.4 jit_solution(6300900823430810439)
XLA Ops:
  0.0 2.4 %pack.1 = (bf16[1,4,5120]{2,1,0:T(4,128)(2,1)S(1)}, bf16[2,4,5120]{2,1,0:T(4,128)(2,1)S(1)}, bf16[1,4,5120]{2,1,0:T(4,128)(2,1)S(1)}, bf16[1,4,5120]{2,1,0:T(4,1...) custom-call(s32[1,128]{1,0:T(1,128)} %bitcast.5, bf16[128,5120]{1,0:T(8,128)(2,1)} %refs_1_.1, ...), custom_call_target="tpu_custom_call" | custom-call | tf_op jit(solution)/shard_map/pack/pallas_call | solution.py:131
  2.4 3.0 %collective-permute-start = (bf16[3,4,5120]{2,1,0:T(4,128)(2,1)S(1)}, bf16[3,4,5120]{2,1,0:T(4,128)(2,1)S(1)}, u32[]{:S(2)}, u32[]{:S(2)}) collective-permute-start(bf16[3,4,5120]{2,1,0:T(4,128)(2,1)S(1)} %get-tuple-element.23), channel_id=1, source_target_pairs={{0,2},{1,3},{2,0},{3,1},{4,6},{5,7},{6,4},{7,5},{8,10},{9,11},{10,... | collective-permute-start | bytes 368648 | tf_op jit(solution)/shard_map/ppermute | solution.py:416
  5.4 1.6 %collective-permute-start.3 = (bf16[2,4,5120]{2,1,0:T(4,128)(2,1)S(1)}, bf16[2,4,5120]{2,1,0:T(4,128)(2,1)S(1)}, u32[]{:S(2)}, u32[]{:S(2)}) collective-permute-start(bf16[2,4,5120]{2,1,0:T(4,128)(2,1)S(1)} %get-tuple-element.26), channel_id=1, source_target_pairs={{0,4},{1,5},{2,6},{3,7},{4,0},{5,1},{6,2},{7,3},{8,12},{9,13},{10,... | collective-permute-start | bytes 245768 | tf_op jit(solution)/shard_map/ppermute | solution.py:416
  7.0 2.5 %collective-permute-start.5 = (bf16[1,4,5120]{2,1,0:T(4,128)(2,1)S(1)}, bf16[1,4,5120]{2,1,0:T(4,128)(2,1)S(1)}, u32[]{:S(2)}, u32[]{:S(2)}) collective-permute-start(bf16[1,4,5120]{2,1,0:T(4,128)(2,1)S(1)} %get-tuple-element.27), channel_id=1, source_target_pairs={{0,12},{1,13},{2,14},{3,15},{4,8},{5,9},{6,10},{7,11},{8,4},{9,5},... | collective-permute-start | bytes 122888 | tf_op jit(solution)/shard_map/ppermute | solution.py:416
  9.6 0.3 collective-permute-done.3.refs_0_.refs_5_
  9.9 0.3 collective-permute-start.4
  10.1 3.0 %collective-permute-start.1 = (bf16[1,4,5120]{2,1,0:T(4,128)(2,1)S(1)}, bf16[1,4,5120]{2,1,0:T(4,128)(2,1)S(1)}, u32[]{:S(2)}, u32[]{:S(2)}) collective-permute-start(bf16[1,4,5120]{2,1,0:T(4,128)(2,1)S(1)} %get-tuple-element.24), channel_id=1, source_target_pairs={{0,8},{1,9},{2,10},{3,11},{4,12},{5,13},{6,14},{7,15},{8,0},{9,1},... | collective-permute-start | bytes 122888 | tf_op jit(solution)/shard_map/ppermute | solution.py:416
  13.1 1.6 %collective-permute-start.2 = (bf16[1,4,5120]{2,1,0:T(4,128)(2,1)S(1)}, bf16[1,4,5120]{2,1,0:T(4,128)(2,1)S(1)}, u32[]{:S(2)}, u32[]{:S(2)}) collective-permute-start(bf16[1,4,5120]{2,1,0:T(4,128)(2,1)S(1)} %get-tuple-element.25), channel_id=1, source_target_pairs={{0,12},{1,13},{2,14},{3,15},{4,8},{5,9},{6,10},{7,11},{8,4},{9,5},... | collective-permute-start | bytes 122888 | tf_op jit(solution)/shard_map/ppermute | solution.py:416
  14.7 0.6 %collective-permute-done.6.refs_4_ = bf16[1,4,5120]{2,1,0:T(4,128)(2,1)S(1)} collective-permute-done((bf16[1,4,5120]{2,1,0:T(4,128)(2,1)S(1)}, bf16[1,4,5120]{2,1,0:T(4,128)(2,1)S(1)}, u32[]{:S(2)}, u32[]{:S(2)}) %collective-permute-start.6) | collective-permute-done | bytes 40992 | tf_op jit(solution)/shard_map/ppermute | solution.py:416
  15.3 1.5 %collective-permute-done.1.refs_0_ = bf16[1,4,5120]{2,1,0:T(4,128)(2,1)S(1)} collective-permute-done((bf16[1,4,5120]{2,1,0:T(4,128)(2,1)S(1)}, bf16[1,4,5120]{2,1,0:T(4,128)(2,1)S(1)}, u32[]{:S(2)}, u32[]{:S(2)}) %collective-permute-start.1) | collective-permute-done | bytes 40992 | tf_op jit(solution)/shard_map/ppermute | solution.py:416
  16.8 2.3 %collective-permute-done.2.refs_1_ = bf16[1,4,5120]{2,1,0:T(4,128)(2,1)S(1)} collective-permute-done((bf16[1,4,5120]{2,1,0:T(4,128)(2,1)S(1)}, bf16[1,4,5120]{2,1,0:T(4,128)(2,1)S(1)}, u32[]{:S(2)}, u32[]{:S(2)}) %collective-permute-start.2) | collective-permute-done | bytes 40992 | tf_op jit(solution)/shard_map/ppermute | solution.py:416
  19.1 1.6 %collective-permute-done.7.other_ref = bf16[8,4,5120]{2,1,0:T(4,128)(2,1)S(1)} collective-permute-done((bf16[8,4,5120]{2,1,0:T(4,128)(2,1)S(1)}, bf16[8,4,5120]{2,1,0:T(4,128)(2,1)S(1)}, u32[]{:S(2)}, u32[]{:S(2)}) %collective-permute-start.7) | collective-permute-done | bytes 327712 | tf_op jit(solution)/shard_map/ppermute | solution.py:416
  20.8 16.9 %ffn.1 = (bf16[8,4,5120]{2,1,0:T(4,128)(2,1)S(1)}, bf16[8,4,5120]{2,1,0:T(4,128)(2,1)S(1)}) custom-call(bf16[8,4,5120]{2,1,0:T(4,128)(2,1)S(1)} %gather.1.mine_ref, bf16[8,4,5120]{2,1,0:T(4,128)(2,1)S(1)} %collective-permute-done.7.other_ref, bf16[5120,2560]{1,0:T(8,128)(2,1)} %up_ref.1, bf16[2560,5120]{1,0:T(8,128)(2,1)} %down_ref.1, ...), custom_call_target="tpu_custom_call" | custom-call | flops 5033164800 | bytes 52428800 | tf_op jit(solution)/shard_map/ffn/pallas_call | solution.py:317
  37.8 1.5 %collective-permute-done.8.b_ref = bf16[8,4,5120]{2,1,0:T(4,128)(2,1)S(1)} collective-permute-done((bf16[8,4,5120]{2,1,0:T(4,128)(2,1)S(1)}, bf16[8,4,5120]{2,1,0:T(4,128)(2,1)S(1)}, u32[]{:S(2)}, u32[]{:S(2)}) %collective-permute-start.8) | collective-permute-done | bytes 327712 | tf_op jit(solution)/shard_map/ppermute | solution.py:416
  39.5 1.6 %collective-permute-start.9 = (bf16[3,4,5120]{2,1,0:T(4,128)(2,1)S(1)}, bf16[3,4,5120]{2,1,0:T(4,128)(2,1)S(1)}, u32[]{:S(2)}, u32[]{:S(2)}) collective-permute-start(bf16[3,4,5120]{2,1,0:T(4,128)(2,1)S(1)} %get-tuple-element.32), channel_id=1, source_target_pairs={{0,2},{1,3},{2,0},{3,1},{4,6},{5,7},{6,4},{7,5},{8,10},{9,11},{10,... | collective-permute-start | bytes 368648 | tf_op jit(solution)/shard_map/ppermute | solution.py:416
  41.1 0.6 %collective-permute-start.12 = (bf16[2,4,5120]{2,1,0:T(4,128)(2,1)S(1)}, bf16[2,4,5120]{2,1,0:T(4,128)(2,1)S(1)}, u32[]{:S(2)}, u32[]{:S(2)}) collective-permute-start(bf16[2,4,5120]{2,1,0:T(4,128)(2,1)S(1)} %get-tuple-element.35), channel_id=1, source_target_pairs={{0,4},{1,5},{2,6},{3,7},{4,0},{5,1},{6,2},{7,3},{8,12},{9,13},{10,... | collective-permute-start | bytes 245768 | tf_op jit(solution)/shard_map/ppermute | solution.py:416
  41.7 0.9 %collective-permute-start.14 = (bf16[1,4,5120]{2,1,0:T(4,128)(2,1)S(1)}, bf16[1,4,5120]{2,1,0:T(4,128)(2,1)S(1)}, u32[]{:S(2)}, u32[]{:S(2)}) collective-permute-start(bf16[1,4,5120]{2,1,0:T(4,128)(2,1)S(1)} %get-tuple-element.36), channel_id=1, source_target_pairs={{0,12},{1,13},{2,14},{3,15},{4,8},{5,9},{6,10},{7,11},{8,4},{9,5},... | collective-permute-start | bytes 122888 | tf_op jit(solution)/shard_map/ppermute | solution.py:416
  42.6 2.0 %collective-permute-start.15 = (bf16[1,4,5120]{2,1,0:T(4,128)(2,1)S(1)}, bf16[1,4,5120]{2,1,0:T(4,128)(2,1)S(1)}, u32[]{:S(2)}, u32[]{:S(2)}) collective-permute-start(bf16[1,4,5120]{2,1,0:T(4,128)(2,1)S(1)} %get-tuple-element.37), channel_id=1, source_target_pairs={{0,8},{1,9},{2,10},{3,11},{4,12},{5,13},{6,14},{7,15},{8,0},{9,1},... | collective-permute-start | bytes 122888 | tf_op jit(solution)/shard_map/ppermute | solution.py:416
  44.6 1.0 %collective-permute-done.12.refs_0_.refs_5_ = bf16[2,4,5120]{2,1,0:T(4,128)(2,1)S(1)} collective-permute-done((bf16[2,4,5120]{2,1,0:T(4,128)(2,1)S(1)}, bf16[2,4,5120]{2,1,0:T(4,128)(2,1)S(1)}, u32[]{:S(2)}, u32[]{:S(2)}) %collective-permute-start.12) | collective-permute-done | bytes 81952 | tf_op jit(solution)/shard_map/ppermute | solution.py:416
  45.5 0.5 collective-permute-start.13
  46.1 3.1 %collective-permute-start.11 = (bf16[1,4,5120]{2,1,0:T(4,128)(2,1)S(1)}, bf16[1,4,5120]{2,1,0:T(4,128)(2,1)S(1)}, u32[]{:S(2)}, u32[]{:S(2)}) collective-permute-start(bf16[1,4,5120]{2,1,0:T(4,128)(2,1)S(1)} %get-tuple-element.34), channel_id=1, source_target_pairs={{0,12},{1,13},{2,14},{3,15},{4,8},{5,9},{6,10},{7,11},{8,4},{9,5},... | collective-permute-start | bytes 122888 | tf_op jit(solution)/shard_map/ppermute | solution.py:416
  49.5 1.9 %collective-permute-done.10.refs_0_ = bf16[1,4,5120]{2,1,0:T(4,128)(2,1)S(1)} collective-permute-done((bf16[1,4,5120]{2,1,0:T(4,128)(2,1)S(1)}, bf16[1,4,5120]{2,1,0:T(4,128)(2,1)S(1)}, u32[]{:S(2)}, u32[]{:S(2)}) %collective-permute-start.10) | collective-permute-done | bytes 40992 | tf_op jit(solution)/shard_map/ppermute | solution.py:416
  51.4 0.6 %collective-permute-done.11.refs_1_ = bf16[1,4,5120]{2,1,0:T(4,128)(2,1)S(1)} collective-permute-done((bf16[1,4,5120]{2,1,0:T(4,128)(2,1)S(1)}, bf16[1,4,5120]{2,1,0:T(4,128)(2,1)S(1)}, u32[]{:S(2)}, u32[]{:S(2)}) %collective-permute-start.11) | collective-permute-done | bytes 40992 | tf_op jit(solution)/shard_map/ppermute | solution.py:416
  52.0 1.4 %unpack.1 = bf16[128,5120]{1,0:T(8,128)(2,1)} custom-call(s32[1,128]{1,0:T(1,128)S(1)} %get-tuple-element.22.target_ref, bf16[1,4,5120]{2,1,0:T(4,128)(2,1)S(1)} %collective-permute-done.10.refs_0_, bf16[1,4,5120]{2,1,0:T(4,128)(2,1)S(1)} %collective-permute-done.11.refs_1_, bf16[1,4,5120]{2,1,0:T(4,128)(2,1)S(1)} %collective-permute-done.13.refs_2_, ...), custom_call_target="tpu_custom_call" | custom-call | tf_op jit(solution)/shard_map/unpack/pallas_call | solution.py:393
  (19 shorter events, 1.0 us)
Async XLA Ops:
  0.0 20.8 %copy-start = (bf16[5120,2560]{1,0:T(8,128)(2,1)S(1)}, bf16[5120,2560]{1,0:T(8,128)(2,1)}, u32[]{:S(2)}) copy-start(bf16[5120,2560]{1,0:T(8,128)(2,1)} %gate_ref.1) | copy-start | bytes 78643200
  2.4 7.8 %collective-permute-start = (bf16[3,4,5120]{2,1,0:T(4,128)(2,1)S(1)}, bf16[3,4,5120]{2,1,0:T(4,128)(2,1)S(1)}, u32[]{:S(2)}, u32[]{:S(2)}) collective-permute-start(bf16[3,4,5120]{2,1,0:T(4,128)(2,1)S(1)} %get-tuple-element.23), channel_id=1, source_target_pairs={{0,2},{1,3},{2,0},{3,1},{4,6},{5,7},{6,4},{7,5},{8,10},{9,11},{10,... | collective-permute-start | bytes 368648 | tf_op jit(solution)/shard_map/ppermute | solution.py:416
  5.4 4.4 %collective-permute-start.3 = (bf16[2,4,5120]{2,1,0:T(4,128)(2,1)S(1)}, bf16[2,4,5120]{2,1,0:T(4,128)(2,1)S(1)}, u32[]{:S(2)}, u32[]{:S(2)}) collective-permute-start(bf16[2,4,5120]{2,1,0:T(4,128)(2,1)S(1)} %get-tuple-element.26), channel_id=1, source_target_pairs={{0,4},{1,5},{2,6},{3,7},{4,0},{5,1},{6,2},{7,3},{8,12},{9,13},{10,... | collective-permute-start | bytes 245768 | tf_op jit(solution)/shard_map/ppermute | solution.py:416
  7.0 7.7 %collective-permute-start.5 = (bf16[1,4,5120]{2,1,0:T(4,128)(2,1)S(1)}, bf16[1,4,5120]{2,1,0:T(4,128)(2,1)S(1)}, u32[]{:S(2)}, u32[]{:S(2)}) collective-permute-start(bf16[1,4,5120]{2,1,0:T(4,128)(2,1)S(1)} %get-tuple-element.27), channel_id=1, source_target_pairs={{0,12},{1,13},{2,14},{3,15},{4,8},{5,9},{6,10},{7,11},{8,4},{9,5},... | collective-permute-start | bytes 122888 | tf_op jit(solution)/shard_map/ppermute | solution.py:416
  9.5 5.8 %collective-permute-start.6 = (bf16[1,4,5120]{2,1,0:T(4,128)(2,1)S(1)}, bf16[1,4,5120]{2,1,0:T(4,128)(2,1)S(1)}, u32[]{:S(2)}, u32[]{:S(2)}) collective-permute-start(bf16[1,4,5120]{2,1,0:T(4,128)(2,1)S(1)} %get-tuple-element.28), channel_id=1, source_target_pairs={{0,8},{1,9},{2,10},{3,11},{4,12},{5,13},{6,14},{7,15},{8,0},{9,1},... | collective-permute-start | bytes 122888 | tf_op jit(solution)/shard_map/ppermute | solution.py:416
  9.9 5.4 %collective-permute-start.4 = (bf16[1,4,5120]{2,1,0:T(4,128)(2,1)S(1)}, bf16[1,4,5120]{2,1,0:T(4,128)(2,1)S(1)}, u32[]{:S(2)}, u32[]{:S(2)}) collective-permute-start(bf16[1,4,5120]{2,1,0:T(4,128)(2,1)S(1)} %forward.5), channel_id=1, source_target_pairs={{0,2},{1,3},{2,0},{3,1},{4,6},{5,7},{6,4},{7,5},{8,10},{9,11},{10,... | collective-permute-start | bytes 122888 | tf_op jit(solution)/shard_map/ppermute | solution.py:416
  10.1 6.6 %collective-permute-start.1 = (bf16[1,4,5120]{2,1,0:T(4,128)(2,1)S(1)}, bf16[1,4,5120]{2,1,0:T(4,128)(2,1)S(1)}, u32[]{:S(2)}, u32[]{:S(2)}) collective-permute-start(bf16[1,4,5120]{2,1,0:T(4,128)(2,1)S(1)} %get-tuple-element.24), channel_id=1, source_target_pairs={{0,8},{1,9},{2,10},{3,11},{4,12},{5,13},{6,14},{7,15},{8,0},{9,1},... | collective-permute-start | bytes 122888 | tf_op jit(solution)/shard_map/ppermute | solution.py:416
  13.1 5.9 %collective-permute-start.2 = (bf16[1,4,5120]{2,1,0:T(4,128)(2,1)S(1)}, bf16[1,4,5120]{2,1,0:T(4,128)(2,1)S(1)}, u32[]{:S(2)}, u32[]{:S(2)}) collective-permute-start(bf16[1,4,5120]{2,1,0:T(4,128)(2,1)S(1)} %get-tuple-element.25), channel_id=1, source_target_pairs={{0,12},{1,13},{2,14},{3,15},{4,8},{5,9},{6,10},{7,11},{8,4},{9,5},... | collective-permute-start | bytes 122888 | tf_op jit(solution)/shard_map/ppermute | solution.py:416
  19.1 1.7 %collective-permute-start.7 = (bf16[8,4,5120]{2,1,0:T(4,128)(2,1)S(1)}, bf16[8,4,5120]{2,1,0:T(4,128)(2,1)S(1)}, u32[]{:S(2)}, u32[]{:S(2)}) collective-permute-start(bf16[8,4,5120]{2,1,0:T(4,128)(2,1)S(1)} %gather.1.mine_ref), channel_id=1, source_target_pairs={{0,1},{1,0},{2,3},{3,2},{4,5},{5,4},{6,7},{7,6},{8,9},{9,8},{10,11... | collective-permute-start | bytes 983048 | tf_op jit(solution)/shard_map/ppermute | solution.py:416
  37.6 1.7 %collective-permute-start.8 = (bf16[8,4,5120]{2,1,0:T(4,128)(2,1)S(1)}, bf16[8,4,5120]{2,1,0:T(4,128)(2,1)S(1)}, u32[]{:S(2)}, u32[]{:S(2)}) collective-permute-start(bf16[8,4,5120]{2,1,0:T(4,128)(2,1)S(1)} %get-tuple-element.31), channel_id=1, source_target_pairs={{0,1},{1,0},{2,3},{3,2},{4,5},{5,4},{6,7},{7,6},{8,9},{9,8},{10,11... | collective-permute-start | bytes 983048 | tf_op jit(solution)/shard_map/ppermute | solution.py:416
  39.5 6.5 %collective-permute-start.9 = (bf16[3,4,5120]{2,1,0:T(4,128)(2,1)S(1)}, bf16[3,4,5120]{2,1,0:T(4,128)(2,1)S(1)}, u32[]{:S(2)}, u32[]{:S(2)}) collective-permute-start(bf16[3,4,5120]{2,1,0:T(4,128)(2,1)S(1)} %get-tuple-element.32), channel_id=1, source_target_pairs={{0,2},{1,3},{2,0},{3,1},{4,6},{5,7},{6,4},{7,5},{8,10},{9,11},{10,... | collective-permute-start | bytes 368648 | tf_op jit(solution)/shard_map/ppermute | solution.py:416
  41.1 4.4 %collective-permute-start.12 = (bf16[2,4,5120]{2,1,0:T(4,128)(2,1)S(1)}, bf16[2,4,5120]{2,1,0:T(4,128)(2,1)S(1)}, u32[]{:S(2)}, u32[]{:S(2)}) collective-permute-start(bf16[2,4,5120]{2,1,0:T(4,128)(2,1)S(1)} %get-tuple-element.35), channel_id=1, source_target_pairs={{0,4},{1,5},{2,6},{3,7},{4,0},{5,1},{6,2},{7,3},{8,12},{9,13},{10,... | collective-permute-start | bytes 245768 | tf_op jit(solution)/shard_map/ppermute | solution.py:416
  41.7 7.6 %collective-permute-start.14 = (bf16[1,4,5120]{2,1,0:T(4,128)(2,1)S(1)}, bf16[1,4,5120]{2,1,0:T(4,128)(2,1)S(1)}, u32[]{:S(2)}, u32[]{:S(2)}) collective-permute-start(bf16[1,4,5120]{2,1,0:T(4,128)(2,1)S(1)} %get-tuple-element.36), channel_id=1, source_target_pairs={{0,12},{1,13},{2,14},{3,15},{4,8},{5,9},{6,10},{7,11},{8,4},{9,5},... | collective-permute-start | bytes 122888 | tf_op jit(solution)/shard_map/ppermute | solution.py:416
  42.6 6.9 %collective-permute-start.15 = (bf16[1,4,5120]{2,1,0:T(4,128)(2,1)S(1)}, bf16[1,4,5120]{2,1,0:T(4,128)(2,1)S(1)}, u32[]{:S(2)}, u32[]{:S(2)}) collective-permute-start(bf16[1,4,5120]{2,1,0:T(4,128)(2,1)S(1)} %get-tuple-element.37), channel_id=1, source_target_pairs={{0,8},{1,9},{2,10},{3,11},{4,12},{5,13},{6,14},{7,15},{8,0},{9,1},... | collective-permute-start | bytes 122888 | tf_op jit(solution)/shard_map/ppermute | solution.py:416
  45.5 4.0 %collective-permute-start.13 = (bf16[1,4,5120]{2,1,0:T(4,128)(2,1)S(1)}, bf16[1,4,5120]{2,1,0:T(4,128)(2,1)S(1)}, u32[]{:S(2)}, u32[]{:S(2)}) collective-permute-start(bf16[1,4,5120]{2,1,0:T(4,128)(2,1)S(1)} %forward.7), channel_id=1, source_target_pairs={{0,2},{1,3},{2,0},{3,1},{4,6},{5,7},{6,4},{7,5},{8,10},{9,11},{10,... | collective-permute-start | bytes 122888 | tf_op jit(solution)/shard_map/ppermute | solution.py:416
  46.0 5.4 %collective-permute-start.10 = (bf16[1,4,5120]{2,1,0:T(4,128)(2,1)S(1)}, bf16[1,4,5120]{2,1,0:T(4,128)(2,1)S(1)}, u32[]{:S(2)}, u32[]{:S(2)}) collective-permute-start(bf16[1,4,5120]{2,1,0:T(4,128)(2,1)S(1)} %get-tuple-element.33), channel_id=1, source_target_pairs={{0,8},{1,9},{2,10},{3,11},{4,12},{5,13},{6,14},{7,15},{8,0},{9,1},... | collective-permute-start | bytes 122888 | tf_op jit(solution)/shard_map/ppermute | solution.py:416
  46.1 5.9 %collective-permute-start.11 = (bf16[1,4,5120]{2,1,0:T(4,128)(2,1)S(1)}, bf16[1,4,5120]{2,1,0:T(4,128)(2,1)S(1)}, u32[]{:S(2)}, u32[]{:S(2)}) collective-permute-start(bf16[1,4,5120]{2,1,0:T(4,128)(2,1)S(1)} %get-tuple-element.34), channel_id=1, source_target_pairs={{0,12},{1,13},{2,14},{3,15},{4,8},{5,9},{6,10},{7,11},{8,4},{9,5},... | collective-permute-start | bytes 122888 | tf_op jit(solution)/shard_map/ppermute | solution.py:416
